TPU v7x, 32 devices: a whole 2x2x4 slice. The times are simulated.
32 devices in a mesh: grp: 4 (over y, x), seq: 8 (over z, core).
Axes of the slice: x: 2, y: 2, z: 4, core: 2. Of those that a mesh axis runs over, the one named last changes fastest.
Arguments:
- queries: bfloat16 [12288, 4096], P(('grp', 'seq')), may hold values from -6 to 6
- keys: bfloat16 [12288, 4096], P(('grp', 'seq')), may hold values from -6 to 6
- values: bfloat16 [12288, 4096], P(('grp', 'seq')), may hold values from -6 to 6
- gain: float32 [4096], replicated, may hold values from 0.5 to 1.5
Outputs:
- attended: bfloat16 [12288, 4096], P(('grp', 'seq'))
All inputs are finite; a program needn't handle non-finite values.
Results may differ from a plain program's by a relative error of at most 0.0049.
Values sent between devices are 32-bit elements; how exact they have to be, the bound alone decides.
No kernel may reach another device: no remote copies, remote signals or barrier semaphores. Data moves between devices by JAX's collectives and lax.ppermute only.
A program may use at most 320 MiB of HBM per device.

v0:
```python
import jax
import jax.numpy as jnp
from jax import lax
from jax.sharding import PartitionSpec as P

H = 32
E = 128


def carried_in(value, axis, combine, identity):
    length, position = (lax.axis_size(axis), lax.axis_index(axis))
    everything = lax.all_gather(value, axis)
    start = jnp.broadcast_to(jnp.asarray(identity, value.dtype), value.shape)

    def turn(k, before):
        reached = k < position
        new = combine(before, everything[k])
        return jnp.where(reached, new, before)

    return lax.fori_loop(0, length, turn, start)


def add_states(earlier, later):
    return earlier + later


def shards(queries, keys, values, gain):
    rows = queries.shape[0]
    qx = queries.reshape(rows, H, E)
    kx = keys.reshape(rows, H, E)
    vx = values.reshape(rows, H, E)
    state = jnp.einsum("the,thf->hef", kx, vx, preferred_element_type=jnp.float32)
    zeros = jnp.zeros_like(state)
    within = carried_in(state, "seq", add_states, zeros)
    group_sum = lax.psum(state, "seq")
    before = carried_in(group_sum, "grp", add_states, zeros)
    prefix = before + within
    causal = lax.broadcasted_iota(jnp.int32, (rows, rows), 0) >= lax.broadcasted_iota(
        jnp.int32, (rows, rows), 1
    )
    scores = jnp.einsum("the,she->hts", qx, kx, preferred_element_type=jnp.float32)
    weights = jnp.where(causal[None, :, :], scores, 0.0).astype(jnp.bfloat16)
    local_part = jnp.einsum("hts,shf->thf", weights, vx, preferred_element_type=jnp.float32)
    carried = jnp.einsum(
        "the,hef->thf", qx, prefix.astype(jnp.bfloat16), preferred_element_type=jnp.float32
    )
    mixed = local_part + carried
    meansq = jnp.mean(mixed * mixed, axis=-1, keepdims=True)
    normed = mixed / jnp.sqrt(meansq + 1e-06) * gain.reshape(H, E)[None, :, :]
    return normed.reshape(rows, H * E).astype(jnp.bfloat16)


def solution(mesh):
    in_specs = (P(("grp", "seq"), None), P(("grp", "seq"), None), P(("grp", "seq"), None), P())
    out_specs = P(("grp", "seq"), None)
    return jax.shard_map(shards, mesh=mesh, in_specs=in_specs, out_specs=out_specs, check_vma=False)
```

profile of v0, /device:TPU:0, one launch (start us, length us, event | category | flops | bytes accessed | tf_op | source)
XLA Modules:
  0.0 361.0 jit_solution(1908244973804894814)
XLA Ops:
  6.5 0.0 copy-start
  6.5 0.0 all-gather.6.cloned.1.call-start
  6.5 4.8 %copy.18 = bf16[384,4096]{0,1:T(8,128)(2,1)} copy(bf16[384,4096]{1,0:T(8,128)(2,1)} %param.9) | data formatting | bytes 6291456 | tf_op jit(solution)/shard_map/reshape | solution.py:30
  11.3 5.2 %fusion.6 = f32[32,128,128]{2,1,0:T(8,128)} fusion(bf16[384,32,128]{0,2,1:T(8,128)(2,1)} %bitcast.58, bf16[384,4096]{1,0:T(8,128)(2,1)} %param.10), kind=kOutput, calls=%fused_computation.11 | convolution fusion | flops 402653184 | bytes 8388608 | tf_op jit(solution)/shard_map/the,thf->hef/dot_general | solution.py:32
  16.5 0.0 all-gather.6.cloned.1.call-update
  16.5 154.0 %all-gather.6.cloned.1.call-done = f32[256,128,128]{2,1,0:T(8,128)} async-done(((f32[32,128,128]{2,1,0:T(8,128)}), f32[256,128,128]{2,1,0:T(8,128)}) %all-gather.6.cloned.1.call-update) | async-done | bytes 16777232 | tf_op jit(solution)/shard_map/all_gather | solution.py:12
  170.5 0.0 all-reduce.2.cloned.1.call-start
  170.5 0.7 all-reduce.2.cloned.1.call-update
  171.2 0.0 all-gather.4.cloned.1.call-start
  171.3 65.6 %all-reduce.2.cloned.1.call-done = f32[1,32,128,128]{3,2,1,0:T(8,128)} async-done(((f32[1,32,128,128]{3,2,1,0:T(8,128)}), f32[1,32,128,128]{3,2,1,0:T(8,128)}) %all-reduce.2.cloned.1.call-update) | async-done | bytes 2097168 | tf_op jit(solution)/shard_map/psum | solution.py:35
  236.8 0.0 all-gather.4.cloned.1.call-update
  236.9 0.0 copy-done
  236.9 11.3 %fusion = f32[32,384,128]{1,2,0:T(8,128)} fusion(pred[384,384]{1,0:T(8,128)(4,1)S(1)} %iota_compare_fusion, bf16[384,32,128]{0,2,1:T(8,128)(2,1)} %bitcast.59, bf16[384,4096]{1,0:T(8,128)(2,1)} %param.10, bf16[384,4096]{1,0:T(8,128)(2,1)S(1)} %copy-done), kind=kOutput, calls=%fused_computation.3 | convolution fusion | flops 2425356288 | bytes 15876096 | tf_op jit(solution)/shard_map/hts,shf->thf/dot_general | solution.py:43
  248.2 33.0 %while.29 = (s32[]{:T(128)}, f32[32,128,128]{2,1,0:T(8,128)}, s32[]{:T(128)}, f32[8,32,128,128]{3,2,1,0:T(8,128)}, s32[]{:T(128)}, /*index=5*/s32[]{:T(128)}) while((s32[]{:T(128)}, f32[32,128,128]{2,1,0:T(8,128)}, s32[]{:T(128)}, f32[8,32,128,128]{3,2,1,0:T(8,128)}, s32[]{:T(128)}, /*index=5*/s32[]{:T(128)}) %tuple.72), condition=%wide.region_4.5_spmd.clone, body=%wide.region_3.4_spmd.clone.sunk | while | flops 1572868 | bytes 6291557 | solution.py:20
  248.2 3.9 %add_select_fusion.5 = f32[32,128,128]{2,1,0:T(8,128)} fusion(f32[32,128,128]{2,1,0:T(8,128)} %get-tuple-element.288, f32[8,32,128,128]{3,2,1,0:T(8,128)} %get-tuple-element.296, s32[]{:T(128)S(6)} %copy.49, pred[]{:T(512)S(6)} %compare.7, pred[]{:T(512)S(6)} %lt.43), kind=kLoop, calls=%fused_computation.1.clone.1 | loop fusion | flops 1572864 | bytes 6291462 | tf_op jit(solution)/shard_map/while/body/eval_jaxpr/jit(_where)/select_n | solution.py:18
  252.1 4.1 %add_select_fusion.5 = f32[32,128,128]{2,1,0:T(8,128)} fusion(f32[32,128,128]{2,1,0:T(8,128)} %get-tuple-element.288, f32[8,32,128,128]{3,2,1,0:T(8,128)} %get-tuple-element.296, s32[]{:T(128)S(6)} %copy.49, pred[]{:T(512)S(6)} %compare.7, pred[]{:T(512)S(6)} %lt.43), kind=kLoop, calls=%fused_computation.1.clone.1 | loop fusion | flops 1572864 | bytes 6291462 | tf_op jit(solution)/shard_map/while/body/eval_jaxpr/jit(_where)/select_n | solution.py:18
  256.2 4.1 %add_select_fusion.5 = f32[32,128,128]{2,1,0:T(8,128)} fusion(f32[32,128,128]{2,1,0:T(8,128)} %get-tuple-element.288, f32[8,32,128,128]{3,2,1,0:T(8,128)} %get-tuple-element.296, s32[]{:T(128)S(6)} %copy.49, pred[]{:T(512)S(6)} %compare.7, pred[]{:T(512)S(6)} %lt.43), kind=kLoop, calls=%fused_computation.1.clone.1 | loop fusion | flops 1572864 | bytes 6291462 | tf_op jit(solution)/shard_map/while/body/eval_jaxpr/jit(_where)/select_n | solution.py:18
  260.4 4.1 %add_select_fusion.5 = f32[32,128,128]{2,1,0:T(8,128)} fusion(f32[32,128,128]{2,1,0:T(8,128)} %get-tuple-element.288, f32[8,32,128,128]{3,2,1,0:T(8,128)} %get-tuple-element.296, s32[]{:T(128)S(6)} %copy.49, pred[]{:T(512)S(6)} %compare.7, pred[]{:T(512)S(6)} %lt.43), kind=kLoop, calls=%fused_computation.1.clone.1 | loop fusion | flops 1572864 | bytes 6291462 | tf_op jit(solution)/shard_map/while/body/eval_jaxpr/jit(_where)/select_n | solution.py:18
  264.5 4.1 %add_select_fusion.5 = f32[32,128,128]{2,1,0:T(8,128)} fusion(f32[32,128,128]{2,1,0:T(8,128)} %get-tuple-element.288, f32[8,32,128,128]{3,2,1,0:T(8,128)} %get-tuple-element.296, s32[]{:T(128)S(6)} %copy.49, pred[]{:T(512)S(6)} %compare.7, pred[]{:T(512)S(6)} %lt.43), kind=kLoop, calls=%fused_computation.1.clone.1 | loop fusion | flops 1572864 | bytes 6291462 | tf_op jit(solution)/shard_map/while/body/eval_jaxpr/jit(_where)/select_n | solution.py:18
  268.6 4.1 %add_select_fusion.5 = f32[32,128,128]{2,1,0:T(8,128)} fusion(f32[32,128,128]{2,1,0:T(8,128)} %get-tuple-element.288, f32[8,32,128,128]{3,2,1,0:T(8,128)} %get-tuple-element.296, s32[]{:T(128)S(6)} %copy.49, pred[]{:T(512)S(6)} %compare.7, pred[]{:T(512)S(6)} %lt.43), kind=kLoop, calls=%fused_computation.1.clone.1 | loop fusion | flops 1572864 | bytes 6291462 | tf_op jit(solution)/shard_map/while/body/eval_jaxpr/jit(_where)/select_n | solution.py:18
  272.7 4.1 %add_select_fusion.5 = f32[32,128,128]{2,1,0:T(8,128)} fusion(f32[32,128,128]{2,1,0:T(8,128)} %get-tuple-element.288, f32[8,32,128,128]{3,2,1,0:T(8,128)} %get-tuple-element.296, s32[]{:T(128)S(6)} %copy.49, pred[]{:T(512)S(6)} %compare.7, pred[]{:T(512)S(6)} %lt.43), kind=kLoop, calls=%fused_computation.1.clone.1 | loop fusion | flops 1572864 | bytes 6291462 | tf_op jit(solution)/shard_map/while/body/eval_jaxpr/jit(_where)/select_n | solution.py:18
  276.9 4.4 %add_select_fusion.5 = f32[32,128,128]{2,1,0:T(8,128)} fusion(f32[32,128,128]{2,1,0:T(8,128)} %get-tuple-element.288, f32[8,32,128,128]{3,2,1,0:T(8,128)} %get-tuple-element.296, s32[]{:T(128)S(6)} %copy.49, pred[]{:T(512)S(6)} %compare.7, pred[]{:T(512)S(6)} %lt.43), kind=kLoop, calls=%fused_computation.1.clone.1 | loop fusion | flops 1572864 | bytes 6291462 | tf_op jit(solution)/shard_map/while/body/eval_jaxpr/jit(_where)/select_n | solution.py:18
  281.3 44.7 %all-gather.4.cloned.1.call-done = f32[4,32,128,128]{3,2,1,0:T(8,128)} async-done(((f32[1,32,128,128]{3,2,1,0:T(8,128)}), f32[4,32,128,128]{3,2,1,0:T(8,128)}) %all-gather.4.cloned.1.call-update) | async-done | bytes 8388624 | tf_op jit(solution)/shard_map/all_gather | solution.py:12
  325.9 15.6 %while.28 = (s32[]{:T(128)}, f32[32,128,128]{2,1,0:T(8,128)}, s32[]{:T(128)}, f32[4,32,128,128]{3,2,1,0:T(8,128)}, s32[]{:T(128)}, /*index=5*/s32[]{:T(128)}) while((s32[]{:T(128)}, f32[32,128,128]{2,1,0:T(8,128)}, s32[]{:T(128)}, f32[4,32,128,128]{3,2,1,0:T(8,128)}, s32[]{:T(128)}, /*index=5*/s32[]{:T(128)}) %tuple.60), condition=%wide.region_2.3_spmd.clone, body=%wide.region_1.2_spmd.clone.sunk | while | flops 1572868 | bytes 6291557 | solution.py:20
  326.0 3.4 add_select_fusion.4
  329.4 4.1 %add_select_fusion.4 = f32[32,128,128]{2,1,0:T(8,128)} fusion(f32[32,128,128]{2,1,0:T(8,128)} %get-tuple-element.270, f32[4,32,128,128]{3,2,1,0:T(8,128)} %get-tuple-element.278, s32[]{:T(128)S(6)} %copy.43, pred[]{:T(512)S(6)} %compare.6, pred[]{:T(512)S(6)} %lt.42), kind=kLoop, calls=%fused_computation.clone.1 | loop fusion | flops 1572864 | bytes 6291462 | tf_op jit(solution)/shard_map/while/body/eval_jaxpr/jit(_where)/select_n | solution.py:18
  333.4 4.1 %add_select_fusion.4 = f32[32,128,128]{2,1,0:T(8,128)} fusion(f32[32,128,128]{2,1,0:T(8,128)} %get-tuple-element.270, f32[4,32,128,128]{3,2,1,0:T(8,128)} %get-tuple-element.278, s32[]{:T(128)S(6)} %copy.43, pred[]{:T(512)S(6)} %compare.6, pred[]{:T(512)S(6)} %lt.42), kind=kLoop, calls=%fused_computation.clone.1 | loop fusion | flops 1572864 | bytes 6291462 | tf_op jit(solution)/shard_map/while/body/eval_jaxpr/jit(_where)/select_n | solution.py:18
  337.5 4.1 %add_select_fusion.4 = f32[32,128,128]{2,1,0:T(8,128)} fusion(f32[32,128,128]{2,1,0:T(8,128)} %get-tuple-element.270, f32[4,32,128,128]{3,2,1,0:T(8,128)} %get-tuple-element.278, s32[]{:T(128)S(6)} %copy.43, pred[]{:T(512)S(6)} %compare.6, pred[]{:T(512)S(6)} %lt.42), kind=kLoop, calls=%fused_computation.clone.1 | loop fusion | flops 1572864 | bytes 6291462 | tf_op jit(solution)/shard_map/while/body/eval_jaxpr/jit(_where)/select_n | solution.py:18
  341.6 0.0 slice-start
  341.6 0.0 slice-start.1
  341.6 0.0 copy-start.1
  341.6 5.7 %multiply_reduce_fusion = (f32[384,32]{0,1:T(8,128)S(1)}, f32[32,128,384]{2,1,0:T(8,128)S(1)}) fusion(f32[32,384,128]{1,2,0:T(8,128)} %fusion, f32[32,128,128]{2,1,0:T(8,128)} %get-tuple-element.163, f32[32,128,128]{2,1,0:T(8,128)} %get-tuple-element.164, bf16[384,4096]{1,0:T(8,128)(2,1)S(1)} %copy-done), kind=kOutput, calls=%fused_computation.8 | convolution fusion | flops 408408064 | bytes 19972096 | tf_op jit(solution)/shard_map/the,hef->thf/dot_general | solution.py:44
  347.3 0.0 slice-done
  347.3 0.2 slice-done.1
  347.5 0.0 copy-done.1
  347.5 2.4 multiply_convert_fusion
  349.9 4.6 %copy.16 = bf16[384,4096]{1,0:T(8,128)(2,1)} copy(bf16[384,4096]{0,1:T(8,128)(2,1)} %bitcast.60) | data formatting | bytes 6291456 | tf_op jit(solution)/shard_map/convert_element_type | solution.py:50
  (5 shorter events, 0.1 us)
Async XLA Ops:
  6.5 230.4 %copy-start = (bf16[384,4096]{1,0:T(8,128)(2,1)S(1)}, bf16[384,4096]{1,0:T(8,128)(2,1)}, u32[]{:S(2)}) copy-start(bf16[384,4096]{1,0:T(8,128)(2,1)} %param.8) | copy-start | bytes 9437188
  6.5 163.9 %all-gather.6.cloned.1.call-start = ((), (), s32[]{:S(2)}) async-start(), calls=%async_computation.2 | async-start | bytes 18874368 | tf_op jit(solution)/shard_map/all_gather | solution.py:12
  170.5 66.3 %all-reduce.2.cloned.1.call-start = ((), (), s32[]{:S(2)}) async-start(), calls=%async_computation | async-start | bytes 4194304 | tf_op jit(solution)/shard_map/psum | solution.py:35
  171.2 154.7 %all-gather.4.cloned.1.call-start = ((), (), s32[]{:S(2)}) async-start(), calls=%async_computation.1 | async-start | bytes 10485760 | tf_op jit(solution)/shard_map/all_gather | solution.py:12
  341.6 5.7 %slice-start = ((s8[6291456]{0:T(1024)(128)(4,1)}), s8[4194304]{0:T(1024)(128)(4,1)S(1)}, s32[]{:S(2)}) async-start(s8[6291456]{0:T(1024)(128)(4,1)} %bitcast.55), calls=%async_computation.3 | async-start | bytes 8388608
  341.6 5.9 %slice-start.1 = ((s8[6291456]{0:T(1024)(128)(4,1)}), s8[2097152]{0:T(1024)(128)(4,1)S(1)}, s32[]{:S(2)}) async-start(s8[6291456]{0:T(1024)(128)(4,1)} %bitcast.55), calls=%async_computation.4 | async-start | bytes 4194304
  341.6 5.9 %copy-start.1 = (f32[4096]{0:T(1024)S(1)}, f32[4096]{0:T(1024)}, u32[]{:S(2)}) copy-start(f32[4096]{0:T(1024)} %param.11) | copy-start | bytes 49156
Sparse Core Ops, SparseCore 0:
  16.6 153.7 all-gather.5
  173.7 63.1 all-reduce.1
  238.7 87.2 all-gather.3
where the time goes:
time: 361 us
  waiting for transfers between devices  265 us (73%)
  other arithmetic  51.1 us (14%)
  matrix products  22.1 us (6%)
  between operations  13.2 us (4%)
  local copies, waits for them, and re-layouts  9.61 us (3%)
    all_gather x2, waiting for transfers between devices, carried_in(): everything = lax.all_gather(value, axis)  199 us
    psum x1, waiting for transfers between devices, shards(): group_sum = lax.psum(state, 'seq')  65.6 us
    select_n x12, other arithmetic, turn(): return jnp.where(reached, new, before)  48.6 us
    dot_general x1, matrix products, shards(): jnp.einsum('hts,shf->thf', weights, vx, preferred_element_type=jnp.float32)  11.3 us
  transfers between devices with their start and end apart: 3, of which 3 were waited for; matrix products, arithmetic and copies ran while one was open for 12% of the time, Pallas kernels for 0%

commit v1 on v0

v1 whole, which is shorter than its diff:
```python
import functools

import jax
import jax.numpy as jnp
from jax import lax
from jax.experimental import pallas as pl
from jax.experimental.pallas import tpu as pltpu
from jax.sharding import PartitionSpec as P

H = 32
E = 128
AXES = ("grp", "seq")
HEADS_STEP = 4
HALF = H // 2
STEPS = HALF // HEADS_STEP
WIDTH = HEADS_STEP * E


def state_kernel(half_ref, k_ref, v_ref, out_ref):
    for h in range(HEADS_STEP):
        cols = slice(h * E, (h + 1) * E)
        out_ref[cols, :] = lax.dot_general(
            k_ref[:, cols],
            v_ref[:, cols],
            (((0,), (0,)), ((), ())),
            preferred_element_type=jnp.float32,
        )


def states_of_half(half, keys, values):
    rows = keys.shape[0]
    block = pl.BlockSpec((rows, WIDTH), lambda i, half: (0, half[0] * STEPS + i))
    return pl.pallas_call(
        state_kernel,
        grid_spec=pltpu.PrefetchScalarGridSpec(
            num_scalar_prefetch=1,
            grid=(STEPS,),
            in_specs=[block, block],
            out_specs=pl.BlockSpec((WIDTH, E), lambda i, half: (i, 0)),
        ),
        out_shape=jax.ShapeDtypeStruct((HALF * E, E), jnp.float32),
        name="states",
    )(half, keys, values)


def scan_kernel(chips, x_ref, out_ref):
    rows = x_ref.shape[0] // chips
    total = jnp.zeros((rows, E), jnp.float32)
    for i in range(chips):
        part = slice(i * rows, (i + 1) * rows)
        out_ref[part, :] = total
        if i < chips - 1:
            total = total + x_ref[part, :]


def scan_chips(chips, x):
    return pl.pallas_call(
        functools.partial(scan_kernel, chips),
        in_specs=[pl.BlockSpec(memory_space=pltpu.VMEM)],
        out_specs=pl.BlockSpec(memory_space=pltpu.VMEM),
        out_shape=jax.ShapeDtypeStruct(x.shape, jnp.float32),
        name="chip_scan",
    )(x)


def mix_kernel(half_ref, q_ref, k_ref, v_ref, p_ref, gain_ref, *rest):
    out_ref = rest[-1]
    rows = q_ref.shape[0]
    tile = E
    causal = lax.broadcasted_iota(jnp.int32, (tile, tile), 0) >= lax.broadcasted_iota(
        jnp.int32, (tile, tile), 1
    )
    for h in range(HEADS_STEP):
        cols = slice(h * E, (h + 1) * E)
        low = p_ref[cols, :].astype(jnp.bfloat16)
        for r in range(rows // tile):
            here = slice(r * tile, (r + 1) * tile)
            seen = slice(0, (r + 1) * tile)
            q = q_ref[here, cols]
            scores = lax.dot_general(
                q, k_ref[seen, cols], (((1,), (1,)), ((), ())), preferred_element_type=jnp.float32
            )
            diagonal = jnp.where(causal, scores[:, r * tile :], 0.0).astype(jnp.bfloat16)
            parts = [diagonal, q]
            if r > 0:
                parts = [scores[:, : r * tile].astype(jnp.bfloat16)] + parts
            left = jnp.concatenate(parts, axis=1)
            right = jnp.concatenate([v_ref[seen, cols], low], axis=0)
            mixed = jnp.dot(left, right, preferred_element_type=jnp.float32)
            meansq = jnp.mean(mixed * mixed, axis=-1, keepdims=True)
            normed = mixed * lax.rsqrt(meansq + 1e-6) * gain_ref[:, cols]
            out_ref[here, cols] = normed.astype(jnp.bfloat16)


def mix_half(half, queries, keys, values, prefix, gain, base):
    rows = queries.shape[0]
    block = pl.BlockSpec((rows, WIDTH), lambda i, half: (0, half[0] * STEPS + i))
    in_specs = [
        block,
        block,
        block,
        pl.BlockSpec((WIDTH, E), lambda i, half: (i, 0)),
        pl.BlockSpec((1, WIDTH), lambda i, half: (0, half[0] * STEPS + i)),
    ]
    args = [half, queries, keys, values, prefix, gain]
    aliases = {}
    if base is not None:
        in_specs.append(pl.BlockSpec(memory_space=pl.ANY))
        args.append(base)
        aliases = {len(args) - 1: 0}
    return pl.pallas_call(
        mix_kernel,
        grid_spec=pltpu.PrefetchScalarGridSpec(
            num_scalar_prefetch=1, grid=(STEPS,), in_specs=in_specs, out_specs=block
        ),
        out_shape=jax.ShapeDtypeStruct(queries.shape, jnp.bfloat16),
        input_output_aliases=aliases,
        name="mix",
    )(*args)


def shards(queries, keys, values, gain):
    devices = lax.axis_size("grp") * lax.axis_size("seq")
    chips = devices // 2
    core = lax.rem(lax.axis_index("seq"), 2).astype(jnp.int32)
    mine, other = core.reshape(1), (1 - core).reshape(1)
    sibling = [(i, i ^ 1) for i in range(devices)]
    groups = [[2 * i + c for i in range(chips)] for c in (0, 1)]
    gain = gain.reshape(1, H * E)

    send = states_of_half(other, keys, values)
    got = lax.ppermute(send, AXES, sibling)
    keep = states_of_half(mine, keys, values)
    chip = keep + got
    everyone = lax.all_to_all(chip, AXES, 0, 0, axis_index_groups=groups, tiled=True)
    before = scan_chips(chips, everyone)
    before = lax.all_to_all(before, AXES, 0, 0, axis_index_groups=groups, tiled=True)
    second = core == 1
    to_sibling = before + jnp.where(second, 0.0, keep)
    prefix_mine = before + jnp.where(second, got, 0.0)
    prefix_other = lax.ppermute(to_sibling, AXES, sibling)
    out = mix_half(mine, queries, keys, values, prefix_mine, gain, None)
    return mix_half(other, queries, keys, values, prefix_other, gain, out)


def solution(mesh):
    rows = P(("grp", "seq"), None)
    return jax.shard_map(
        shards, mesh=mesh, in_specs=(rows, rows, rows, P()), out_specs=rows, check_vma=False
    )
```

time: 361 us -> 100 us (0.28)
  waiting for transfers between devices: 265 us -> 27 us
  other arithmetic: 51.1 us -> 2.86 us
  blocking collectives: 0 us -> 36 us
  Pallas kernels: 0 us -> 28.7 us
  matrix products: 22.1 us -> 0 us
  between operations: 13.2 us -> 0.03 us
  local copies, waits for them, and re-layouts: 9.61 us -> 0.98 us
  starting transfers between devices: 0.04 us -> 4.11 us
    all_gather x2 -> x0, waiting for transfers between devices: 199 us -> none  [carried_in(): everything = lax.all_gather(value, axis)]
    psum x1 -> x0, waiting for transfers between devices: 65.6 us -> none  [shards(): group_sum = lax.psum(state, 'seq')]
    select_n x12 -> x0, other arithmetic: 48.6 us -> none  [turn(): return jnp.where(reached, new, before)]
    all_to_all x0 -> x1, blocking collectives: none -> 36 us  [shards(): lax.all_to_all(chip, AXES, 0, 0, axis_index_groups=groups, tiled=True)]
    pallas_call x0 -> x5, Pallas kernels: none -> 28.7 us  [the longest x2 17.8 us: mix_half(): pl.pallas_call(mix_kernel, grid_spec=pltpu.PrefetchScalarGridSpec(num_sca...]
    all_to_all x0 -> x1, waiting for transfers between devices: none -> 27 us  [shards(): lax.all_to_all(before, AXES, 0, 0, axis_index_groups=groups, tiled=True)]
    dot_general x3 -> x0, matrix products: 22.1 us -> none  [the longest x1 11.3 us: shards(): jnp.einsum('hts,shf->thf', weights, vx, preferred_element_type=jnp.float32)]
    reshape x1 -> x0, local copies, waits for them, and re-layouts: 4.78 us -> none  [shards(): kx = keys.reshape(rows, H, E)]
  transfers between devices with their start and end apart: 3 -> 3, of which waited for: 3 -> 1; matrix products, arithmetic and copies ran while one was open for 12% -> 0% of each run, Pallas kernels for 0% -> 13%
where the time goes in v1:
time: 100 us; the launch traced here: 99.7 us
  blocking collectives  36 us (36%)
  Pallas kernels  28.7 us (29%)
  waiting for transfers between devices  27 us (27%)
  starting transfers between devices  4.11 us (4%)
  other arithmetic  2.86 us (3%)
    all_to_all x1, blocking collectives, shards(): lax.all_to_all(chip, AXES, 0, 0, axis_index_groups=groups, tiled=True)  36 us
    all_to_all x1, waiting for transfers between devices, shards(): lax.all_to_all(before, AXES, 0, 0, axis_index_groups=groups, tiled=True)  27 us
    pallas_call x2, Pallas kernels, mix_half(): pl.pallas_call(mix_kernel, grid_spec=pltpu.PrefetchScalarGridSpec(num_sca...  17.8 us
    pallas_call x2, Pallas kernels, states_of_half(): pl.pallas_call(state_kernel, grid_spec=pltpu.PrefetchScalarGridSpec(num_s...  8.63 us
    all_to_all x1, starting transfers between devices, shards(): lax.all_to_all(before, AXES, 0, 0, axis_index_groups=groups, tiled=True)  3.65 us
    pallas_call x1, Pallas kernels, scan_chips(): pl.pallas_call(functools.partial(scan_kernel, chips), in_specs=[pl.BlockS...  2.33 us
  transfers between devices with their start and end apart: 3, of which 1 were waited for; matrix products, arithmetic and copies ran while one was open for 0% of the time, Pallas kernels for 13%

profile of v1, /device:TPU:0, one launch (start us, length us, event | category | flops | bytes accessed | tf_op | source)
XLA Modules:
  0.0 99.7 jit_solution(11871189697328876025)
XLA Ops:
  0.0 4.3 %states.3 = f32[2048,128]{1,0:T(8,128)} custom-call(s32[1]{0:T(128)} %bitcast.half_ref, bf16[384,4096]{1,0:T(8,128)(2,1)} %k_ref.7, bf16[384,4096]{1,0:T(8,128)(2,1)} %v_ref.7), custom_call_target="tpu_custom_call" | custom-call | tf_op jit(solution)/shard_map/states/pallas_call | solution.py:33
  4.3 0.5 collective-permute-start
  4.8 4.3 %states.2 = f32[2048,128]{1,0:T(8,128)} custom-call(s32[1]{0:T(128)} %bitcast.1.half_ref, bf16[384,4096]{1,0:T(8,128)(2,1)} %k_ref.7, bf16[384,4096]{1,0:T(8,128)(2,1)} %v_ref.7), custom_call_target="tpu_custom_call" | custom-call | tf_op jit(solution)/shard_map/states/pallas_call | solution.py:33
  9.1 0.0 collective-permute-done
  9.1 1.3 %add.9 = f32[2048,128]{1,0:T(8,128)S(1)} add(f32[2048,128]{1,0:T(8,128)} %states.2, f32[2048,128]{1,0:T(8,128)S(1)} %collective-permute-done) | non-fusion elementwise | flops 262144 | bytes 3145728 | tf_op jit(solution)/shard_map/add | solution.py:134
  10.4 0.0 copy-start
  10.4 36.0 %all_to_all.23 = f32[16,128,128]{2,1,0:T(8,128)} all-to-all(f32[16,128,128]{2,1,0:T(8,128)S(1)} %bitcast.9), channel_id=1, replica_groups={{0,2,4,6,8,10,12,14,16,18,20,22,24,26,28,30},{1,3,5,7,9,11,13,15,17,19,..., dimensions={0} | all-to-all | bytes 2097152 | tf_op jit(solution)/shard_map/all_to_all | solution.py:135
  46.4 2.3 %chip_scan.1 = f32[2048,128]{1,0:T(8,128)} custom-call(f32[2048,128]{1,0:T(8,128)} %bitcast.11), custom_call_target="tpu_custom_call" | custom-call | tf_op jit(solution)/shard_map/chip_scan/pallas_call | solution.py:57
  48.8 3.7 %all-to-all-start.1 = ((f32[16,128,128]{2,1,0:T(8,128)}), f32[16,128,128]{2,1,0:T(8,128)S(1)}, u32[]{:S(2)}, u32[]{:S(2)}) async-start(f32[16,128,128]{2,1,0:T(8,128)} %bitcast.10), calls=%async_computation.1 | async-start | bytes 2097152 | tf_op jit(solution)/shard_map/all_to_all | solution.py:137
  52.4 27.0 %all-to-all-done.1 = f32[16,128,128]{2,1,0:T(8,128)S(1)} async-done(((f32[16,128,128]{2,1,0:T(8,128)}), f32[16,128,128]{2,1,0:T(8,128)S(1)}, u32[]{:S(2)}, u32[]{:S(2)}) %all-to-all-start.1) | async-done | bytes 1048608 | tf_op jit(solution)/shard_map/all_to_all | solution.py:137
  79.4 0.0 copy-done
  79.4 1.5 %bitcast_add_fusion = (f32[2048,128]{1,0:T(8,128)}, f32[2048,128]{1,0:T(8,128)}) fusion(f32[16,128,128]{2,1,0:T(8,128)S(1)} %all-to-all-done.1, f32[2048,128]{1,0:T(8,128)S(1)} %collective-permute-done, pred[]{:T(512)S(6)} %eq.3, f32[2048,128]{1,0:T(8,128)S(1)} %copy-done), kind=kLoop, calls=%fused_computation | loop fusion | flops 1048576 | bytes 5242881 | tf_op jit(solution)/shard_map/add | solution.py:140
  80.9 0.0 collective-permute-start.1
  80.9 8.9 %mix.2.rest_0_ = bf16[384,4096]{1,0:T(8,128)(2,1)} custom-call(s32[1]{0:T(128)} %bitcast.1.half_ref, bf16[384,4096]{1,0:T(8,128)(2,1)} %q_ref.3, bf16[384,4096]{1,0:T(8,128)(2,1)} %k_ref.7, bf16[384,4096]{1,0:T(8,128)(2,1)} %v_ref.7, f32[2048,128]{1,0:T(8,128)} %get-tuple-element.5.p_ref, f32[1,4096]{1,0:T(1,128)} %bitcast.12), custom_call_target="tpu_custom_call" | custom-call | tf_op jit(solution)/shard_map/mix/pallas_call | solution.py:111
  89.8 0.0 collective-permute-done.1.p_ref
  89.8 0.0 copy-start.1
  89.8 1.0 copy-done.1
  90.8 8.9 %mix.3 = bf16[384,4096]{1,0:T(8,128)(2,1)} custom-call(s32[1]{0:T(128)} %bitcast.half_ref, bf16[384,4096]{1,0:T(8,128)(2,1)} %q_ref.3, bf16[384,4096]{1,0:T(8,128)(2,1)} %k_ref.7, bf16[384,4096]{1,0:T(8,128)(2,1)} %v_ref.7, f32[2048,128]{1,0:T(8,128)} %copy-done.1, f32[1,4096]{1,0:T(1,128)} %bitcast.13, ...), custom_call_target="tpu_custom_call", output_to_operand_aliasing={{}: (6, {})} | custom-call | tf_op jit(solution)/shard_map/mix/pallas_call | solution.py:111
Async XLA Ops:
  4.3 4.8 %collective-permute-start = (f32[2048,128]{1,0:T(8,128)}, f32[2048,128]{1,0:T(8,128)S(1)}, u32[]{:S(2)}, u32[]{:S(2)}) collective-permute-start(f32[2048,128]{1,0:T(8,128)} %states.3), channel_id=1, source_target_pairs={{0,1},{1,0},{2,3},{3,2},{4,5},{5,4},{6,7},{7,6},{8,9},{9,8},{10,11... | collective-permute-start | bytes 3145736 | tf_op jit(solution)/shard_map/ppermute | solution.py:132
  10.4 69.0 %copy-start = (f32[2048,128]{1,0:T(8,128)S(1)}, f32[2048,128]{1,0:T(8,128)}, u32[]{:S(2)}) copy-start(f32[2048,128]{1,0:T(8,128)} %states.2) | copy-start | bytes 3145732
  48.8 30.6 %all-to-all-start.1 = ((f32[16,128,128]{2,1,0:T(8,128)}), f32[16,128,128]{2,1,0:T(8,128)S(1)}, u32[]{:S(2)}, u32[]{:S(2)}) async-start(f32[16,128,128]{2,1,0:T(8,128)} %bitcast.10), calls=%async_computation.1 | async-start | bytes 2097152 | tf_op jit(solution)/shard_map/all_to_all | solution.py:137
  80.9 8.9 %collective-permute-start.1 = (f32[2048,128]{1,0:T(8,128)}, f32[2048,128]{1,0:T(8,128)S(1)}, u32[]{:S(2)}, u32[]{:S(2)}) collective-permute-start(f32[2048,128]{1,0:T(8,128)} %get-tuple-element.6), channel_id=1, source_target_pairs={{0,1},{1,0},{2,3},{3,2},{4,5},{5,4},{6,7},{7,6},{8,9},{9,8},{10,11... | collective-permute-start | bytes 3145736 | tf_op jit(solution)/shard_map/ppermute | solution.py:141
  89.8 1.0 copy-start.1

commit v2 on v1

v2 whole, which is shorter than its diff:
```python
import functools

import jax
import jax.numpy as jnp
from jax import lax
from jax.experimental import pallas as pl
from jax.experimental.pallas import tpu as pltpu
from jax.sharding import PartitionSpec as P

H = 32
E = 128
AXES = ("grp", "seq")
HALF = H // 2
PIECE = 4
WIDTH = PIECE * E
VMEM = pl.BlockSpec(memory_space=pltpu.VMEM)
SMEM = pl.BlockSpec(memory_space=pltpu.SMEM)
HBM = pl.BlockSpec(memory_space=pltpu.HBM)


def limit(mebibytes):
    return pltpu.CompilerParams(vmem_limit_bytes=mebibytes * 1024 * 1024)


def in_vmem(x):
    return pltpu.with_memory_space_constraint(x, pltpu.VMEM)


def in_hbm(x):
    return pltpu.with_memory_space_constraint(x, pltpu.HBM)


def lane_tile(start, size):
    return pl.ds(pl.multiple_of(start, E), size)


def state_kernel(first_ref, k_ref, v_ref, out_ref, k_buf, v_buf, sems):
    heads = out_ref.shape[0] // E
    base = first_ref[0] * E
    copies = []
    for piece in range(heads // PIECE):
        for n, (ref, buf) in enumerate(((k_ref, k_buf), (v_ref, v_buf))):
            copy = pltpu.make_async_copy(
                ref.at[:, lane_tile(base + piece * WIDTH, WIDTH)],
                buf.at[piece],
                sems.at[n, piece],
            )
            copy.start()
            copies.append(copy)
    for piece in range(heads // PIECE):
        copies[2 * piece].wait()
        copies[2 * piece + 1].wait()
        for h in range(PIECE):
            cols = slice(h * E, (h + 1) * E)
            here = (piece * PIECE + h) * E
            out_ref[here : here + E, :] = lax.dot_general(
                k_buf[piece, :, cols],
                v_buf[piece, :, cols],
                (((0,), (0,)), ((), ())),
                preferred_element_type=jnp.float32,
            )


def states_of(first, heads, keys, values):
    rows = keys.shape[0]
    pieces = heads // PIECE
    return pl.pallas_call(
        state_kernel,
        in_specs=[SMEM, HBM, HBM],
        out_specs=VMEM,
        out_shape=pltpu.VMEM((heads * E, E), jnp.float32),
        scratch_shapes=[
            pltpu.VMEM((pieces, rows, WIDTH), jnp.bfloat16),
            pltpu.VMEM((pieces, rows, WIDTH), jnp.bfloat16),
            pltpu.SemaphoreType.DMA((2, pieces)),
        ],
        compiler_params=limit(6),
        name="states",
    )(first, in_hbm(keys), in_hbm(values))


def pair_kernel(core_ref, keep_ref, got_ref, chip_ref, first_ref, chip_buf, first_buf, sems):
    rows = chip_buf.shape[1]
    copies = []
    for piece in range(chip_buf.shape[0]):
        part = slice(piece * rows, (piece + 1) * rows)
        keep, got = keep_ref[part, :], got_ref[part, :]
        chip_buf[piece] = keep + got
        first_buf[piece] = jnp.where(core_ref[0] == 0, keep, got)
        for n, (buf, ref) in enumerate(((chip_buf, chip_ref), (first_buf, first_ref))):
            copy = pltpu.make_async_copy(buf.at[piece], ref.at[part, :], sems.at[n, piece])
            copy.start()
            copies.append(copy)
    for copy in copies:
        copy.wait()


def pair_states(core, keep, got):
    shape = pltpu.HBM(keep.shape, jnp.float32)
    buf = pltpu.VMEM((PIECE, keep.shape[0] // PIECE, E), jnp.float32)
    return pl.pallas_call(
        pair_kernel,
        in_specs=[SMEM, VMEM, VMEM],
        out_specs=(HBM, HBM),
        out_shape=(shape, shape),
        scratch_shapes=[buf, buf, pltpu.SemaphoreType.DMA((2, PIECE))],
        compiler_params=limit(6),
        name="pair",
    )(core, in_vmem(keep), in_vmem(got))


def shift_kernel(core_ref, before_ref, first_ref, out_ref):
    add = (core_ref[0] == 0).astype(jnp.float32)
    out_ref[...] = before_ref[...] + add * first_ref[...]


def for_sibling(core, before, first):
    return pl.pallas_call(
        shift_kernel,
        in_specs=[SMEM, VMEM, VMEM],
        out_specs=VMEM,
        out_shape=pltpu.VMEM(before.shape, jnp.float32),
        compiler_params=limit(6),
        name="for_sibling",
    )(core, in_vmem(before), in_vmem(first))


def scan_kernel(chips, x_ref, out_ref):
    rows = x_ref.shape[0] // chips
    total = jnp.zeros((rows, E), jnp.float32)
    for i in range(chips):
        part = slice(i * rows, (i + 1) * rows)
        out_ref[part, :] = total
        if i < chips - 1:
            total = total + x_ref[part, :]


def scan_chips(chips, x):
    return pl.pallas_call(
        functools.partial(scan_kernel, chips),
        in_specs=[VMEM],
        out_specs=VMEM,
        out_shape=pltpu.VMEM(x.shape, jnp.float32),
        compiler_params=limit(4),
        name="chip_scan",
    )(in_vmem(x))


def local_kernel(q_ref, k_ref, v_ref, out_ref):
    rows, width = q_ref.shape
    causal = lax.broadcasted_iota(jnp.int32, (rows, rows), 0) >= lax.broadcasted_iota(
        jnp.int32, (rows, rows), 1
    )
    for h in range(width // E):
        cols = slice(h * E, (h + 1) * E)
        scores = lax.dot_general(
            q_ref[:, cols],
            k_ref[:, cols],
            (((1,), (1,)), ((), ())),
            preferred_element_type=jnp.float32,
        )
        weights = jnp.where(causal, scores, 0.0).astype(jnp.bfloat16)
        out_ref[:, cols] = jnp.dot(weights, v_ref[:, cols], preferred_element_type=jnp.float32)


def local_mix(queries, keys, values):
    rows, width = queries.shape
    block = pl.BlockSpec((rows, 8 * E), lambda i: (0, i))
    return pl.pallas_call(
        local_kernel,
        grid=(width // (8 * E),),
        in_specs=[block, block, block],
        out_specs=block,
        out_shape=pltpu.HBM(queries.shape, jnp.float32),
        compiler_params=limit(24),
        name="local",
    )(queries, keys, values)


def finish_kernel(core_ref, q_ref, m_ref, p_ref, first_ref, gain_ref, *rest):
    out_ref, buf, sems = rest[-3:]
    heads = p_ref.shape[0] // E
    base = core_ref[0] * E
    stores = []
    for piece in range(heads // PIECE):
        for h in range(PIECE):
            here = (piece * PIECE + h) * E
            cols = lane_tile(base + here, E)
            low = p_ref[here : here + E, :]
            if first_ref is not None:
                low = low + core_ref[1].astype(jnp.float32) * first_ref[here : here + E, :]
            mixed = m_ref[:, cols] + jnp.dot(
                q_ref[:, cols], low.astype(jnp.bfloat16), preferred_element_type=jnp.float32
            )
            meansq = jnp.mean(mixed * mixed, axis=-1, keepdims=True)
            normed = mixed * lax.rsqrt(meansq + 1e-6) * gain_ref[:, cols]
            buf[piece, :, h * E : (h + 1) * E] = normed.astype(jnp.bfloat16)
        copy = pltpu.make_async_copy(
            buf.at[piece], out_ref.at[:, lane_tile(base + piece * WIDTH, WIDTH)], sems.at[piece]
        )
        copy.start()
        stores.append(copy)
    for copy in stores:
        copy.wait()


def finish_mine_kernel(core_ref, q_ref, m_ref, p_ref, first_ref, gain_ref, *rest):
    finish_kernel(core_ref, q_ref, m_ref, p_ref, first_ref, gain_ref, *rest)


def finish_other_kernel(core_ref, q_ref, m_ref, p_ref, gain_ref, *rest):
    finish_kernel(core_ref, q_ref, m_ref, p_ref, None, gain_ref, *rest)


def finish(core, queries, mixed, prefix, first, gain, base):
    rows = queries.shape[0]
    pieces = prefix.shape[0] // E // PIECE
    args = [core, in_vmem(queries), in_vmem(mixed), in_vmem(prefix)]
    in_specs = [SMEM, VMEM, VMEM, VMEM]
    if first is not None:
        args.append(in_vmem(first))
        in_specs.append(VMEM)
    args.append(gain)
    in_specs.append(VMEM)
    aliases = {}
    if base is not None:
        in_specs.append(HBM)
        args.append(in_hbm(base))
        aliases = {len(args) - 1: 0}
    return pl.pallas_call(
        finish_other_kernel if first is None else finish_mine_kernel,
        in_specs=in_specs,
        out_specs=HBM,
        out_shape=pltpu.HBM(queries.shape, jnp.bfloat16),
        scratch_shapes=[
            pltpu.VMEM((pieces, rows, WIDTH), jnp.bfloat16),
            pltpu.SemaphoreType.DMA((pieces,)),
        ],
        input_output_aliases=aliases,
        compiler_params=limit(6),
        name="finish",
    )(*args)


def shards(queries, keys, values, gain):
    devices = lax.axis_size("grp") * lax.axis_size("seq")
    chips = devices // 2
    core = lax.rem(lax.axis_index("seq"), 2).astype(jnp.int32)
    sibling = [(i, i ^ 1) for i in range(devices)]
    groups = [[2 * i + c for i in range(chips)] for c in (0, 1)]
    gain = gain.reshape(1, H * E)
    which = core.reshape(1)
    mine = jnp.stack([core * HALF, core])
    other = jnp.stack([(1 - core) * HALF, core])

    def exchange(x):
        return lax.all_to_all(x, AXES, 0, 0, axis_index_groups=groups, tiled=True)

    send = states_of(other, HALF, keys, values)
    got = lax.ppermute(send, AXES, sibling)
    keep = states_of(mine, HALF, keys, values)
    chip, first = pair_states(which, keep, got)
    chip, queries = lax.optimization_barrier((chip, queries))
    everyone = exchange(chip)
    mixed = local_mix(in_hbm(queries), in_hbm(keys), in_hbm(values))
    everyone, mixed = lax.optimization_barrier((everyone, mixed))
    before = exchange(scan_chips(chips, everyone))
    prefix_other = lax.ppermute(for_sibling(which, before, first), AXES, sibling)
    out = finish(mine, queries, mixed, before, first, gain, None)
    return finish(other, queries, mixed, prefix_other, None, gain, out)


def solution(mesh):
    rows = P(("grp", "seq"), None)
    return jax.shard_map(
        shards, mesh=mesh, in_specs=(rows, rows, rows, P()), out_specs=rows, check_vma=False
    )
```

time: 100 us -> 82 us (0.82)
  waiting for transfers between devices: 27 us -> 17.5 us
  blocking collectives: 36 us -> 30.5 us
  starting transfers between devices: 4.11 us -> 8.53 us
  Pallas kernels: 28.7 us -> 24.8 us
  other arithmetic: 2.86 us -> 0.15 us
    all_to_all x1, waiting for transfers between devices: 27 us -> 17.5 us  [exchange(): return lax.all_to_all(x, AXES, 0, 0, axis_index_groups=groups, tiled=True)]
    all_to_all x1, blocking collectives: 36 us -> 30.5 us  [exchange(): return lax.all_to_all(x, AXES, 0, 0, axis_index_groups=groups, tiled=True)]
    all_to_all x1, starting transfers between devices: 3.65 us -> 7.94 us  [exchange(): return lax.all_to_all(x, AXES, 0, 0, axis_index_groups=groups, tiled=True)]
    pallas_call x5 -> x8, Pallas kernels: 28.7 us -> 24.8 us  [the longest x1 10.6 us: local_mix(): pl.pallas_call(local_kernel, grid=(width // (8 * E),), in_specs=[block, b...]
    add x2 -> x0, other arithmetic: 2.86 us -> none  [the longest x1 1.53 us: shards(): prefix_mine = before + jnp.where(second, got, 0.0)]
  transfers between devices with their start and end apart: 3 -> 3, of which waited for: 1 -> 1; matrix products, arithmetic and copies ran while one was open for 0% -> 0% of each run, Pallas kernels for 13% -> 20%
where the time goes in v2:
time: 82 us; the launch traced here: 81.7 us
  blocking collectives  30.5 us (37%)
  Pallas kernels  24.8 us (30%)
  waiting for transfers between devices  17.5 us (21%)
  starting transfers between devices  8.53 us (10%)
    all_to_all x1, blocking collectives, exchange(): return lax.all_to_all(x, AXES, 0, 0, axis_index_groups=groups, tiled=True)  30.5 us
    all_to_all x1, waiting for transfers between devices, exchange(): return lax.all_to_all(x, AXES, 0, 0, axis_index_groups=groups, tiled=True)  17.5 us
    pallas_call x1, Pallas kernels, local_mix(): pl.pallas_call(local_kernel, grid=(width // (8 * E),), in_specs=[block, b...  10.6 us
    all_to_all x1, starting transfers between devices, exchange(): return lax.all_to_all(x, AXES, 0, 0, axis_index_groups=groups, tiled=True)  7.94 us
    pallas_call x2, Pallas kernels, states_of(): pl.pallas_call(state_kernel, in_specs=[SMEM, HBM, HBM], out_specs=VMEM, o...  5.95 us
    pallas_call x2, Pallas kernels, finish(): pl.pallas_call(finish_other_kernel if first is None else finish_mine_kern...  5.21 us
  transfers between devices with their start and end apart: 3, of which 1 were waited for; matrix products, arithmetic and copies ran while one was open for 0% of the time, Pallas kernels for 20%

profile of v2, /device:TPU:0, one launch (start us, length us, event | category | flops | bytes accessed | tf_op | source)
XLA Modules:
  0.0 81.7 jit_solution(17727412044571354658)
XLA Ops:
  0.0 0.1 pad_add_fusion.first_ref.core_ref
  0.1 3.0 %states.3 = f32[2048,128]{1,0:T(8,128)S(1)} custom-call(s32[2]{0:T(128)S(1)} %pad_add_fusion.first_ref.core_ref, bf16[384,4096]{1,0:T(8,128)(2,1)} %k_ref.5, bf16[384,4096]{1,0:T(8,128)(2,1)} %v_ref.5), custom_call_target="tpu_custom_call" | custom-call | tf_op jit(solution)/shard_map/states/pallas_call | solution.py:67
  3.1 0.5 collective-permute-start
  3.6 0.1 pad_add_fusion.1.first_ref.core_ref
  3.7 3.0 %states.2.keep_ref = f32[2048,128]{1,0:T(8,128)S(1)} custom-call(s32[2]{0:T(128)S(1)} %pad_add_fusion.1.first_ref.core_ref, bf16[384,4096]{1,0:T(8,128)(2,1)} %k_ref.5, bf16[384,4096]{1,0:T(8,128)(2,1)} %v_ref.5), custom_call_target="tpu_custom_call" | custom-call | tf_op jit(solution)/shard_map/states/pallas_call | solution.py:67
  6.6 0.0 collective-permute-done.got_ref
  6.6 1.4 %pair.1 = (f32[2048,128]{1,0:T(8,128)}, f32[2048,128]{1,0:T(8,128)}) custom-call(s32[1]{0:T(128)} %bitcast.1.core_ref, f32[2048,128]{1,0:T(8,128)S(1)} %states.2.keep_ref, f32[2048,128]{1,0:T(8,128)S(1)} %collective-permute-done.got_ref), custom_call_target="tpu_custom_call" | custom-call | tf_op jit(solution)/shard_map/pair/pallas_call | solution.py:101
  8.1 7.9 %all-to-all-start = ((f32[16,128,128]{2,1,0:T(8,128)}), f32[16,128,128]{2,1,0:T(8,128)}, u32[]{:S(2)}, u32[]{:S(2)}) async-start(f32[16,128,128]{2,1,0:T(8,128)} %bitcast.13), calls=%async_computation | async-start | bytes 2097152 | tf_op jit(solution)/shard_map/all_to_all | solution.py:257
  16.0 0.0 copy-start.1
  16.1 0.0 copy-start.3
  16.1 10.6 %local.1.m_ref = f32[384,4096]{1,0:T(8,128)} custom-call(bf16[384,4096]{1,0:T(8,128)(2,1)} %q_ref.2, bf16[384,4096]{1,0:T(8,128)(2,1)} %k_ref.5, bf16[384,4096]{1,0:T(8,128)(2,1)} %v_ref.5), custom_call_target="tpu_custom_call" | custom-call | tf_op jit(solution)/shard_map/local/pallas_call | solution.py:169
  26.7 17.5 %all-to-all-done = f32[16,128,128]{2,1,0:T(8,128)} async-done(((f32[16,128,128]{2,1,0:T(8,128)}), f32[16,128,128]{2,1,0:T(8,128)}, u32[]{:S(2)}, u32[]{:S(2)}) %all-to-all-start) | async-done | bytes 1048608 | tf_op jit(solution)/shard_map/all_to_all | solution.py:257
  44.2 0.0 copy-start.2
  44.2 0.0 copy-start
  44.2 1.4 %chip_scan.1 = f32[2048,128]{1,0:T(8,128)S(1)} custom-call(f32[2048,128]{1,0:T(8,128)} %bitcast.4.x_ref), custom_call_target="tpu_custom_call" | custom-call | tf_op jit(solution)/shard_map/chip_scan/pallas_call | solution.py:139
  45.7 30.5 %all_to_all.23 = f32[16,128,128]{2,1,0:T(8,128)S(1)} all-to-all(f32[16,128,128]{2,1,0:T(8,128)S(1)} %bitcast.10), channel_id=1, replica_groups={{0,2,4,6,8,10,12,14,16,18,20,22,24,26,28,30},{1,3,5,7,9,11,13,15,17,19,..., dimensions={0} | all-to-all | bytes 2097152 | tf_op jit(solution)/shard_map/all_to_all | solution.py:257
  76.2 0.0 copy-done.2
  76.2 0.1 for_sibling.1
  76.3 0.1 collective-permute-start.1
  76.4 0.0 copy-done.1
  76.4 0.0 copy-done.3
  76.4 0.0 copy-done
  76.4 2.6 %finish.2.rest_0_ = bf16[384,4096]{1,0:T(8,128)(2,1)} custom-call(s32[2]{0:T(128)S(1)} %pad_add_fusion.1.first_ref.core_ref, bf16[384,4096]{1,0:T(8,128)(2,1)S(1)} %copy-done.1, f32[384,4096]{1,0:T(8,128)S(1)} %copy-done, f32[2048,128]{1,0:T(8,128)S(1)} %bitcast.9, f32[2048,128]{1,0:T(8,128)S(1)} %copy-done.2, f32[1,4096]{1,0:T(1,128)S(1)} %bitcast.11), custom_call_target="tpu_custom_call" | custom-call | tf_op jit(solution)/shard_map/finish/pallas_call | solution.py:230
  79.1 0.0 collective-permute-done.1.p_ref
  79.1 2.6 %finish.3 = bf16[384,4096]{1,0:T(8,128)(2,1)} custom-call(s32[2]{0:T(128)S(1)} %pad_add_fusion.first_ref.core_ref, bf16[384,4096]{1,0:T(8,128)(2,1)S(1)} %copy-done.1, f32[384,4096]{1,0:T(8,128)S(1)} %copy-done, f32[2048,128]{1,0:T(8,128)S(1)} %collective-permute-done.1.p_ref, f32[1,4096]{1,0:T(1,128)S(1)} %bitcast.12, ...), custom_call_target="tpu_custom_call", output_to_operand_aliasing={{}: (5, {})} | custom-call | tf_op jit(solution)/shard_map/finish/pallas_call | solution.py:230
Async XLA Ops:
  3.1 3.6 %collective-permute-start = (f32[2048,128]{1,0:T(8,128)S(1)}, f32[2048,128]{1,0:T(8,128)S(1)}, u32[]{:S(2)}, u32[]{:S(2)}) collective-permute-start(f32[2048,128]{1,0:T(8,128)S(1)} %states.3), channel_id=1, source_target_pairs={{0,1},{1,0},{2,3},{3,2},{4,5},{5,4},{6,7},{7,6},{8,9},{9,8},{10,11... | collective-permute-start | bytes 3145736 | tf_op jit(solution)/shard_map/ppermute | solution.py:260
  8.1 36.1 %all-to-all-start = ((f32[16,128,128]{2,1,0:T(8,128)}), f32[16,128,128]{2,1,0:T(8,128)}, u32[]{:S(2)}, u32[]{:S(2)}) async-start(f32[16,128,128]{2,1,0:T(8,128)} %bitcast.13), calls=%async_computation | async-start | bytes 2097152 | tf_op jit(solution)/shard_map/all_to_all | solution.py:257
  16.0 60.4 %copy-start.1 = (bf16[384,4096]{1,0:T(8,128)(2,1)S(1)}, bf16[384,4096]{1,0:T(8,128)(2,1)}, u32[]{:S(2)}) copy-start(bf16[384,4096]{1,0:T(8,128)(2,1)} %q_ref.2) | copy-start | bytes 9437188
  16.1 60.4 %copy-start.3 = (f32[4096]{0:T(1024)S(1)}, f32[4096]{0:T(1024)}, u32[]{:S(2)}) copy-start(f32[4096]{0:T(1024)} %param.7) | copy-start | bytes 49156
  44.2 32.0 %copy-start.2 = (f32[2048,128]{1,0:T(8,128)S(1)}, f32[2048,128]{1,0:T(8,128)}, u32[]{:S(2)}) copy-start(f32[2048,128]{1,0:T(8,128)} %get-tuple-element.16.first_ref) | copy-start | bytes 3145732
  44.2 32.2 %copy-start = (f32[384,4096]{1,0:T(8,128)S(1)}, f32[384,4096]{1,0:T(8,128)}, u32[]{:S(2)}) copy-start(f32[384,4096]{1,0:T(8,128)} %local.1.m_ref) | copy-start | bytes 18874372
  76.3 2.8 %collective-permute-start.1 = (f32[2048,128]{1,0:T(8,128)S(1)}, f32[2048,128]{1,0:T(8,128)S(1)}, u32[]{:S(2)}, u32[]{:S(2)}) collective-permute-start(f32[2048,128]{1,0:T(8,128)S(1)} %for_sibling.1), channel_id=1, source_target_pairs={{0,1},{1,0},{2,3},{3,2},{4,5},{5,4},{6,7},{7,6},{8,9},{9,8},{10,11... | collective-permute-start | bytes 3145736 | tf_op jit(solution)/shard_map/ppermute | solution.py:268

commit v3 on v0

v3 whole, which is shorter than its diff:
```python
import functools

import jax
import jax.numpy as jnp
from jax import lax
from jax.experimental import pallas as pl
from jax.experimental.pallas import tpu as pltpu
from jax.sharding import PartitionSpec as P

H = 32
E = 128
AXES = ("grp", "seq")
HALF = H // 2
CHUNKS = 2
HEADS = HALF // CHUNKS
PIECE = 4
WIDTH = PIECE * E


def limit(mebibytes):
    return pltpu.CompilerParams(vmem_limit_bytes=mebibytes * 1024 * 1024)


def lane_tile(start, size):
    return pl.ds(pl.multiple_of(start, E), size)


def bit_of(level):
    index, length = lax.axis_index("seq"), lax.axis_size("seq")
    levels = length.bit_length() - 1
    if level < levels:
        return (index >> level) & 1
    return (lax.axis_index("grp") >> (level - levels)) & 1


def first_column(chunk, mine):
    core = bit_of(0)
    half = core if mine else 1 - core
    return (half * HALF + chunk * HEADS) * E


def state_kernel(chunk, mine, k_ref, v_ref, out_ref, k_buf, v_buf, sems):
    base = first_column(chunk, mine)
    copies = []
    for piece in range(HEADS // PIECE):
        for n, (ref, buf) in enumerate(((k_ref, k_buf), (v_ref, v_buf))):
            copy = pltpu.make_async_copy(
                ref.at[:, lane_tile(base + piece * WIDTH, WIDTH)],
                buf.at[piece],
                sems.at[n, piece],
            )
            copy.start()
            copies.append(copy)
    for piece in range(HEADS // PIECE):
        copies[2 * piece].wait()
        copies[2 * piece + 1].wait()
        for h in range(PIECE):
            cols = slice(h * E, (h + 1) * E)
            here = (piece * PIECE + h) * E
            out_ref[here : here + E, :] = lax.dot_general(
                k_buf[piece, :, cols],
                v_buf[piece, :, cols],
                (((0,), (0,)), ((), ())),
                preferred_element_type=jnp.float32,
            )


def call(kernel, name, arrays, shapes, scratch=(), tie=(), alias=None, mebibytes=4):
    count, operands = len(arrays), list(arrays) + list(tie)

    def body(*refs):
        kernel(*refs[:count], *refs[len(operands) :])

    return pl.pallas_call(
        body,
        in_specs=[pl.BlockSpec(memory_space=space) for _, space in operands],
        out_specs=tuple(pl.BlockSpec(memory_space=space) for space, _, _ in shapes),
        out_shape=tuple(space(shape, kind) for space, shape, kind in shapes),
        scratch_shapes=scratch,
        input_output_aliases={} if alias is None else {alias: 0},
        compiler_params=limit(mebibytes),
        name=name,
    )(*[pltpu.with_memory_space_constraint(x, space) for x, space in operands])


def states_of(chunk, mine, keys, values, tie):
    pieces = HEADS // PIECE
    buf = pltpu.VMEM((pieces, keys.shape[0], WIDTH), jnp.bfloat16)
    return call(
        functools.partial(state_kernel, chunk, mine),
        "states",
        [(keys, pltpu.HBM), (values, pltpu.HBM)],
        [(pltpu.VMEM, (HEADS * E, E), jnp.float32)],
        [buf, buf, pltpu.SemaphoreType.DMA((2, pieces))],
        tie,
        mebibytes=6,
    )[0]


def vmem_call(kernel, name, shapes, tie, *arrays):
    return call(
        kernel,
        name,
        [(x, pltpu.VMEM) for x in arrays],
        [(pltpu.VMEM, shape, jnp.float32) for shape in shapes],
        tie=tie,
    )


def up_kernel(level, halve, keep_ref, got_ref, low_ref, *outs):
    keep, got = keep_ref[...], got_ref[...]
    low_ref[...] = jnp.where(bit_of(level) == 0, keep, got)
    total = keep + got
    if not halve:
        outs[0][...] = total
        return
    rows = total.shape[0] // 2
    one, two = total[:rows], total[rows:]
    lower = bit_of(level + 1) == 0
    outs[0][...] = jnp.where(lower, one, two)
    outs[1][...] = jnp.where(lower, two, one)


def go_up(level, halve, keep, got, tie):
    rows = keep.shape[0]
    shapes = [(rows, E)] + ([(rows // 2, E)] * 2 if halve else [(rows, E)])
    kernel = functools.partial(up_kernel, level, halve)
    return vmem_call(kernel, "up", shapes, tie, keep, got)


def group_kernel(bit, total_ref, got_ref, *refs):
    before_ref = refs[0] if len(refs) == 3 else None
    sum_ref, out_ref = refs[-2:]
    got = got_ref[...]
    before = jnp.where(bit_of(bit) == 0, 0.0, got)
    if before_ref is not None:
        before = before + before_ref[...]
    out_ref[...] = before
    sum_ref[...] = total_ref[...] + got


def go_along(bit, total, got, before, tie):
    arrays = [total, got] + ([] if before is None else [before])
    kernel = functools.partial(group_kernel, bit)
    return vmem_call(kernel, "group", [total.shape] * 2, tie, *arrays)


def split(level, before, low, own_ref, send_ref):
    lower = bit_of(level) == 0
    own_ref[...] = before + jnp.where(lower, 0.0, low)
    send_ref[...] = before + jnp.where(lower, low, 0.0)


def top_kernel(bit, level, got_ref, low_ref, *refs):
    own_ref, send_ref = refs[-2:]
    before = jnp.where(bit_of(bit) == 0, 0.0, got_ref[...])
    if len(refs) == 3:
        before = before + refs[0][...]
    split(level, before, low_ref[...], own_ref, send_ref)


def turn_down(bit, level, got, low, before, tie):
    arrays = [got, low] + ([] if before is None else [before])
    kernel = functools.partial(top_kernel, bit, level)
    return vmem_call(kernel, "top", [low.shape] * 2, tie, *arrays)


def down_kernel(level, own_ref, got_ref, low_ref, next_ref, send_ref):
    lower = bit_of(level + 1) == 0
    own, got = own_ref[...], got_ref[...]
    before = jnp.concatenate([jnp.where(lower, own, got), jnp.where(lower, got, own)], axis=0)
    split(level, before, low_ref[...], next_ref, send_ref)


def go_down(level, own, got, low, tie):
    kernel = functools.partial(down_kernel, level)
    return vmem_call(kernel, "down", [low.shape] * 2, tie, own, got, low)


def local_kernel(chunk, mine, q_ref, k_ref, v_ref, out_ref):
    rows = q_ref.shape[0]
    base = first_column(chunk, mine)
    causal = lax.broadcasted_iota(jnp.int32, (rows, rows), 0) >= lax.broadcasted_iota(
        jnp.int32, (rows, rows), 1
    )
    for h in range(HEADS):
        cols = lane_tile(base + h * E, E)
        scores = lax.dot_general(
            q_ref[:, cols],
            k_ref[:, cols],
            (((1,), (1,)), ((), ())),
            preferred_element_type=jnp.float32,
        )
        weights = jnp.where(causal, scores, 0.0).astype(jnp.bfloat16)
        out_ref[:, h * E : (h + 1) * E] = jnp.dot(
            weights, v_ref[:, cols], preferred_element_type=jnp.float32
        )


def local_mix(chunk, mine, queries, keys, values, tie):
    return call(
        functools.partial(local_kernel, chunk, mine),
        "local",
        [(queries, pltpu.VMEM), (keys, pltpu.VMEM), (values, pltpu.VMEM)],
        [(pltpu.VMEM, (queries.shape[0], HEADS * E), jnp.float32)],
        tie=tie,
        mebibytes=8,
    )[0]


def finish_kernel(chunk, mine, q_ref, m_ref, p_ref, gain_ref, *rest):
    out_ref, buf, sems = rest[-3:]
    base = first_column(chunk, mine)
    stores = []
    for piece in range(HEADS // PIECE):
        for h in range(PIECE):
            here = (piece * PIECE + h) * E
            cols = lane_tile(base + here, E)
            low = p_ref[here : here + E, :].astype(jnp.bfloat16)
            mixed = m_ref[:, here : here + E] + jnp.dot(
                q_ref[:, cols], low, preferred_element_type=jnp.float32
            )
            meansq = jnp.mean(mixed * mixed, axis=-1, keepdims=True)
            normed = mixed * lax.rsqrt(meansq + 1e-6) * gain_ref[:, cols]
            buf[piece, :, h * E : (h + 1) * E] = normed.astype(jnp.bfloat16)
        copy = pltpu.make_async_copy(
            buf.at[piece], out_ref.at[:, lane_tile(base + piece * WIDTH, WIDTH)], sems.at[piece]
        )
        copy.start()
        stores.append(copy)
    for copy in stores:
        copy.wait()


def finish(chunk, mine, queries, mixed, prefix, gain, out, tie):
    pieces = HEADS // PIECE
    arrays = [(queries, pltpu.VMEM), (mixed, pltpu.VMEM), (prefix, pltpu.VMEM), (gain, pltpu.VMEM)]
    if out is not None:
        arrays.append((out, pltpu.HBM))
    return call(
        functools.partial(finish_kernel, chunk, mine),
        "finish",
        arrays,
        [(pltpu.HBM, queries.shape, jnp.bfloat16)],
        [
            pltpu.VMEM((pieces, queries.shape[0], WIDTH), jnp.bfloat16),
            pltpu.SemaphoreType.DMA((pieces,)),
        ],
        tie,
        None if out is None else 4,
        mebibytes=6,
    )[0]


def shards(queries, keys, values, gain):
    groups, length = lax.axis_size("grp"), lax.axis_size("seq")
    devices = groups * length
    levels = length.bit_length() - 1
    group_bits = groups.bit_length() - 1
    gain = gain.reshape(1, H * E)
    chunks = range(CHUNKS)

    def swap(x, level):
        return lax.ppermute(x, AXES, [(i, i ^ (1 << level)) for i in range(devices)])

    latest = []

    def after(array, space=pltpu.VMEM):
        latest[:] = [(array, space)]
        return array

    todo = [(c, mine) for c in chunks for mine in (True, False)]
    mixed = {}

    def some_local():
        if todo:
            c, mine = todo.pop(0)
            mixed[c, mine] = after(local_mix(c, mine, queries, keys, values, latest))

    def up(level, c):
        halve = level < levels - 1
        low[c][level], keep[c], *send = go_up(level, halve, keep[c], got[c], latest)
        got[c] = swap(after(send[0] if halve else keep[c]), level + 1)

    keep, got = [None] * CHUNKS, [None] * CHUNKS
    low = [[None] * levels for _ in chunks]
    for c in chunks:
        got[c] = swap(after(states_of(c, False, keys, values, latest)), 0)
        keep[c] = after(states_of(c, True, keys, values, latest))
        up(0, c)
    some_local()
    for level in range(1, levels):
        for c in chunks:
            up(level, c)
        some_local()
    before = [None] * CHUNKS
    for bit in range(levels, levels + group_bits - 1):
        for c in chunks:
            keep[c], before[c] = go_along(bit, keep[c], got[c], before[c], latest)
            got[c] = swap(after(keep[c]), bit + 1)
        some_local()
    top, last_bit = levels - 1, levels + group_bits - 1
    for c in chunks:
        keep[c], send = turn_down(last_bit, top, got[c], low[c][top], before[c], latest)
        got[c] = swap(after(send), top)
    while todo:
        some_local()
    for level in range(top - 1, 0, -1):
        for c in chunks:
            keep[c], send = go_down(level, keep[c], got[c], low[c][level], latest)
            got[c] = swap(after(send), level)
    out = None
    for c in chunks:
        keep[c], send = go_down(0, keep[c], got[c], low[c][0], latest)
        got[c] = swap(after(send), 0)
        for mine, prefix in ((True, keep[c]), (False, got[c])):
            out = finish(c, mine, queries, mixed[c, mine], prefix, gain, out, latest)
            latest[:] = []
        after(out, pltpu.HBM)
    return out


def solution(mesh):
    rows = P(("grp", "seq"), None)
    return jax.shard_map(
        shards, mesh=mesh, in_specs=(rows, rows, rows, P()), out_specs=rows, check_vma=False
    )
```

time: 361 us -> 70.1 us (0.19)
  waiting for transfers between devices: 265 us -> 31.4 us
  other arithmetic: 51.1 us -> 0 us
  matrix products: 22.1 us -> 0 us
  Pallas kernels: 0 us -> 21 us
  starting transfers between devices: 0.04 us -> 17.3 us
  between operations: 13.2 us -> 0.27 us
  local copies, waits for them, and re-layouts: 9.61 us -> 0.03 us
    all_gather x2 -> x0, waiting for transfers between devices: 199 us -> none  [carried_in(): everything = lax.all_gather(value, axis)]
    psum x1 -> x0, waiting for transfers between devices: 65.6 us -> none  [shards(): group_sum = lax.psum(state, 'seq')]
    select_n x12 -> x0, other arithmetic: 48.6 us -> none  [turn(): return jnp.where(reached, new, before)]
    ppermute x0 -> x16, waiting for transfers between devices: none -> 31.4 us  [swap(): return lax.ppermute(x, AXES, [(i, i ^ 1 << level) for i in range(devices)])]
    dot_general x3 -> x0, matrix products: 22.1 us -> none  [the longest x1 11.3 us: shards(): jnp.einsum('hts,shf->thf', weights, vx, preferred_element_type=jnp.float32)]
    pallas_call x0 -> x26, Pallas kernels: none -> 21 us  [call(): pl.pallas_call(body, in_specs=[pl.BlockSpec(memory_space=space) for _, sp...]
    ppermute x0 -> x16, starting transfers between devices: none -> 17.3 us  [swap(): return lax.ppermute(x, AXES, [(i, i ^ 1 << level) for i in range(devices)])]
    reshape x1 -> x0, local copies, waits for them, and re-layouts: 4.78 us -> none  [shards(): kx = keys.reshape(rows, H, E)]
  transfers between devices with their start and end apart: 3 -> 16, of which waited for: 3 -> 12; matrix products, arithmetic and copies ran while one was open for 12% -> 0% of each run, Pallas kernels for 0% -> 22%
where the time goes in v3:
time: 70.1 us; the launch traced here: 69.9 us
  waiting for transfers between devices  31.4 us (45%)
  Pallas kernels  21 us (30%)
  starting transfers between devices  17.3 us (25%)
    ppermute x16, waiting for transfers between devices, swap(): return lax.ppermute(x, AXES, [(i, i ^ 1 << level) for i in range(devices)])  31.4 us
    pallas_call x26, Pallas kernels, call(): pl.pallas_call(body, in_specs=[pl.BlockSpec(memory_space=space) for _, sp...  21 us
    ppermute x16, starting transfers between devices, swap(): return lax.ppermute(x, AXES, [(i, i ^ 1 << level) for i in range(devices)])  17.3 us
  transfers between devices with their start and end apart: 16, of which 12 were waited for; matrix products, arithmetic and copies ran while one was open for 0% of the time, Pallas kernels for 22%

profile of v3, /device:TPU:0, one launch (start us, length us, event | category | flops | bytes accessed | tf_op | source)
XLA Modules:
  0.0 69.9 jit_solution(8106887692501725427)
XLA Ops:
  0.0 1.8 %states.4.refs_2_ = f32[1024,128]{1,0:T(8,128)S(1)} custom-call(bf16[384,4096]{1,0:T(8,128)(2,1)} %refs_1_.15, bf16[384,4096]{1,0:T(8,128)(2,1)} %refs_2_.7), custom_call_target="tpu_custom_call" | custom-call | tf_op jit(solution)/shard_map/states/pallas_call | solution.py:74
  1.8 0.5 collective-permute-start
  2.3 1.8 %states.5.refs_0_.refs_2_ = f32[1024,128]{1,0:T(8,128)S(1)} custom-call(bf16[384,4096]{1,0:T(8,128)(2,1)} %refs_1_.15, bf16[384,4096]{1,0:T(8,128)(2,1)} %refs_2_.7, f32[1024,128]{1,0:T(8,128)S(1)} %states.4.refs_2_), custom_call_target="tpu_custom_call" | custom-call | tf_op jit(solution)/shard_map/states/pallas_call | solution.py:74
  4.1 0.1 up.6
  4.2 1.9 %states.6.refs_2_ = f32[1024,128]{1,0:T(8,128)S(1)} custom-call(bf16[384,4096]{1,0:T(8,128)(2,1)} %refs_1_.15, bf16[384,4096]{1,0:T(8,128)(2,1)} %refs_2_.7, f32[512,128]{1,0:T(8,128)S(1)} %get-tuple-element.37.refs_2_), custom_call_target="tpu_custom_call" | custom-call | tf_op jit(solution)/shard_map/states/pallas_call | solution.py:74
  6.2 0.2 collective-permute-start.1
  6.4 3.0 %collective-permute-start.3 = (f32[512,128]{1,0:T(8,128)S(1)}, f32[512,128]{1,0:T(8,128)S(1)}, u32[]{:S(2)}, u32[]{:S(2)}) collective-permute-start(f32[512,128]{1,0:T(8,128)S(1)} %get-tuple-element.37.refs_2_), channel_id=1, source_target_pairs={{0,2},{1,3},{2,0},{3,1},{4,6},{5,7},{6,4},{7,5},{8,10},{9,11},{10,... | collective-permute-start | bytes 786440 | tf_op jit(solution)/shard_map/ppermute | solution.py:264
  9.3 1.8 %states.7.refs_0_.refs_2_ = f32[1024,128]{1,0:T(8,128)S(1)} custom-call(bf16[384,4096]{1,0:T(8,128)(2,1)} %refs_1_.15, bf16[384,4096]{1,0:T(8,128)(2,1)} %refs_2_.7, f32[1024,128]{1,0:T(8,128)S(1)} %states.6.refs_2_), custom_call_target="tpu_custom_call" | custom-call | tf_op jit(solution)/shard_map/states/pallas_call | solution.py:74
  11.1 0.1 up.7
  11.2 0.3 collective-permute-start.2
  11.5 1.8 %local.4.refs_2_.refs_1_ = f32[384,1024]{1,0:T(8,128)S(1)} custom-call(bf16[384,4096]{1,0:T(8,128)(2,1)S(1)} %copy-done.2, bf16[384,4096]{1,0:T(8,128)(2,1)S(1)} %copy-done, bf16[384,4096]{1,0:T(8,128)(2,1)S(1)} %copy-done.1, f32[512,128]{1,0:T(8,128)S(1)} %get-tuple-element.39.refs_3_), custom_call_target="tpu_custom_call" | custom-call | tf_op jit(solution)/shard_map/local/pallas_call | solution.py:74
  13.3 3.1 %collective-permute-done.3.refs_1_ = f32[512,128]{1,0:T(8,128)S(1)} collective-permute-done((f32[512,128]{1,0:T(8,128)S(1)}, f32[512,128]{1,0:T(8,128)S(1)}, u32[]{:S(2)}, u32[]{:S(2)}) %collective-permute-start.3) | collective-permute-done | bytes 262176 | tf_op jit(solution)/shard_map/ppermute | solution.py:264
  16.4 0.1 up.8
  16.5 3.1 %collective-permute-start.5 = (f32[256,128]{1,0:T(8,128)S(1)}, f32[256,128]{1,0:T(8,128)S(1)}, u32[]{:S(2)}, u32[]{:S(2)}) collective-permute-start(f32[256,128]{1,0:T(8,128)S(1)} %get-tuple-element.41.refs_2_), channel_id=1, source_target_pairs={{0,4},{1,5},{2,6},{3,7},{4,0},{5,1},{6,2},{7,3},{8,12},{9,13},{10,... | collective-permute-start | bytes 393224 | tf_op jit(solution)/shard_map/ppermute | solution.py:264
  19.6 4.7 %collective-permute-done.2.refs_1_ = f32[512,128]{1,0:T(8,128)S(1)} collective-permute-done((f32[512,128]{1,0:T(8,128)S(1)}, f32[512,128]{1,0:T(8,128)S(1)}, u32[]{:S(2)}, u32[]{:S(2)}) %collective-permute-start.2) | collective-permute-done | bytes 262176 | tf_op jit(solution)/shard_map/ppermute | solution.py:264
  24.3 0.1 up.9
  24.4 1.0 %collective-permute-start.4 = (f32[256,128]{1,0:T(8,128)S(1)}, f32[256,128]{1,0:T(8,128)S(1)}, u32[]{:S(2)}, u32[]{:S(2)}) collective-permute-start(f32[256,128]{1,0:T(8,128)S(1)} %get-tuple-element.43.refs_3_), channel_id=1, source_target_pairs={{0,4},{1,5},{2,6},{3,7},{4,0},{5,1},{6,2},{7,3},{8,12},{9,13},{10,... | collective-permute-start | bytes 393224 | tf_op jit(solution)/shard_map/ppermute | solution.py:264
  25.4 1.8 %local.5.refs_2_.refs_1_ = f32[384,1024]{1,0:T(8,128)S(1)} custom-call(bf16[384,4096]{1,0:T(8,128)(2,1)S(1)} %copy-done.2, bf16[384,4096]{1,0:T(8,128)(2,1)S(1)} %copy-done, bf16[384,4096]{1,0:T(8,128)(2,1)S(1)} %copy-done.1, f32[256,128]{1,0:T(8,128)S(1)} %get-tuple-element.43.refs_3_), custom_call_target="tpu_custom_call" | custom-call | tf_op jit(solution)/shard_map/local/pallas_call | solution.py:74
  27.2 1.6 %collective-permute-start.7 = (f32[256,128]{1,0:T(8,128)S(1)}, f32[256,128]{1,0:T(8,128)S(1)}, u32[]{:S(2)}, u32[]{:S(2)}) collective-permute-start(f32[256,128]{1,0:T(8,128)S(1)} %get-tuple-element.45.refs_2_.refs_0_), channel_id=1, source_target_pairs={{0,8},{1,9},{2,10},{3,11},{4,12},{5,13},{6,14},{7,15},{8,0},{9,1},... | collective-permute-start | bytes 393224 | tf_op jit(solution)/shard_map/ppermute | solution.py:264
  28.8 4.3 %collective-permute-done.4.refs_1_ = f32[256,128]{1,0:T(8,128)S(1)} collective-permute-done((f32[256,128]{1,0:T(8,128)S(1)}, f32[256,128]{1,0:T(8,128)S(1)}, u32[]{:S(2)}, u32[]{:S(2)}) %collective-permute-start.4) | collective-permute-done | bytes 131104 | tf_op jit(solution)/shard_map/ppermute | solution.py:264
  33.1 1.5 %collective-permute-start.6 = (f32[256,128]{1,0:T(8,128)S(1)}, f32[256,128]{1,0:T(8,128)S(1)}, u32[]{:S(2)}, u32[]{:S(2)}) collective-permute-start(f32[256,128]{1,0:T(8,128)S(1)} %get-tuple-element.46.refs_3_.refs_0_), channel_id=1, source_target_pairs={{0,8},{1,9},{2,10},{3,11},{4,12},{5,13},{6,14},{7,15},{8,0},{9,1},... | collective-permute-start | bytes 393224 | tf_op jit(solution)/shard_map/ppermute | solution.py:264
  34.6 1.8 %local.6.refs_2_.refs_1_ = f32[384,1024]{1,0:T(8,128)S(1)} custom-call(bf16[384,4096]{1,0:T(8,128)(2,1)S(1)} %copy-done.2, bf16[384,4096]{1,0:T(8,128)(2,1)S(1)} %copy-done, bf16[384,4096]{1,0:T(8,128)(2,1)S(1)} %copy-done.1, f32[256,128]{1,0:T(8,128)S(1)} %get-tuple-element.46.refs_3_.refs_0_), custom_call_target="tpu_custom_call" | custom-call | tf_op jit(solution)/shard_map/local/pallas_call | solution.py:74
  36.4 1.6 %collective-permute-start.9 = (f32[256,128]{1,0:T(8,128)S(1)}, f32[256,128]{1,0:T(8,128)S(1)}, u32[]{:S(2)}, u32[]{:S(2)}) collective-permute-start(f32[256,128]{1,0:T(8,128)S(1)} %get-tuple-element.47.refs_2_), channel_id=1, source_target_pairs={{0,16},{1,17},{2,18},{3,19},{4,20},{5,21},{6,22},{7,23},{8,24},{9,... | collective-permute-start | bytes 393224 | tf_op jit(solution)/shard_map/ppermute | solution.py:264
  38.0 0.6 collective-permute-done.6.refs_1_
  38.6 1.4 %collective-permute-start.8 = (f32[256,128]{1,0:T(8,128)S(1)}, f32[256,128]{1,0:T(8,128)S(1)}, u32[]{:S(2)}, u32[]{:S(2)}) collective-permute-start(f32[256,128]{1,0:T(8,128)S(1)} %get-tuple-element.48.refs_3_), channel_id=1, source_target_pairs={{0,16},{1,17},{2,18},{3,19},{4,20},{5,21},{6,22},{7,23},{8,24},{9,... | collective-permute-start | bytes 393224 | tf_op jit(solution)/shard_map/ppermute | solution.py:264
  40.1 1.8 %local.7.refs_3_.refs_1_ = f32[384,1024]{1,0:T(8,128)S(1)} custom-call(bf16[384,4096]{1,0:T(8,128)(2,1)S(1)} %copy-done.2, bf16[384,4096]{1,0:T(8,128)(2,1)S(1)} %copy-done, bf16[384,4096]{1,0:T(8,128)(2,1)S(1)} %copy-done.1, f32[256,128]{1,0:T(8,128)S(1)} %get-tuple-element.48.refs_3_), custom_call_target="tpu_custom_call" | custom-call | tf_op jit(solution)/shard_map/local/pallas_call | solution.py:74
  41.8 0.8 %collective-permute-done.9.refs_0_ = f32[256,128]{1,0:T(8,128)S(1)} collective-permute-done((f32[256,128]{1,0:T(8,128)S(1)}, f32[256,128]{1,0:T(8,128)S(1)}, u32[]{:S(2)}, u32[]{:S(2)}) %collective-permute-start.9) | collective-permute-done | bytes 131104 | tf_op jit(solution)/shard_map/ppermute | solution.py:264
  42.7 0.1 collective-permute-start.11
  42.8 1.6 %collective-permute-done.8.refs_0_ = f32[256,128]{1,0:T(8,128)S(1)} collective-permute-done((f32[256,128]{1,0:T(8,128)S(1)}, f32[256,128]{1,0:T(8,128)S(1)}, u32[]{:S(2)}, u32[]{:S(2)}) %collective-permute-start.8) | collective-permute-done | bytes 131104 | tf_op jit(solution)/shard_map/ppermute | solution.py:264
  44.4 4.6 %collective-permute-done.11.refs_1_ = f32[256,128]{1,0:T(8,128)S(1)} collective-permute-done((f32[256,128]{1,0:T(8,128)S(1)}, f32[256,128]{1,0:T(8,128)S(1)}, u32[]{:S(2)}, u32[]{:S(2)}) %collective-permute-start.11) | collective-permute-done | bytes 131104 | tf_op jit(solution)/shard_map/ppermute | solution.py:264
  49.0 0.1 down.4
  49.1 0.1 collective-permute-start.13
  49.2 2.5 %collective-permute-start.10 = (f32[256,128]{1,0:T(8,128)S(1)}, f32[256,128]{1,0:T(8,128)S(1)}, u32[]{:S(2)}, u32[]{:S(2)}) collective-permute-start(f32[256,128]{1,0:T(8,128)S(1)} %get-tuple-element.55.refs_3_), channel_id=1, source_target_pairs={{0,4},{1,5},{2,6},{3,7},{4,0},{5,1},{6,2},{7,3},{8,12},{9,13},{10,... | collective-permute-start | bytes 393224 | tf_op jit(solution)/shard_map/ppermute | solution.py:264
  51.7 3.5 %collective-permute-done.10.refs_1_ = f32[256,128]{1,0:T(8,128)S(1)} collective-permute-done((f32[256,128]{1,0:T(8,128)S(1)}, f32[256,128]{1,0:T(8,128)S(1)}, u32[]{:S(2)}, u32[]{:S(2)}) %collective-permute-start.10) | collective-permute-done | bytes 131104 | tf_op jit(solution)/shard_map/ppermute | solution.py:264
  55.2 0.1 down.5
  55.3 2.1 %collective-permute-done.13.refs_1_ = f32[512,128]{1,0:T(8,128)S(1)} collective-permute-done((f32[512,128]{1,0:T(8,128)S(1)}, f32[512,128]{1,0:T(8,128)S(1)}, u32[]{:S(2)}, u32[]{:S(2)}) %collective-permute-start.13) | collective-permute-done | bytes 262176 | tf_op jit(solution)/shard_map/ppermute | solution.py:264
  57.4 0.2 down.6
  57.5 0.1 collective-permute-start.14
  57.6 0.3 collective-permute-start.12
  57.9 1.4 %finish.4.refs_4_ = bf16[384,4096]{1,0:T(8,128)(2,1)} custom-call(bf16[384,4096]{1,0:T(8,128)(2,1)S(1)} %copy-done.2, f32[384,1024]{1,0:T(8,128)S(1)} %local.4.refs_2_.refs_1_, f32[1024,128]{1,0:T(8,128)S(1)} %get-tuple-element.66.refs_2_, f32[1,4096]{1,0:T(1,128)S(1)} %bitcast.1, f32[1024,128]{1,0:T(8,128)S(1)} %get-tuple-element.65.refs_4_), custom_call_target="tpu_custom_call" | custom-call | tf_op jit(solution)/shard_map/finish/pallas_call | solution.py:74
  59.3 0.2 collective-permute-done.14.refs_2_
  59.5 1.4 %finish.5.refs_3_.refs_4_ = bf16[384,4096]{1,0:T(8,128)(2,1)} custom-call(bf16[384,4096]{1,0:T(8,128)(2,1)S(1)} %copy-done.2, f32[384,1024]{1,0:T(8,128)S(1)} %local.5.refs_2_.refs_1_, f32[1024,128]{1,0:T(8,128)S(1)} %collective-permute-done.14.refs_2_, f32[1,4096]{1,0:T(1,128)S(1)} %bitcast.2, ...), custom_call_target="tpu_custom_call", output_to_operand_aliasing={{}: (4, {})} | custom-call | tf_op jit(solution)/shard_map/finish/pallas_call | solution.py:74
  61.0 5.4 %collective-permute-done.12.refs_1_ = f32[512,128]{1,0:T(8,128)S(1)} collective-permute-done((f32[512,128]{1,0:T(8,128)S(1)}, f32[512,128]{1,0:T(8,128)S(1)}, u32[]{:S(2)}, u32[]{:S(2)}) %collective-permute-start.12) | collective-permute-done | bytes 262176 | tf_op jit(solution)/shard_map/ppermute | solution.py:264
  66.3 0.2 down.7
  66.5 0.1 collective-permute-start.15
  66.6 1.5 %finish.6.refs_4_ = bf16[384,4096]{1,0:T(8,128)(2,1)} custom-call(bf16[384,4096]{1,0:T(8,128)(2,1)S(1)} %copy-done.2, f32[384,1024]{1,0:T(8,128)S(1)} %local.6.refs_2_.refs_1_, f32[1024,128]{1,0:T(8,128)S(1)} %get-tuple-element.68.refs_2_, f32[1,4096]{1,0:T(1,128)S(1)} %bitcast.3, ...), custom_call_target="tpu_custom_call", output_to_operand_aliasing={{}: (4, {})} | custom-call | tf_op jit(solution)/shard_map/finish/pallas_call | solution.py:74
  68.0 0.4 collective-permute-done.15.refs_2_
  68.5 1.4 %finish.7 = bf16[384,4096]{1,0:T(8,128)(2,1)} custom-call(bf16[384,4096]{1,0:T(8,128)(2,1)S(1)} %copy-done.2, f32[384,1024]{1,0:T(8,128)S(1)} %local.7.refs_3_.refs_1_, f32[1024,128]{1,0:T(8,128)S(1)} %collective-permute-done.15.refs_2_, f32[1,4096]{1,0:T(1,128)S(1)} %bitcast.4, bf16[384,4096]{1,0:T(8,128)(2,1)} %finish.6.refs_4_), custom_call_target="tpu_custom_call", output_to_operand_aliasing={{}: (4, {})} | custom-call | tf_op jit(solution)/shard_map/finish/pallas_call | solution.py:74
  (18 shorter events, 0.2 us)
Async XLA Ops:
  1.8 2.3 %collective-permute-start = (f32[1024,128]{1,0:T(8,128)S(1)}, f32[1024,128]{1,0:T(8,128)S(1)}, u32[]{:S(2)}, u32[]{:S(2)}) collective-permute-start(f32[1024,128]{1,0:T(8,128)S(1)} %states.4.refs_2_), channel_id=1, source_target_pairs={{0,1},{1,0},{2,3},{3,2},{4,5},{5,4},{6,7},{7,6},{8,9},{9,8},{10,11... | collective-permute-start | bytes 1572872 | tf_op jit(solution)/shard_map/ppermute | solution.py:264
  4.2 7.3 %copy-start.2 = (bf16[384,4096]{1,0:T(8,128)(2,1)S(1)}, bf16[384,4096]{1,0:T(8,128)(2,1)}, u32[]{:S(2)}) copy-start(bf16[384,4096]{1,0:T(8,128)(2,1)} %refs_0_.23) | copy-start | bytes 9437188
  6.2 5.3 %copy-start = (bf16[384,4096]{1,0:T(8,128)(2,1)S(1)}, bf16[384,4096]{1,0:T(8,128)(2,1)}, u32[]{:S(2)}) copy-start(bf16[384,4096]{1,0:T(8,128)(2,1)} %refs_1_.15) | copy-start | bytes 9437188
  6.2 5.3 %copy-start.1 = (bf16[384,4096]{1,0:T(8,128)(2,1)S(1)}, bf16[384,4096]{1,0:T(8,128)(2,1)}, u32[]{:S(2)}) copy-start(bf16[384,4096]{1,0:T(8,128)(2,1)} %refs_2_.7) | copy-start | bytes 9437188
  6.2 4.9 %collective-permute-start.1 = (f32[1024,128]{1,0:T(8,128)S(1)}, f32[1024,128]{1,0:T(8,128)S(1)}, u32[]{:S(2)}, u32[]{:S(2)}) collective-permute-start(f32[1024,128]{1,0:T(8,128)S(1)} %states.6.refs_2_), channel_id=1, source_target_pairs={{0,1},{1,0},{2,3},{3,2},{4,5},{5,4},{6,7},{7,6},{8,9},{9,8},{10,11... | collective-permute-start | bytes 1572872 | tf_op jit(solution)/shard_map/ppermute | solution.py:264
  6.4 10.1 %collective-permute-start.3 = (f32[512,128]{1,0:T(8,128)S(1)}, f32[512,128]{1,0:T(8,128)S(1)}, u32[]{:S(2)}, u32[]{:S(2)}) collective-permute-start(f32[512,128]{1,0:T(8,128)S(1)} %get-tuple-element.37.refs_2_), channel_id=1, source_target_pairs={{0,2},{1,3},{2,0},{3,1},{4,6},{5,7},{6,4},{7,5},{8,10},{9,11},{10,... | collective-permute-start | bytes 786440 | tf_op jit(solution)/shard_map/ppermute | solution.py:264
  11.2 13.1 %collective-permute-start.2 = (f32[512,128]{1,0:T(8,128)S(1)}, f32[512,128]{1,0:T(8,128)S(1)}, u32[]{:S(2)}, u32[]{:S(2)}) collective-permute-start(f32[512,128]{1,0:T(8,128)S(1)} %get-tuple-element.39.refs_3_), channel_id=1, source_target_pairs={{0,2},{1,3},{2,0},{3,1},{4,6},{5,7},{6,4},{7,5},{8,10},{9,11},{10,... | collective-permute-start | bytes 786440 | tf_op jit(solution)/shard_map/ppermute | solution.py:264
  16.5 10.7 %collective-permute-start.5 = (f32[256,128]{1,0:T(8,128)S(1)}, f32[256,128]{1,0:T(8,128)S(1)}, u32[]{:S(2)}, u32[]{:S(2)}) collective-permute-start(f32[256,128]{1,0:T(8,128)S(1)} %get-tuple-element.41.refs_2_), channel_id=1, source_target_pairs={{0,4},{1,5},{2,6},{3,7},{4,0},{5,1},{6,2},{7,3},{8,12},{9,13},{10,... | collective-permute-start | bytes 393224 | tf_op jit(solution)/shard_map/ppermute | solution.py:264
  24.4 8.7 %collective-permute-start.4 = (f32[256,128]{1,0:T(8,128)S(1)}, f32[256,128]{1,0:T(8,128)S(1)}, u32[]{:S(2)}, u32[]{:S(2)}) collective-permute-start(f32[256,128]{1,0:T(8,128)S(1)} %get-tuple-element.43.refs_3_), channel_id=1, source_target_pairs={{0,4},{1,5},{2,6},{3,7},{4,0},{5,1},{6,2},{7,3},{8,12},{9,13},{10,... | collective-permute-start | bytes 393224 | tf_op jit(solution)/shard_map/ppermute | solution.py:264
  27.2 9.2 %collective-permute-start.7 = (f32[256,128]{1,0:T(8,128)S(1)}, f32[256,128]{1,0:T(8,128)S(1)}, u32[]{:S(2)}, u32[]{:S(2)}) collective-permute-start(f32[256,128]{1,0:T(8,128)S(1)} %get-tuple-element.45.refs_2_.refs_0_), channel_id=1, source_target_pairs={{0,8},{1,9},{2,10},{3,11},{4,12},{5,13},{6,14},{7,15},{8,0},{9,1},... | collective-permute-start | bytes 393224 | tf_op jit(solution)/shard_map/ppermute | solution.py:264
  33.1 5.5 %collective-permute-start.6 = (f32[256,128]{1,0:T(8,128)S(1)}, f32[256,128]{1,0:T(8,128)S(1)}, u32[]{:S(2)}, u32[]{:S(2)}) collective-permute-start(f32[256,128]{1,0:T(8,128)S(1)} %get-tuple-element.46.refs_3_.refs_0_), channel_id=1, source_target_pairs={{0,8},{1,9},{2,10},{3,11},{4,12},{5,13},{6,14},{7,15},{8,0},{9,1},... | collective-permute-start | bytes 393224 | tf_op jit(solution)/shard_map/ppermute | solution.py:264
  36.4 6.2 %collective-permute-start.9 = (f32[256,128]{1,0:T(8,128)S(1)}, f32[256,128]{1,0:T(8,128)S(1)}, u32[]{:S(2)}, u32[]{:S(2)}) collective-permute-start(f32[256,128]{1,0:T(8,128)S(1)} %get-tuple-element.47.refs_2_), channel_id=1, source_target_pairs={{0,16},{1,17},{2,18},{3,19},{4,20},{5,21},{6,22},{7,23},{8,24},{9,... | collective-permute-start | bytes 393224 | tf_op jit(solution)/shard_map/ppermute | solution.py:264
  38.6 5.7 %collective-permute-start.8 = (f32[256,128]{1,0:T(8,128)S(1)}, f32[256,128]{1,0:T(8,128)S(1)}, u32[]{:S(2)}, u32[]{:S(2)}) collective-permute-start(f32[256,128]{1,0:T(8,128)S(1)} %get-tuple-element.48.refs_3_), channel_id=1, source_target_pairs={{0,16},{1,17},{2,18},{3,19},{4,20},{5,21},{6,22},{7,23},{8,24},{9,... | collective-permute-start | bytes 393224 | tf_op jit(solution)/shard_map/ppermute | solution.py:264
  41.8 16.1 %copy-start.3 = (f32[4096]{0:T(1024)S(1)}, f32[4096]{0:T(1024)}, u32[]{:S(2)}) copy-start(f32[4096]{0:T(1024)} %param.7) | copy-start | bytes 49156
  42.7 6.4 %collective-permute-start.11 = (f32[256,128]{1,0:T(8,128)S(1)}, f32[256,128]{1,0:T(8,128)S(1)}, u32[]{:S(2)}, u32[]{:S(2)}) collective-permute-start(f32[256,128]{1,0:T(8,128)S(1)} %get-tuple-element.53.refs_3_), channel_id=1, source_target_pairs={{0,4},{1,5},{2,6},{3,7},{4,0},{5,1},{6,2},{7,3},{8,12},{9,13},{10,... | collective-permute-start | bytes 393224 | tf_op jit(solution)/shard_map/ppermute | solution.py:264
  49.1 8.3 %collective-permute-start.13 = (f32[512,128]{1,0:T(8,128)S(1)}, f32[512,128]{1,0:T(8,128)S(1)}, u32[]{:S(2)}, u32[]{:S(2)}) collective-permute-start(f32[512,128]{1,0:T(8,128)S(1)} %get-tuple-element.59.refs_3_), channel_id=1, source_target_pairs={{0,2},{1,3},{2,0},{3,1},{4,6},{5,7},{6,4},{7,5},{8,10},{9,11},{10,... | collective-permute-start | bytes 786440 | tf_op jit(solution)/shard_map/ppermute | solution.py:264
  49.2 6.0 %collective-permute-start.10 = (f32[256,128]{1,0:T(8,128)S(1)}, f32[256,128]{1,0:T(8,128)S(1)}, u32[]{:S(2)}, u32[]{:S(2)}) collective-permute-start(f32[256,128]{1,0:T(8,128)S(1)} %get-tuple-element.55.refs_3_), channel_id=1, source_target_pairs={{0,4},{1,5},{2,6},{3,7},{4,0},{5,1},{6,2},{7,3},{8,12},{9,13},{10,... | collective-permute-start | bytes 393224 | tf_op jit(solution)/shard_map/ppermute | solution.py:264
  57.5 2.0 %collective-permute-start.14 = (f32[1024,128]{1,0:T(8,128)S(1)}, f32[1024,128]{1,0:T(8,128)S(1)}, u32[]{:S(2)}, u32[]{:S(2)}) collective-permute-start(f32[1024,128]{1,0:T(8,128)S(1)} %get-tuple-element.65.refs_4_), channel_id=1, source_target_pairs={{0,1},{1,0},{2,3},{3,2},{4,5},{5,4},{6,7},{7,6},{8,9},{9,8},{10,11... | collective-permute-start | bytes 1572872 | tf_op jit(solution)/shard_map/ppermute | solution.py:264
  57.6 8.7 %collective-permute-start.12 = (f32[512,128]{1,0:T(8,128)S(1)}, f32[512,128]{1,0:T(8,128)S(1)}, u32[]{:S(2)}, u32[]{:S(2)}) collective-permute-start(f32[512,128]{1,0:T(8,128)S(1)} %get-tuple-element.61.refs_3_), channel_id=1, source_target_pairs={{0,2},{1,3},{2,0},{3,1},{4,6},{5,7},{6,4},{7,5},{8,10},{9,11},{10,... | collective-permute-start | bytes 786440 | tf_op jit(solution)/shard_map/ppermute | solution.py:264
  66.5 2.0 %collective-permute-start.15 = (f32[1024,128]{1,0:T(8,128)S(1)}, f32[1024,128]{1,0:T(8,128)S(1)}, u32[]{:S(2)}, u32[]{:S(2)}) collective-permute-start(f32[1024,128]{1,0:T(8,128)S(1)} %get-tuple-element.67.refs_5_), channel_id=1, source_target_pairs={{0,1},{1,0},{2,3},{3,2},{4,5},{5,4},{6,7},{7,6},{8,9},{9,8},{10,11... | collective-permute-start | bytes 1572872 | tf_op jit(solution)/shard_map/ppermute | solution.py:264

commit v4 on v3

--- a/solution.py
+++ b/solution.py
@@ -65,7 +65,7 @@
             )
 
 
-def call(kernel, name, arrays, shapes, scratch=(), tie=(), alias=None, mebibytes=4):
+def call(kernel, name, arrays, shapes, scratch=(), tie=(), alias=None, mebibytes=4, flops=10**10):
     count, operands = len(arrays), list(arrays) + list(tie)
 
     def body(*refs):
@@ -79,6 +79,7 @@
         scratch_shapes=scratch,
         input_output_aliases={} if alias is None else {alias: 0},
         compiler_params=limit(mebibytes),
+        cost_estimate=pl.CostEstimate(flops=flops, bytes_accessed=1, transcendentals=0),
         name=name,
     )(*[pltpu.with_memory_space_constraint(x, space) for x, space in operands])
 
@@ -121,6 +122,10 @@
     outs[1][...] = jnp.where(lower, two, one)
 
 
+def copy_kernel(x_ref, out_ref):
+    out_ref[...] = x_ref[...]
+
+
 def go_up(level, halve, keep, got, tie):
     rows = keep.shape[0]
     shapes = [(rows, E)] + ([(rows // 2, E)] * 2 if halve else [(rows, E)])
@@ -128,21 +133,19 @@
     return vmem_call(kernel, "up", shapes, tie, keep, got)
 
 
-def group_kernel(bit, total_ref, got_ref, *refs):
-    before_ref = refs[0] if len(refs) == 3 else None
-    sum_ref, out_ref = refs[-2:]
-    got = got_ref[...]
+def group_kernel(bit, other, turned, total_ref, got_ref, before_ref, send_ref):
+    total, got = total_ref[...], got_ref[...]
     before = jnp.where(bit_of(bit) == 0, 0.0, got)
-    if before_ref is not None:
-        before = before + before_ref[...]
-    out_ref[...] = before
-    sum_ref[...] = total_ref[...] + got
-
-
-def go_along(bit, total, got, before, tie):
-    arrays = [total, got] + ([] if before is None else [before])
-    kernel = functools.partial(group_kernel, bit)
-    return vmem_call(kernel, "group", [total.shape] * 2, tie, *arrays)
+    before_ref[...] = before
+    if turned:
+        send_ref[...] = before + jnp.where(bit_of(other) == 0, total, 0.0)
+    else:
+        send_ref[...] = total + got
+
+
+def go_along(bit, other, turned, total, got, tie):
+    kernel = functools.partial(group_kernel, bit, other, turned)
+    return vmem_call(kernel, "group", [total.shape] * 2, tie, total, got)
 
 
 def split(level, before, low, own_ref, send_ref):
@@ -151,18 +154,16 @@
     send_ref[...] = before + jnp.where(lower, low, 0.0)
 
 
-def top_kernel(bit, level, got_ref, low_ref, *refs):
-    own_ref, send_ref = refs[-2:]
-    before = jnp.where(bit_of(bit) == 0, 0.0, got_ref[...])
-    if len(refs) == 3:
-        before = before + refs[0][...]
-    split(level, before, low_ref[...], own_ref, send_ref)
-
-
-def turn_down(bit, level, got, low, before, tie):
-    arrays = [got, low] + ([] if before is None else [before])
-    kernel = functools.partial(top_kernel, bit, level)
-    return vmem_call(kernel, "top", [low.shape] * 2, tie, *arrays)
+def top_kernel(bit, turned, level, got_ref, low_ref, before_ref, own_ref, send_ref):
+    got = got_ref[...]
+    if not turned:
+        got = jnp.where(bit_of(bit) == 0, 0.0, got)
+    split(level, before_ref[...] + got, low_ref[...], own_ref, send_ref)
+
+
+def turn_down(bit, turned, level, got, low, before, tie):
+    kernel = functools.partial(top_kernel, bit, turned, level)
+    return vmem_call(kernel, "top", [low.shape] * 2, tie, got, low, before)
 
 
 def down_kernel(level, own_ref, got_ref, low_ref, next_ref, send_ref):
@@ -177,35 +178,47 @@
     return vmem_call(kernel, "down", [low.shape] * 2, tie, own, got, low)
 
 
-def local_kernel(chunk, mine, q_ref, k_ref, v_ref, out_ref):
+def local_kernel(chunk, mine, q_ref, k_ref, v_ref, out_ref, q_out_ref, k_buf, v_buf, sems):
     rows = q_ref.shape[0]
     base = first_column(chunk, mine)
+    copies = []
+    for piece in range(HEADS // PIECE):
+        cols = lane_tile(base + piece * WIDTH, WIDTH)
+        here = slice(piece * WIDTH, (piece + 1) * WIDTH)
+        for n, (ref, buf) in enumerate(((q_ref, q_out_ref), (k_ref, k_buf), (v_ref, v_buf))):
+            copy = pltpu.make_async_copy(ref.at[:, cols], buf.at[:, here], sems.at[n, piece])
+            copy.start()
+            copies.append(copy)
     causal = lax.broadcasted_iota(jnp.int32, (rows, rows), 0) >= lax.broadcasted_iota(
         jnp.int32, (rows, rows), 1
     )
     for h in range(HEADS):
-        cols = lane_tile(base + h * E, E)
+        if h % PIECE == 0:
+            for n in range(3):
+                copies[h // PIECE * 3 + n].wait()
+        cols = slice(h * E, (h + 1) * E)
         scores = lax.dot_general(
-            q_ref[:, cols],
-            k_ref[:, cols],
+            q_out_ref[:, cols],
+            k_buf[:, cols],
             (((1,), (1,)), ((), ())),
             preferred_element_type=jnp.float32,
         )
         weights = jnp.where(causal, scores, 0.0).astype(jnp.bfloat16)
-        out_ref[:, h * E : (h + 1) * E] = jnp.dot(
-            weights, v_ref[:, cols], preferred_element_type=jnp.float32
-        )
+        out_ref[:, cols] = jnp.dot(weights, v_buf[:, cols], preferred_element_type=jnp.float32)
 
 
 def local_mix(chunk, mine, queries, keys, values, tie):
+    shape = (queries.shape[0], HEADS * E)
+    buf = pltpu.VMEM(shape, jnp.bfloat16)
     return call(
         functools.partial(local_kernel, chunk, mine),
         "local",
-        [(queries, pltpu.VMEM), (keys, pltpu.VMEM), (values, pltpu.VMEM)],
-        [(pltpu.VMEM, (queries.shape[0], HEADS * E), jnp.float32)],
-        tie=tie,
-        mebibytes=8,
-    )[0]
+        [(queries, pltpu.HBM), (keys, pltpu.HBM), (values, pltpu.HBM)],
+        [(pltpu.VMEM, shape, jnp.float32), (pltpu.VMEM, shape, jnp.bfloat16)],
+        [buf, buf, pltpu.SemaphoreType.DMA((3, HEADS // PIECE))],
+        tie,
+        mebibytes=10,
+    )
 
 
 def finish_kernel(chunk, mine, q_ref, m_ref, p_ref, gain_ref, *rest):
@@ -218,7 +231,7 @@
             cols = lane_tile(base + here, E)
             low = p_ref[here : here + E, :].astype(jnp.bfloat16)
             mixed = m_ref[:, here : here + E] + jnp.dot(
-                q_ref[:, cols], low, preferred_element_type=jnp.float32
+                q_ref[:, here : here + E], low, preferred_element_type=jnp.float32
             )
             meansq = jnp.mean(mixed * mixed, axis=-1, keepdims=True)
             normed = mixed * lax.rsqrt(meansq + 1e-6) * gain_ref[:, cols]
@@ -232,7 +245,7 @@
         copy.wait()
 
 
-def finish(chunk, mine, queries, mixed, prefix, gain, out, tie):
+def finish(chunk, mine, shape, mixed, queries, prefix, gain, out, tie):
     pieces = HEADS // PIECE
     arrays = [(queries, pltpu.VMEM), (mixed, pltpu.VMEM), (prefix, pltpu.VMEM), (gain, pltpu.VMEM)]
     if out is not None:
@@ -241,9 +254,9 @@
         functools.partial(finish_kernel, chunk, mine),
         "finish",
         arrays,
-        [(pltpu.HBM, queries.shape, jnp.bfloat16)],
+        [(pltpu.HBM, shape, jnp.bfloat16)],
         [
-            pltpu.VMEM((pieces, queries.shape[0], WIDTH), jnp.bfloat16),
+            pltpu.VMEM((pieces, shape[0], WIDTH), jnp.bfloat16),
             pltpu.SemaphoreType.DMA((pieces,)),
         ],
         tie,
@@ -256,7 +269,6 @@
     groups, length = lax.axis_size("grp"), lax.axis_size("seq")
     devices = groups * length
     levels = length.bit_length() - 1
-    group_bits = groups.bit_length() - 1
     gain = gain.reshape(1, H * E)
     chunks = range(CHUNKS)
 
@@ -275,14 +287,18 @@
     def some_local():
         if todo:
             c, mine = todo.pop(0)
-            mixed[c, mine] = after(local_mix(c, mine, queries, keys, values, latest))
+            mixed[c, mine] = local_mix(c, mine, queries, keys, values, latest)
+            after(mixed[c, mine][0])
+
+    order = [(levels, levels + 1), (levels + 1, levels)]
 
     def up(level, c):
         halve = level < levels - 1
         low[c][level], keep[c], *send = go_up(level, halve, keep[c], got[c], latest)
-        got[c] = swap(after(send[0] if halve else keep[c]), level + 1)
-
-    keep, got = [None] * CHUNKS, [None] * CHUNKS
+        along = level + 1 if halve else order[c % 2][0]
+        got[c] = swap(after(send[0] if halve else keep[c]), along)
+
+    keep, got, before = [None] * CHUNKS, [None] * CHUNKS, [None] * CHUNKS
     low = [[None] * levels for _ in chunks]
     for c in chunks:
         got[c] = swap(after(states_of(c, False, keys, values, latest)), 0)
@@ -292,19 +308,20 @@
     for level in range(1, levels):
         for c in chunks:
             up(level, c)
-        some_local()
-    before = [None] * CHUNKS
-    for bit in range(levels, levels + group_bits - 1):
-        for c in chunks:
-            keep[c], before[c] = go_along(bit, keep[c], got[c], before[c], latest)
-            got[c] = swap(after(keep[c]), bit + 1)
-        some_local()
-    top, last_bit = levels - 1, levels + group_bits - 1
+            if level == 1:
+                some_local()
     for c in chunks:
-        keep[c], send = turn_down(last_bit, top, got[c], low[c][top], before[c], latest)
+        bit, other = order[c % 2]
+        before[c], send = go_along(bit, other, c % 2 == 1, keep[c], got[c], latest)
+        got[c] = swap(after(send), other)
+    top = levels - 1
+    for c in chunks:
+        turned = c % 2 == 1
+        keep[c], send = turn_down(order[0][1], turned, top, got[c], low[c][top], before[c], latest)
         got[c] = swap(after(send), top)
     while todo:
         some_local()
+    gain = after(vmem_call(copy_kernel, "gain", [gain.shape], latest, gain)[0])
     for level in range(top - 1, 0, -1):
         for c in chunks:
             keep[c], send = go_down(level, keep[c], got[c], low[c][level], latest)
@@ -314,7 +331,7 @@
         keep[c], send = go_down(0, keep[c], got[c], low[c][0], latest)
         got[c] = swap(after(send), 0)
         for mine, prefix in ((True, keep[c]), (False, got[c])):
-            out = finish(c, mine, queries, mixed[c, mine], prefix, gain, out, latest)
+            out = finish(c, mine, queries.shape, *mixed[c, mine], prefix, gain, out, latest)
             latest[:] = []
         after(out, pltpu.HBM)
     return out

time: 70.1 us -> 67 us (0.956)
  Pallas kernels: 21 us -> 26.7 us
  waiting for transfers between devices: 31.4 us -> 26.6 us
  starting transfers between devices: 17.3 us -> 13.2 us
    pallas_call x26 -> x27, Pallas kernels: 21 us -> 26.7 us  [call(): pl.pallas_call(body, in_specs=[pl.BlockSpec(memory_space=space) for _, sp...]
    ppermute x16, waiting for transfers between devices: 31.4 us -> 26.6 us  [swap(): return lax.ppermute(x, AXES, [(i, i ^ 1 << level) for i in range(devices)])]
    ppermute x16, starting transfers between devices: 17.3 us -> 13.2 us  [swap(): return lax.ppermute(x, AXES, [(i, i ^ 1 << level) for i in range(devices)])]
  transfers between devices with their start and end apart: 16 -> 16, of which waited for: 12 -> 10; matrix products, arithmetic and copies ran while one was open for 0% -> 0% of each run, Pallas kernels for 22% -> 35%
where the time goes in v4:
time: 67 us; the launch traced here: 66.7 us
  Pallas kernels  26.7 us (40%)
  waiting for transfers between devices  26.6 us (40%)
  starting transfers between devices  13.2 us (20%)
    pallas_call x27, Pallas kernels, call(): pl.pallas_call(body, in_specs=[pl.BlockSpec(memory_space=space) for _, sp...  26.7 us
    ppermute x16, waiting for transfers between devices, swap(): return lax.ppermute(x, AXES, [(i, i ^ 1 << level) for i in range(devices)])  26.6 us
    ppermute x16, starting transfers between devices, swap(): return lax.ppermute(x, AXES, [(i, i ^ 1 << level) for i in range(devices)])  13.2 us
  transfers between devices with their start and end apart: 16, of which 10 were waited for; matrix products, arithmetic and copies ran while one was open for 0% of the time, Pallas kernels for 35%

profile of v4, /device:TPU:0, one launch (start us, length us, event | category | flops | bytes accessed | tf_op | source)
XLA Modules:
  0.0 66.7 jit_solution(17987254480577735144)
XLA Ops:
  0.0 1.8 %states.4.refs_2_ = f32[1024,128]{1,0:T(8,128)S(1)} custom-call(bf16[384,4096]{1,0:T(8,128)(2,1)} %refs_1_.15, bf16[384,4096]{1,0:T(8,128)(2,1)} %refs_2_.7), custom_call_target="tpu_custom_call" | custom-call | flops 10000000000 | bytes 1 | tf_op jit(solution)/shard_map/states/pallas_call | solution.py:74
  1.8 0.5 collective-permute-start
  2.3 1.8 %states.5.refs_0_.refs_2_ = f32[1024,128]{1,0:T(8,128)S(1)} custom-call(bf16[384,4096]{1,0:T(8,128)(2,1)} %refs_1_.15, bf16[384,4096]{1,0:T(8,128)(2,1)} %refs_2_.7, f32[1024,128]{1,0:T(8,128)S(1)} %states.4.refs_2_), custom_call_target="tpu_custom_call" | custom-call | flops 10000000000 | bytes 1 | tf_op jit(solution)/shard_map/states/pallas_call | solution.py:74
  4.1 0.1 up.6
  4.2 2.8 %collective-permute-start.3 = (f32[512,128]{1,0:T(8,128)S(1)}, f32[512,128]{1,0:T(8,128)S(1)}, u32[]{:S(2)}, u32[]{:S(2)}) collective-permute-start(f32[512,128]{1,0:T(8,128)S(1)} %get-tuple-element.45.refs_2_), channel_id=1, source_target_pairs={{0,2},{1,3},{2,0},{3,1},{4,6},{5,7},{6,4},{7,5},{8,10},{9,11},{10,... | collective-permute-start | bytes 786440 | tf_op jit(solution)/shard_map/ppermute | solution.py:276
  7.0 1.8 %states.6.refs_2_ = f32[1024,128]{1,0:T(8,128)S(1)} custom-call(bf16[384,4096]{1,0:T(8,128)(2,1)} %refs_1_.15, bf16[384,4096]{1,0:T(8,128)(2,1)} %refs_2_.7, f32[512,128]{1,0:T(8,128)S(1)} %get-tuple-element.45.refs_2_), custom_call_target="tpu_custom_call" | custom-call | flops 10000000000 | bytes 1 | tf_op jit(solution)/shard_map/states/pallas_call | solution.py:74
  8.8 0.1 collective-permute-start.1
  8.9 1.8 %states.7.refs_0_.refs_2_ = f32[1024,128]{1,0:T(8,128)S(1)} custom-call(bf16[384,4096]{1,0:T(8,128)(2,1)} %refs_1_.15, bf16[384,4096]{1,0:T(8,128)(2,1)} %refs_2_.7, f32[1024,128]{1,0:T(8,128)S(1)} %states.6.refs_2_), custom_call_target="tpu_custom_call" | custom-call | flops 10000000000 | bytes 1 | tf_op jit(solution)/shard_map/states/pallas_call | solution.py:74
  10.7 0.0 collective-permute-done.1.refs_1_
  10.7 0.1 up.7
  10.8 0.3 collective-permute-start.2
  11.2 3.2 %local.4 = (f32[384,1024]{1,0:T(8,128)S(1)}, bf16[384,1024]{1,0:T(8,128)(2,1)S(1)}) custom-call(bf16[384,4096]{1,0:T(8,128)(2,1)} %refs_0_.15, bf16[384,4096]{1,0:T(8,128)(2,1)} %refs_1_.15, bf16[384,4096]{1,0:T(8,128)(2,1)} %refs_2_.7, f32[512,128]{1,0:T(8,128)S(1)} %get-tuple-element.47.refs_3_), custom_call_target="tpu_custom_call" | custom-call | flops 10000000000 | bytes 1 | tf_op jit(solution)/shard_map/local/pallas_call | solution.py:74
  14.4 0.1 up.8
  14.5 2.8 %collective-permute-start.5 = (f32[256,128]{1,0:T(8,128)S(1)}, f32[256,128]{1,0:T(8,128)S(1)}, u32[]{:S(2)}, u32[]{:S(2)}) collective-permute-start(f32[256,128]{1,0:T(8,128)S(1)} %get-tuple-element.50.refs_3_), channel_id=1, source_target_pairs={{0,4},{1,5},{2,6},{3,7},{4,0},{5,1},{6,2},{7,3},{8,12},{9,13},{10,... | collective-permute-start | bytes 393224 | tf_op jit(solution)/shard_map/ppermute | solution.py:276
  17.3 3.2 %local.5 = (f32[384,1024]{1,0:T(8,128)S(1)}, bf16[384,1024]{1,0:T(8,128)(2,1)S(1)}) custom-call(bf16[384,4096]{1,0:T(8,128)(2,1)} %refs_0_.15, bf16[384,4096]{1,0:T(8,128)(2,1)} %refs_1_.15, bf16[384,4096]{1,0:T(8,128)(2,1)} %refs_2_.7, f32[256,128]{1,0:T(8,128)S(1)} %get-tuple-element.50.refs_3_), custom_call_target="tpu_custom_call" | custom-call | flops 10000000000 | bytes 1 | tf_op jit(solution)/shard_map/local/pallas_call | solution.py:74
  20.6 1.8 %collective-permute-done.2.refs_1_ = f32[512,128]{1,0:T(8,128)S(1)} collective-permute-done((f32[512,128]{1,0:T(8,128)S(1)}, f32[512,128]{1,0:T(8,128)S(1)}, u32[]{:S(2)}, u32[]{:S(2)}) %collective-permute-start.2) | collective-permute-done | bytes 262176 | tf_op jit(solution)/shard_map/ppermute | solution.py:276
  22.4 0.1 up.9
  22.4 0.3 collective-permute-start.4
  22.8 3.2 %local.6 = (f32[384,1024]{1,0:T(8,128)S(1)}, bf16[384,1024]{1,0:T(8,128)(2,1)S(1)}) custom-call(bf16[384,4096]{1,0:T(8,128)(2,1)} %refs_0_.15, bf16[384,4096]{1,0:T(8,128)(2,1)} %refs_1_.15, bf16[384,4096]{1,0:T(8,128)(2,1)} %refs_2_.7, f32[256,128]{1,0:T(8,128)S(1)} %get-tuple-element.53.refs_3_), custom_call_target="tpu_custom_call" | custom-call | flops 10000000000 | bytes 1 | tf_op jit(solution)/shard_map/local/pallas_call | solution.py:74
  26.1 1.5 %collective-permute-start.7 = (f32[256,128]{1,0:T(8,128)S(1)}, f32[256,128]{1,0:T(8,128)S(1)}, u32[]{:S(2)}, u32[]{:S(2)}) collective-permute-start(f32[256,128]{1,0:T(8,128)S(1)} %get-tuple-element.56.refs_2_.refs_0_), channel_id=1, source_target_pairs={{0,8},{1,9},{2,10},{3,11},{4,12},{5,13},{6,14},{7,15},{8,0},{9,1},... | collective-permute-start | bytes 393224 | tf_op jit(solution)/shard_map/ppermute | solution.py:276
  27.6 3.1 %collective-permute-done.4.refs_1_ = f32[256,128]{1,0:T(8,128)S(1)} collective-permute-done((f32[256,128]{1,0:T(8,128)S(1)}, f32[256,128]{1,0:T(8,128)S(1)}, u32[]{:S(2)}, u32[]{:S(2)}) %collective-permute-start.4) | collective-permute-done | bytes 131104 | tf_op jit(solution)/shard_map/ppermute | solution.py:276
  30.7 1.7 %collective-permute-start.6 = (f32[256,128]{1,0:T(8,128)S(1)}, f32[256,128]{1,0:T(8,128)S(1)}, u32[]{:S(2)}, u32[]{:S(2)}) collective-permute-start(f32[256,128]{1,0:T(8,128)S(1)} %get-tuple-element.57.refs_2_.refs_0_), channel_id=1, source_target_pairs={{0,16},{1,17},{2,18},{3,19},{4,20},{5,21},{6,22},{7,23},{8,24},{9,... | collective-permute-start | bytes 393224 | tf_op jit(solution)/shard_map/ppermute | solution.py:276
  32.3 0.5 collective-permute-start.9
  32.9 4.2 %collective-permute-done.6.refs_1_ = f32[256,128]{1,0:T(8,128)S(1)} collective-permute-done((f32[256,128]{1,0:T(8,128)S(1)}, f32[256,128]{1,0:T(8,128)S(1)}, u32[]{:S(2)}, u32[]{:S(2)}) %collective-permute-start.6) | collective-permute-done | bytes 131104 | tf_op jit(solution)/shard_map/ppermute | solution.py:276
  37.1 1.6 %collective-permute-start.8 = (f32[256,128]{1,0:T(8,128)S(1)}, f32[256,128]{1,0:T(8,128)S(1)}, u32[]{:S(2)}, u32[]{:S(2)}) collective-permute-start(f32[256,128]{1,0:T(8,128)S(1)} %get-tuple-element.59.refs_3_), channel_id=1, source_target_pairs={{0,8},{1,9},{2,10},{3,11},{4,12},{5,13},{6,14},{7,15},{8,0},{9,1},... | collective-permute-start | bytes 393224 | tf_op jit(solution)/shard_map/ppermute | solution.py:276
  38.7 0.2 collective-permute-done.9.refs_0_
  39.0 0.1 collective-permute-start.11
  39.1 3.1 %collective-permute-done.8.refs_0_ = f32[256,128]{1,0:T(8,128)S(1)} collective-permute-done((f32[256,128]{1,0:T(8,128)S(1)}, f32[256,128]{1,0:T(8,128)S(1)}, u32[]{:S(2)}, u32[]{:S(2)}) %collective-permute-start.8) | collective-permute-done | bytes 131104 | tf_op jit(solution)/shard_map/ppermute | solution.py:276
  42.2 0.1 collective-permute-start.10
  42.3 3.2 %local.7 = (f32[384,1024]{1,0:T(8,128)S(1)}, bf16[384,1024]{1,0:T(8,128)(2,1)S(1)}) custom-call(bf16[384,4096]{1,0:T(8,128)(2,1)} %refs_0_.15, bf16[384,4096]{1,0:T(8,128)(2,1)} %refs_1_.15, bf16[384,4096]{1,0:T(8,128)(2,1)} %refs_2_.7, f32[256,128]{1,0:T(8,128)S(1)} %get-tuple-element.65.refs_3_), custom_call_target="tpu_custom_call" | custom-call | flops 10000000000 | bytes 1 | tf_op jit(solution)/shard_map/local/pallas_call | solution.py:74
  45.6 4.6 %collective-permute-done.11.refs_1_ = f32[256,128]{1,0:T(8,128)S(1)} collective-permute-done((f32[256,128]{1,0:T(8,128)S(1)}, f32[256,128]{1,0:T(8,128)S(1)}, u32[]{:S(2)}, u32[]{:S(2)}) %collective-permute-start.11) | collective-permute-done | bytes 131104 | tf_op jit(solution)/shard_map/ppermute | solution.py:276
  50.2 0.1 down.4
  50.2 0.1 collective-permute-start.13
  50.3 1.7 %collective-permute-done.10.refs_1_ = f32[256,128]{1,0:T(8,128)S(1)} collective-permute-done((f32[256,128]{1,0:T(8,128)S(1)}, f32[256,128]{1,0:T(8,128)S(1)}, u32[]{:S(2)}, u32[]{:S(2)}) %collective-permute-start.10) | collective-permute-done | bytes 131104 | tf_op jit(solution)/shard_map/ppermute | solution.py:276
  52.0 0.1 down.5
  52.1 0.4 collective-permute-start.12
  52.5 7.1 %collective-permute-done.13.refs_1_ = f32[512,128]{1,0:T(8,128)S(1)} collective-permute-done((f32[512,128]{1,0:T(8,128)S(1)}, f32[512,128]{1,0:T(8,128)S(1)}, u32[]{:S(2)}, u32[]{:S(2)}) %collective-permute-start.13) | collective-permute-done | bytes 262176 | tf_op jit(solution)/shard_map/ppermute | solution.py:276
  59.5 0.2 down.6
  59.7 0.1 collective-permute-start.14
  59.8 1.4 %finish.4.refs_4_ = bf16[384,4096]{1,0:T(8,128)(2,1)} custom-call(bf16[384,1024]{1,0:T(8,128)(2,1)S(1)} %get-tuple-element.80.refs_0_, f32[384,1024]{1,0:T(8,128)S(1)} %get-tuple-element.49.refs_2_.refs_1_, f32[1024,128]{1,0:T(8,128)S(1)} %get-tuple-element.81.refs_2_, f32[1,4096]{1,0:T(1,128)S(1)} %gain.1.refs_3_, f32[1024,128]{1,0:T(8,128)S(1)} %get-tuple-element.79.refs_4_), custom_call_target="tpu_custom_call" | custom-call | flops 10000000000 | bytes 1 | tf_op jit(solution)/shard_map/finish/pallas_call | solution.py:74
  61.2 0.5 collective-permute-done.14.refs_2_
  61.7 1.4 %finish.5.refs_3_.refs_4_ = bf16[384,4096]{1,0:T(8,128)(2,1)} custom-call(bf16[384,1024]{1,0:T(8,128)(2,1)S(1)} %get-tuple-element.76.refs_0_, f32[384,1024]{1,0:T(8,128)S(1)} %get-tuple-element.51.refs_2_.refs_1_, f32[1024,128]{1,0:T(8,128)S(1)} %collective-permute-done.14.refs_2_, f32[1,4096]{1,0:T(1,128)S(1)} %gain.1.refs_3_, ...), custom_call_target="tpu_custom_call", output_to_operand_aliasing={{}: (4, {})} | custom-call | flops 10000000000 | bytes 1 | tf_op jit(solution)/shard_map/finish/pallas_call | solution.py:74
  63.1 0.0 collective-permute-done.12.refs_1_
  63.1 0.2 down.7
  63.3 0.2 collective-permute-start.15
  63.5 1.4 %finish.6.refs_4_ = bf16[384,4096]{1,0:T(8,128)(2,1)} custom-call(bf16[384,1024]{1,0:T(8,128)(2,1)S(1)} %get-tuple-element.83.refs_0_, f32[384,1024]{1,0:T(8,128)S(1)} %get-tuple-element.55.refs_2_.refs_1_, f32[1024,128]{1,0:T(8,128)S(1)} %get-tuple-element.84.refs_2_, f32[1,4096]{1,0:T(1,128)S(1)} %gain.1.refs_3_, ...), custom_call_target="tpu_custom_call", output_to_operand_aliasing={{}: (4, {})} | custom-call | flops 10000000000 | bytes 1 | tf_op jit(solution)/shard_map/finish/pallas_call | solution.py:74
  64.9 0.3 collective-permute-done.15.refs_2_
  65.3 1.4 %finish.7 = bf16[384,4096]{1,0:T(8,128)(2,1)} custom-call(bf16[384,1024]{1,0:T(8,128)(2,1)S(1)} %get-tuple-element.66.refs_0_, f32[384,1024]{1,0:T(8,128)S(1)} %get-tuple-element.67.refs_1_, f32[1024,128]{1,0:T(8,128)S(1)} %collective-permute-done.15.refs_2_, f32[1,4096]{1,0:T(1,128)S(1)} %gain.1.refs_3_, ...), custom_call_target="tpu_custom_call", output_to_operand_aliasing={{}: (4, {})} | custom-call | flops 10000000000 | bytes 1 | tf_op jit(solution)/shard_map/finish/pallas_call | solution.py:74
  (13 shorter events, 0.2 us)
Async XLA Ops:
  1.8 2.3 %collective-permute-start = (f32[1024,128]{1,0:T(8,128)S(1)}, f32[1024,128]{1,0:T(8,128)S(1)}, u32[]{:S(2)}, u32[]{:S(2)}) collective-permute-start(f32[1024,128]{1,0:T(8,128)S(1)} %states.4.refs_2_), channel_id=1, source_target_pairs={{0,1},{1,0},{2,3},{3,2},{4,5},{5,4},{6,7},{7,6},{8,9},{9,8},{10,11... | collective-permute-start | bytes 1572872 | tf_op jit(solution)/shard_map/ppermute | solution.py:276
  4.2 10.2 %collective-permute-start.3 = (f32[512,128]{1,0:T(8,128)S(1)}, f32[512,128]{1,0:T(8,128)S(1)}, u32[]{:S(2)}, u32[]{:S(2)}) collective-permute-start(f32[512,128]{1,0:T(8,128)S(1)} %get-tuple-element.45.refs_2_), channel_id=1, source_target_pairs={{0,2},{1,3},{2,0},{3,1},{4,6},{5,7},{6,4},{7,5},{8,10},{9,11},{10,... | collective-permute-start | bytes 786440 | tf_op jit(solution)/shard_map/ppermute | solution.py:276
  8.8 2.0 %collective-permute-start.1 = (f32[1024,128]{1,0:T(8,128)S(1)}, f32[1024,128]{1,0:T(8,128)S(1)}, u32[]{:S(2)}, u32[]{:S(2)}) collective-permute-start(f32[1024,128]{1,0:T(8,128)S(1)} %states.6.refs_2_), channel_id=1, source_target_pairs={{0,1},{1,0},{2,3},{3,2},{4,5},{5,4},{6,7},{7,6},{8,9},{9,8},{10,11... | collective-permute-start | bytes 1572872 | tf_op jit(solution)/shard_map/ppermute | solution.py:276
  10.8 11.5 %collective-permute-start.2 = (f32[512,128]{1,0:T(8,128)S(1)}, f32[512,128]{1,0:T(8,128)S(1)}, u32[]{:S(2)}, u32[]{:S(2)}) collective-permute-start(f32[512,128]{1,0:T(8,128)S(1)} %get-tuple-element.47.refs_3_), channel_id=1, source_target_pairs={{0,2},{1,3},{2,0},{3,1},{4,6},{5,7},{6,4},{7,5},{8,10},{9,11},{10,... | collective-permute-start | bytes 786440 | tf_op jit(solution)/shard_map/ppermute | solution.py:276
  14.5 11.5 %collective-permute-start.5 = (f32[256,128]{1,0:T(8,128)S(1)}, f32[256,128]{1,0:T(8,128)S(1)}, u32[]{:S(2)}, u32[]{:S(2)}) collective-permute-start(f32[256,128]{1,0:T(8,128)S(1)} %get-tuple-element.50.refs_3_), channel_id=1, source_target_pairs={{0,4},{1,5},{2,6},{3,7},{4,0},{5,1},{6,2},{7,3},{8,12},{9,13},{10,... | collective-permute-start | bytes 393224 | tf_op jit(solution)/shard_map/ppermute | solution.py:276
  22.4 8.2 %collective-permute-start.4 = (f32[256,128]{1,0:T(8,128)S(1)}, f32[256,128]{1,0:T(8,128)S(1)}, u32[]{:S(2)}, u32[]{:S(2)}) collective-permute-start(f32[256,128]{1,0:T(8,128)S(1)} %get-tuple-element.53.refs_3_), channel_id=1, source_target_pairs={{0,4},{1,5},{2,6},{3,7},{4,0},{5,1},{6,2},{7,3},{8,12},{9,13},{10,... | collective-permute-start | bytes 393224 | tf_op jit(solution)/shard_map/ppermute | solution.py:276
  26.1 6.3 %collective-permute-start.7 = (f32[256,128]{1,0:T(8,128)S(1)}, f32[256,128]{1,0:T(8,128)S(1)}, u32[]{:S(2)}, u32[]{:S(2)}) collective-permute-start(f32[256,128]{1,0:T(8,128)S(1)} %get-tuple-element.56.refs_2_.refs_0_), channel_id=1, source_target_pairs={{0,8},{1,9},{2,10},{3,11},{4,12},{5,13},{6,14},{7,15},{8,0},{9,1},... | collective-permute-start | bytes 393224 | tf_op jit(solution)/shard_map/ppermute | solution.py:276
  30.7 6.4 %collective-permute-start.6 = (f32[256,128]{1,0:T(8,128)S(1)}, f32[256,128]{1,0:T(8,128)S(1)}, u32[]{:S(2)}, u32[]{:S(2)}) collective-permute-start(f32[256,128]{1,0:T(8,128)S(1)} %get-tuple-element.57.refs_2_.refs_0_), channel_id=1, source_target_pairs={{0,16},{1,17},{2,18},{3,19},{4,20},{5,21},{6,22},{7,23},{8,24},{9,... | collective-permute-start | bytes 393224 | tf_op jit(solution)/shard_map/ppermute | solution.py:276
  32.3 6.6 %collective-permute-start.9 = (f32[256,128]{1,0:T(8,128)S(1)}, f32[256,128]{1,0:T(8,128)S(1)}, u32[]{:S(2)}, u32[]{:S(2)}) collective-permute-start(f32[256,128]{1,0:T(8,128)S(1)} %get-tuple-element.58.refs_2_), channel_id=1, source_target_pairs={{0,16},{1,17},{2,18},{3,19},{4,20},{5,21},{6,22},{7,23},{8,24},{9,... | collective-permute-start | bytes 393224 | tf_op jit(solution)/shard_map/ppermute | solution.py:276
  37.1 5.0 %collective-permute-start.8 = (f32[256,128]{1,0:T(8,128)S(1)}, f32[256,128]{1,0:T(8,128)S(1)}, u32[]{:S(2)}, u32[]{:S(2)}) collective-permute-start(f32[256,128]{1,0:T(8,128)S(1)} %get-tuple-element.59.refs_3_), channel_id=1, source_target_pairs={{0,8},{1,9},{2,10},{3,11},{4,12},{5,13},{6,14},{7,15},{8,0},{9,1},... | collective-permute-start | bytes 393224 | tf_op jit(solution)/shard_map/ppermute | solution.py:276
  39.0 11.2 %collective-permute-start.11 = (f32[256,128]{1,0:T(8,128)S(1)}, f32[256,128]{1,0:T(8,128)S(1)}, u32[]{:S(2)}, u32[]{:S(2)}) collective-permute-start(f32[256,128]{1,0:T(8,128)S(1)} %get-tuple-element.64.refs_3_), channel_id=1, source_target_pairs={{0,4},{1,5},{2,6},{3,7},{4,0},{5,1},{6,2},{7,3},{8,12},{9,13},{10,... | collective-permute-start | bytes 393224 | tf_op jit(solution)/shard_map/ppermute | solution.py:276
  42.2 3.3 %copy-start = (f32[4096]{0:T(1024)S(1)}, f32[4096]{0:T(1024)}, u32[]{:S(2)}) copy-start(f32[4096]{0:T(1024)} %param.7) | copy-start | bytes 49156
  42.2 9.8 %collective-permute-start.10 = (f32[256,128]{1,0:T(8,128)S(1)}, f32[256,128]{1,0:T(8,128)S(1)}, u32[]{:S(2)}, u32[]{:S(2)}) collective-permute-start(f32[256,128]{1,0:T(8,128)S(1)} %get-tuple-element.65.refs_3_), channel_id=1, source_target_pairs={{0,4},{1,5},{2,6},{3,7},{4,0},{5,1},{6,2},{7,3},{8,12},{9,13},{10,... | collective-permute-start | bytes 393224 | tf_op jit(solution)/shard_map/ppermute | solution.py:276
  50.2 9.3 %collective-permute-start.13 = (f32[512,128]{1,0:T(8,128)S(1)}, f32[512,128]{1,0:T(8,128)S(1)}, u32[]{:S(2)}, u32[]{:S(2)}) collective-permute-start(f32[512,128]{1,0:T(8,128)S(1)} %get-tuple-element.72.refs_3_), channel_id=1, source_target_pairs={{0,2},{1,3},{2,0},{3,1},{4,6},{5,7},{6,4},{7,5},{8,10},{9,11},{10,... | collective-permute-start | bytes 786440 | tf_op jit(solution)/shard_map/ppermute | solution.py:276
  52.1 11.1 %collective-permute-start.12 = (f32[512,128]{1,0:T(8,128)S(1)}, f32[512,128]{1,0:T(8,128)S(1)}, u32[]{:S(2)}, u32[]{:S(2)}) collective-permute-start(f32[512,128]{1,0:T(8,128)S(1)} %get-tuple-element.74.refs_3_), channel_id=1, source_target_pairs={{0,2},{1,3},{2,0},{3,1},{4,6},{5,7},{6,4},{7,5},{8,10},{9,11},{10,... | collective-permute-start | bytes 786440 | tf_op jit(solution)/shard_map/ppermute | solution.py:276
  59.7 2.0 %collective-permute-start.14 = (f32[1024,128]{1,0:T(8,128)S(1)}, f32[1024,128]{1,0:T(8,128)S(1)}, u32[]{:S(2)}, u32[]{:S(2)}) collective-permute-start(f32[1024,128]{1,0:T(8,128)S(1)} %get-tuple-element.79.refs_4_), channel_id=1, source_target_pairs={{0,1},{1,0},{2,3},{3,2},{4,5},{5,4},{6,7},{7,6},{8,9},{9,8},{10,11... | collective-permute-start | bytes 1572872 | tf_op jit(solution)/shard_map/ppermute | solution.py:276
  63.3 2.0 %collective-permute-start.15 = (f32[1024,128]{1,0:T(8,128)S(1)}, f32[1024,128]{1,0:T(8,128)S(1)}, u32[]{:S(2)}, u32[]{:S(2)}) collective-permute-start(f32[1024,128]{1,0:T(8,128)S(1)} %get-tuple-element.82.refs_5_), channel_id=1, source_target_pairs={{0,1},{1,0},{2,3},{3,2},{4,5},{5,4},{6,7},{7,6},{8,9},{9,8},{10,11... | collective-permute-start | bytes 1572872 | tf_op jit(solution)/shard_map/ppermute | solution.py:276

commit v5 on v4

--- a/solution.py
+++ b/solution.py
@@ -14,6 +14,7 @@
 CHUNKS = 2
 HEADS = HALF // CHUNKS
 PIECE = 4
+HINT = 7 * 10**9
 WIDTH = PIECE * E
 
 
@@ -65,7 +66,7 @@
             )
 
 
-def call(kernel, name, arrays, shapes, scratch=(), tie=(), alias=None, mebibytes=4, flops=10**10):
+def call(kernel, name, arrays, shapes, scratch=(), tie=(), alias=None, mebibytes=4):
     count, operands = len(arrays), list(arrays) + list(tie)
 
     def body(*refs):
@@ -79,7 +80,7 @@
         scratch_shapes=scratch,
         input_output_aliases={} if alias is None else {alias: 0},
         compiler_params=limit(mebibytes),
-        cost_estimate=pl.CostEstimate(flops=flops, bytes_accessed=1, transcendentals=0),
+        cost_estimate=pl.CostEstimate(flops=HINT, bytes_accessed=1, transcendentals=0),
         name=name,
     )(*[pltpu.with_memory_space_constraint(x, space) for x, space in operands])
 
@@ -120,6 +121,48 @@
     lower = bit_of(level + 1) == 0
     outs[0][...] = jnp.where(lower, one, two)
     outs[1][...] = jnp.where(lower, two, one)
+
+
+def pick(lower, one, two):
+    return jnp.where(lower, one, two), jnp.where(lower, two, one)
+
+
+def first_kernel(keep_ref, got_ref, low_ref, *outs):
+    keep, got = keep_ref[...], got_ref[...]
+    low_ref[...] = jnp.where(bit_of(0) == 0, keep, got)
+    total = keep + got
+    rows = total.shape[0] // 2
+    mine, other = pick(bit_of(1) == 0, total[:rows], total[rows:])
+    for n, half in enumerate((other, mine)):
+        stays, goes_on = pick(bit_of(2) == 0, half[: rows // 2], half[rows // 2 :])
+        outs[2 * n][...] = goes_on
+        outs[2 * n + 1][...] = stays
+
+
+def first_up(keep, got, tie):
+    rows = keep.shape[0]
+    shapes = [(rows, E)] + [(rows // 4, E)] * 4
+    return vmem_call(first_kernel, "first_up", shapes, tie, keep, got)
+
+
+def part_kernel(before_ref, low_ref, own_ref, send_ref):
+    split(1, before_ref[...], low_ref[...], own_ref, send_ref)
+
+
+def part_down(before, low, tie):
+    return vmem_call(part_kernel, "part", [low.shape] * 2, tie, before, low)
+
+
+def last_kernel(own_ref, own_on_ref, got_ref, got_on_ref, low_ref, next_ref, send_ref):
+    lower = bit_of(2) == 0
+    mine = jnp.concatenate(pick(lower, own_ref[...], own_on_ref[...]), axis=0)
+    other = jnp.concatenate(pick(lower, got_ref[...], got_on_ref[...]), axis=0)
+    before = jnp.concatenate(pick(bit_of(1) == 0, mine, other), axis=0)
+    split(0, before, low_ref[...], next_ref, send_ref)
+
+
+def last_down(own, got, low, tie):
+    return vmem_call(last_kernel, "last_down", [low.shape] * 2, tie, *own, *got, low)
 
 
 def copy_kernel(x_ref, out_ref):
@@ -300,35 +343,52 @@
 
     keep, got, before = [None] * CHUNKS, [None] * CHUNKS, [None] * CHUNKS
     low = [[None] * levels for _ in chunks]
+    part_keep, part_got, part_low = ([[None, None] for _ in chunks] for _ in range(3))
     for c in chunks:
         got[c] = swap(after(states_of(c, False, keys, values, latest)), 0)
         keep[c] = after(states_of(c, True, keys, values, latest))
-        up(0, c)
+        low[c][0], send_on, send, part_keep[c][1], part_keep[c][0] = first_up(keep[c], got[c], latest)
+        part_got[c][1] = swap(after(send_on), 1)
+        part_got[c][0] = swap(send, 1)
     some_local()
-    for level in range(1, levels):
+    for c in chunks:
+        part_low[c][1], send = go_up(1, False, part_keep[c][1], part_got[c][1], latest)
+        got[c] = swap(after(send), 2)
+        part_low[c][0], keep[c] = go_up(1, False, part_keep[c][0], part_got[c][0], latest)
+        after(keep[c])
+        some_local()
+    for level in range(2, levels):
         for c in chunks:
             up(level, c)
-            if level == 1:
-                some_local()
     for c in chunks:
         bit, other = order[c % 2]
         before[c], send = go_along(bit, other, c % 2 == 1, keep[c], got[c], latest)
         got[c] = swap(after(send), other)
     top = levels - 1
+    def part(c, n, before):
+        part_keep[c][n], send = part_down(before, part_low[c][n], latest)
+        part_got[c][n] = swap(after(send), 1)
+
     for c in chunks:
         turned = c % 2 == 1
         keep[c], send = turn_down(order[0][1], turned, top, got[c], low[c][top], before[c], latest)
         got[c] = swap(after(send), top)
+        if top == 2:
+            part(c, 0, keep[c])
     while todo:
         some_local()
     gain = after(vmem_call(copy_kernel, "gain", [gain.shape], latest, gain)[0])
-    for level in range(top - 1, 0, -1):
+    for level in range(top - 1, 1, -1):
         for c in chunks:
             keep[c], send = go_down(level, keep[c], got[c], low[c][level], latest)
             got[c] = swap(after(send), level)
+            if level == 2:
+                part(c, 0, keep[c])
+    for c in chunks:
+        part(c, 1, got[c])
     out = None
     for c in chunks:
-        keep[c], send = go_down(0, keep[c], got[c], low[c][0], latest)
+        keep[c], send = last_down(part_keep[c], part_got[c], low[c][0], latest)
         got[c] = swap(after(send), 0)
         for mine, prefix in ((True, keep[c]), (False, got[c])):
             out = finish(c, mine, queries.shape, *mixed[c, mine], prefix, gain, out, latest)

time: 67 us -> 65.2 us (0.973)
  waiting for transfers between devices: 26.6 us -> 14 us
  starting transfers between devices: 13.2 us -> 23.8 us
    ppermute x16 -> x20, waiting for transfers between devices: 26.6 us -> 14 us  [swap(): return lax.ppermute(x, AXES, [(i, i ^ 1 << level) for i in range(devices)])]
    ppermute x16 -> x20, starting transfers between devices: 13.2 us -> 23.8 us  [swap(): return lax.ppermute(x, AXES, [(i, i ^ 1 << level) for i in range(devices)])]
    pallas_call x27 -> x31, Pallas kernels: 26.7 us -> 26.8 us  [call(): pl.pallas_call(body, in_specs=[pl.BlockSpec(memory_space=space) for _, sp...]
  transfers between devices with their start and end apart: 16 -> 20, of which waited for: 10 -> 6; matrix products, arithmetic and copies ran while one was open for 0% -> 0% of each run, Pallas kernels for 35% -> 36%
where the time goes in v5:
time: 65.2 us; the launch traced here: 64.9 us
  Pallas kernels  26.8 us (41%)
  starting transfers between devices  23.8 us (37%)
  waiting for transfers between devices  14 us (21%)
    pallas_call x31, Pallas kernels, call(): pl.pallas_call(body, in_specs=[pl.BlockSpec(memory_space=space) for _, sp...  26.8 us
    ppermute x20, starting transfers between devices, swap(): return lax.ppermute(x, AXES, [(i, i ^ 1 << level) for i in range(devices)])  23.8 us
    ppermute x20, waiting for transfers between devices, swap(): return lax.ppermute(x, AXES, [(i, i ^ 1 << level) for i in range(devices)])  14 us
  transfers between devices with their start and end apart: 20, of which 6 were waited for; matrix products, arithmetic and copies ran while one was open for 0% of the time, Pallas kernels for 36%

profile of v5, /device:TPU:0, one launch (start us, length us, event | category | flops | bytes accessed | tf_op | source)
XLA Modules:
  0.0 64.9 jit_solution(6685530208426897867)
XLA Ops:
  0.0 1.8 %states.4.refs_2_ = f32[1024,128]{1,0:T(8,128)S(1)} custom-call(bf16[384,4096]{1,0:T(8,128)(2,1)} %refs_1_.15, bf16[384,4096]{1,0:T(8,128)(2,1)} %refs_2_.7), custom_call_target="tpu_custom_call" | custom-call | flops 7000000000 | bytes 1 | tf_op jit(solution)/shard_map/states/pallas_call | solution.py:75
  1.8 0.5 collective-permute-start
  2.3 1.8 %states.5.refs_0_.refs_2_ = f32[1024,128]{1,0:T(8,128)S(1)} custom-call(bf16[384,4096]{1,0:T(8,128)(2,1)} %refs_1_.15, bf16[384,4096]{1,0:T(8,128)(2,1)} %refs_2_.7, f32[1024,128]{1,0:T(8,128)S(1)} %states.4.refs_2_), custom_call_target="tpu_custom_call" | custom-call | flops 7000000000 | bytes 1 | tf_op jit(solution)/shard_map/states/pallas_call | solution.py:75
  4.1 0.1 first_up.2
  4.2 2.7 %collective-permute-start.5 = (f32[256,128]{1,0:T(8,128)S(1)}, f32[256,128]{1,0:T(8,128)S(1)}, u32[]{:S(2)}, u32[]{:S(2)}) collective-permute-start(f32[256,128]{1,0:T(8,128)S(1)} %get-tuple-element.55.refs_2_), channel_id=1, source_target_pairs={{0,2},{1,3},{2,0},{3,1},{4,6},{5,7},{6,4},{7,5},{8,10},{9,11},{10,... | collective-permute-start | bytes 393224 | tf_op jit(solution)/shard_map/ppermute | solution.py:319
  7.0 1.8 %states.6.refs_2_ = f32[1024,128]{1,0:T(8,128)S(1)} custom-call(bf16[384,4096]{1,0:T(8,128)(2,1)} %refs_1_.15, bf16[384,4096]{1,0:T(8,128)(2,1)} %refs_2_.7, f32[256,128]{1,0:T(8,128)S(1)} %get-tuple-element.55.refs_2_), custom_call_target="tpu_custom_call" | custom-call | flops 7000000000 | bytes 1 | tf_op jit(solution)/shard_map/states/pallas_call | solution.py:75
  8.8 0.1 collective-permute-start.4
  8.8 0.2 collective-permute-start.1
  9.0 1.8 %states.7.refs_0_.refs_2_ = f32[1024,128]{1,0:T(8,128)S(1)} custom-call(bf16[384,4096]{1,0:T(8,128)(2,1)} %refs_1_.15, bf16[384,4096]{1,0:T(8,128)(2,1)} %refs_2_.7, f32[1024,128]{1,0:T(8,128)S(1)} %states.6.refs_2_), custom_call_target="tpu_custom_call" | custom-call | flops 7000000000 | bytes 1 | tf_op jit(solution)/shard_map/states/pallas_call | solution.py:75
  10.8 0.0 collective-permute-done.1.refs_1_
  10.8 0.1 first_up.3
  11.0 2.0 %collective-permute-start.2 = (f32[256,128]{1,0:T(8,128)S(1)}, f32[256,128]{1,0:T(8,128)S(1)}, u32[]{:S(2)}, u32[]{:S(2)}) collective-permute-start(f32[256,128]{1,0:T(8,128)S(1)} %get-tuple-element.57), channel_id=1, source_target_pairs={{0,2},{1,3},{2,0},{3,1},{4,6},{5,7},{6,4},{7,5},{8,10},{9,11},{10,... | collective-permute-start | bytes 393224 | tf_op jit(solution)/shard_map/ppermute | solution.py:319
  13.0 0.1 collective-permute-start.3
  13.1 3.2 %local.4 = (f32[384,1024]{1,0:T(8,128)S(1)}, bf16[384,1024]{1,0:T(8,128)(2,1)S(1)}) custom-call(bf16[384,4096]{1,0:T(8,128)(2,1)} %refs_0_.15, bf16[384,4096]{1,0:T(8,128)(2,1)} %refs_1_.15, bf16[384,4096]{1,0:T(8,128)(2,1)} %refs_2_.7, f32[256,128]{1,0:T(8,128)S(1)} %get-tuple-element.59.refs_3_), custom_call_target="tpu_custom_call" | custom-call | flops 7000000000 | bytes 1 | tf_op jit(solution)/shard_map/local/pallas_call | solution.py:75
  16.3 0.0 collective-permute-done.5.refs_1_
  16.4 3.0 %collective-permute-start.7 = (f32[256,128]{1,0:T(8,128)S(1)}, f32[256,128]{1,0:T(8,128)S(1)}, u32[]{:S(2)}, u32[]{:S(2)}) collective-permute-start(f32[256,128]{1,0:T(8,128)S(1)} %get-tuple-element.64.refs_2_), channel_id=1, source_target_pairs={{0,4},{1,5},{2,6},{3,7},{4,0},{5,1},{6,2},{7,3},{8,12},{9,13},{10,... | collective-permute-start | bytes 393224 | tf_op jit(solution)/shard_map/ppermute | solution.py:319
  19.4 0.0 collective-permute-done.4.refs_1_
  19.4 3.2 %local.5 = (f32[384,1024]{1,0:T(8,128)S(1)}, bf16[384,1024]{1,0:T(8,128)(2,1)S(1)}) custom-call(bf16[384,4096]{1,0:T(8,128)(2,1)} %refs_0_.15, bf16[384,4096]{1,0:T(8,128)(2,1)} %refs_1_.15, bf16[384,4096]{1,0:T(8,128)(2,1)} %refs_2_.7, f32[256,128]{1,0:T(8,128)S(1)} %get-tuple-element.65.refs_3_.refs_0_), custom_call_target="tpu_custom_call" | custom-call | flops 7000000000 | bytes 1 | tf_op jit(solution)/shard_map/local/pallas_call | solution.py:75
  22.6 0.0 collective-permute-done.3.refs_1_
  22.7 0.5 collective-permute-start.6
  23.2 0.0 collective-permute-done.2.refs_1_
  23.2 3.2 %local.6 = (f32[384,1024]{1,0:T(8,128)S(1)}, bf16[384,1024]{1,0:T(8,128)(2,1)S(1)}) custom-call(bf16[384,4096]{1,0:T(8,128)(2,1)} %refs_0_.15, bf16[384,4096]{1,0:T(8,128)(2,1)} %refs_1_.15, bf16[384,4096]{1,0:T(8,128)(2,1)} %refs_2_.7, f32[256,128]{1,0:T(8,128)S(1)} %get-tuple-element.68.refs_3_.refs_0_), custom_call_target="tpu_custom_call" | custom-call | flops 7000000000 | bytes 1 | tf_op jit(solution)/shard_map/local/pallas_call | solution.py:75
  26.5 1.6 %collective-permute-start.9 = (f32[256,128]{1,0:T(8,128)S(1)}, f32[256,128]{1,0:T(8,128)S(1)}, u32[]{:S(2)}, u32[]{:S(2)}) collective-permute-start(f32[256,128]{1,0:T(8,128)S(1)} %get-tuple-element.70.refs_2_.refs_0_), channel_id=1, source_target_pairs={{0,8},{1,9},{2,10},{3,11},{4,12},{5,13},{6,14},{7,15},{8,0},{9,1},... | collective-permute-start | bytes 393224 | tf_op jit(solution)/shard_map/ppermute | solution.py:319
  28.1 3.4 %collective-permute-done.6.refs_1_ = f32[256,128]{1,0:T(8,128)S(1)} collective-permute-done((f32[256,128]{1,0:T(8,128)S(1)}, f32[256,128]{1,0:T(8,128)S(1)}, u32[]{:S(2)}, u32[]{:S(2)}) %collective-permute-start.6) | collective-permute-done | bytes 131104 | tf_op jit(solution)/shard_map/ppermute | solution.py:319
  31.5 1.6 %collective-permute-start.8 = (f32[256,128]{1,0:T(8,128)S(1)}, f32[256,128]{1,0:T(8,128)S(1)}, u32[]{:S(2)}, u32[]{:S(2)}) collective-permute-start(f32[256,128]{1,0:T(8,128)S(1)} %get-tuple-element.71.refs_2_.refs_0_), channel_id=1, source_target_pairs={{0,16},{1,17},{2,18},{3,19},{4,20},{5,21},{6,22},{7,23},{8,24},{9,... | collective-permute-start | bytes 393224 | tf_op jit(solution)/shard_map/ppermute | solution.py:319
  33.1 0.6 collective-permute-start.11
  33.7 3.6 %collective-permute-done.8.refs_1_ = f32[256,128]{1,0:T(8,128)S(1)} collective-permute-done((f32[256,128]{1,0:T(8,128)S(1)}, f32[256,128]{1,0:T(8,128)S(1)}, u32[]{:S(2)}, u32[]{:S(2)}) %collective-permute-start.8) | collective-permute-done | bytes 131104 | tf_op jit(solution)/shard_map/ppermute | solution.py:319
  37.3 1.6 %collective-permute-start.10 = (f32[256,128]{1,0:T(8,128)S(1)}, f32[256,128]{1,0:T(8,128)S(1)}, u32[]{:S(2)}, u32[]{:S(2)}) collective-permute-start(f32[256,128]{1,0:T(8,128)S(1)} %get-tuple-element.73.refs_3_), channel_id=1, source_target_pairs={{0,8},{1,9},{2,10},{3,11},{4,12},{5,13},{6,14},{7,15},{8,0},{9,1},... | collective-permute-start | bytes 393224 | tf_op jit(solution)/shard_map/ppermute | solution.py:319
  38.9 0.3 collective-permute-start.13
  39.2 4.7 %collective-permute-start.16 = (f32[256,128]{1,0:T(8,128)S(1)}, f32[256,128]{1,0:T(8,128)S(1)}, u32[]{:S(2)}, u32[]{:S(2)}) collective-permute-start(f32[256,128]{1,0:T(8,128)S(1)} %get-tuple-element.81.refs_3_), channel_id=1, source_target_pairs={{0,2},{1,3},{2,0},{3,1},{4,6},{5,7},{6,4},{7,5},{8,10},{9,11},{10,... | collective-permute-start | bytes 393224 | tf_op jit(solution)/shard_map/ppermute | solution.py:319
  44.0 0.1 collective-permute-start.12
  44.1 0.0 copy-start
  44.1 3.0 %collective-permute-start.14 = (f32[256,128]{1,0:T(8,128)S(1)}, f32[256,128]{1,0:T(8,128)S(1)}, u32[]{:S(2)}, u32[]{:S(2)}) collective-permute-start(f32[256,128]{1,0:T(8,128)S(1)} %get-tuple-element.85.refs_3_), channel_id=1, source_target_pairs={{0,2},{1,3},{2,0},{3,1},{4,6},{5,7},{6,4},{7,5},{8,10},{9,11},{10,... | collective-permute-start | bytes 393224 | tf_op jit(solution)/shard_map/ppermute | solution.py:319
  47.1 3.2 %local.7 = (f32[384,1024]{1,0:T(8,128)S(1)}, bf16[384,1024]{1,0:T(8,128)(2,1)S(1)}) custom-call(bf16[384,4096]{1,0:T(8,128)(2,1)} %refs_0_.15, bf16[384,4096]{1,0:T(8,128)(2,1)} %refs_1_.15, bf16[384,4096]{1,0:T(8,128)(2,1)} %refs_2_.7, f32[256,128]{1,0:T(8,128)S(1)} %get-tuple-element.85.refs_3_), custom_call_target="tpu_custom_call" | custom-call | flops 7000000000 | bytes 1 | tf_op jit(solution)/shard_map/local/pallas_call | solution.py:75
  50.5 0.1 collective-permute-start.17
  50.5 2.4 %collective-permute-done.12.refs_0_ = f32[256,128]{1,0:T(8,128)S(1)} collective-permute-done((f32[256,128]{1,0:T(8,128)S(1)}, f32[256,128]{1,0:T(8,128)S(1)}, u32[]{:S(2)}, u32[]{:S(2)}) %collective-permute-start.12) | collective-permute-done | bytes 131104 | tf_op jit(solution)/shard_map/ppermute | solution.py:319
  53.0 1.0 %collective-permute-start.15 = (f32[256,128]{1,0:T(8,128)S(1)}, f32[256,128]{1,0:T(8,128)S(1)}, u32[]{:S(2)}, u32[]{:S(2)}) collective-permute-start(f32[256,128]{1,0:T(8,128)S(1)} %get-tuple-element.93.refs_5_), channel_id=1, source_target_pairs={{0,2},{1,3},{2,0},{3,1},{4,6},{5,7},{6,4},{7,5},{8,10},{9,11},{10,... | collective-permute-start | bytes 393224 | tf_op jit(solution)/shard_map/ppermute | solution.py:319
  54.0 3.7 %collective-permute-done.17.refs_3_ = f32[256,128]{1,0:T(8,128)S(1)} collective-permute-done((f32[256,128]{1,0:T(8,128)S(1)}, f32[256,128]{1,0:T(8,128)S(1)}, u32[]{:S(2)}, u32[]{:S(2)}) %collective-permute-start.17) | collective-permute-done | bytes 131104 | tf_op jit(solution)/shard_map/ppermute | solution.py:319
  57.7 0.2 last_down.2
  57.9 0.1 collective-permute-start.18
  58.0 1.4 %finish.4.refs_4_ = bf16[384,4096]{1,0:T(8,128)(2,1)} custom-call(bf16[384,1024]{1,0:T(8,128)(2,1)S(1)} %get-tuple-element.100.refs_0_, f32[384,1024]{1,0:T(8,128)S(1)} %get-tuple-element.63.refs_2_.refs_1_, f32[1024,128]{1,0:T(8,128)S(1)} %get-tuple-element.101.refs_2_, f32[1,4096]{1,0:T(1,128)S(1)} %gain.1.refs_2_.refs_3_, ...), custom_call_target="tpu_custom_call" | custom-call | flops 7000000000 | bytes 1 | tf_op jit(solution)/shard_map/finish/pallas_call | solution.py:75
  59.4 0.5 collective-permute-done.18.refs_2_
  59.9 1.4 %finish.5.refs_5_.refs_4_ = bf16[384,4096]{1,0:T(8,128)(2,1)} custom-call(bf16[384,1024]{1,0:T(8,128)(2,1)S(1)} %get-tuple-element.95.refs_0_, f32[384,1024]{1,0:T(8,128)S(1)} %get-tuple-element.66.refs_2_.refs_1_, f32[1024,128]{1,0:T(8,128)S(1)} %collective-permute-done.18.refs_2_, ...), custom_call_target="tpu_custom_call", output_to_operand_aliasing={{}: (4, {})} | custom-call | flops 7000000000 | bytes 1 | tf_op jit(solution)/shard_map/finish/pallas_call | solution.py:75
  61.3 0.2 last_down.3
  61.5 0.2 collective-permute-start.19
  61.7 1.4 %finish.6.refs_4_ = bf16[384,4096]{1,0:T(8,128)(2,1)} custom-call(bf16[384,1024]{1,0:T(8,128)(2,1)S(1)} %get-tuple-element.103.refs_0_, f32[384,1024]{1,0:T(8,128)S(1)} %get-tuple-element.69.refs_2_.refs_1_, f32[1024,128]{1,0:T(8,128)S(1)} %get-tuple-element.104.refs_2_, f32[1,4096]{1,0:T(1,128)S(1)} %gain.1.refs_2_.refs_3_, ...), custom_call_target="tpu_custom_call", output_to_operand_aliasing={{}: (4, {})} | custom-call | flops 7000000000 | bytes 1 | tf_op jit(solution)/shard_map/finish/pallas_call | solution.py:75
  63.1 0.3 collective-permute-done.19.refs_2_
  63.5 1.4 %finish.7 = bf16[384,4096]{1,0:T(8,128)(2,1)} custom-call(bf16[384,1024]{1,0:T(8,128)(2,1)S(1)} %get-tuple-element.86.refs_0_, f32[384,1024]{1,0:T(8,128)S(1)} %get-tuple-element.87.refs_1_, f32[1024,128]{1,0:T(8,128)S(1)} %collective-permute-done.19.refs_2_, f32[1,4096]{1,0:T(1,128)S(1)} %gain.1.refs_2_.refs_3_, ...), custom_call_target="tpu_custom_call", output_to_operand_aliasing={{}: (4, {})} | custom-call | flops 7000000000 | bytes 1 | tf_op jit(solution)/shard_map/finish/pallas_call | solution.py:75
  (25 shorter events, 0.4 us)
Async XLA Ops:
  1.8 2.3 %collective-permute-start = (f32[1024,128]{1,0:T(8,128)S(1)}, f32[1024,128]{1,0:T(8,128)S(1)}, u32[]{:S(2)}, u32[]{:S(2)}) collective-permute-start(f32[1024,128]{1,0:T(8,128)S(1)} %states.4.refs_2_), channel_id=1, source_target_pairs={{0,1},{1,0},{2,3},{3,2},{4,5},{5,4},{6,7},{7,6},{8,9},{9,8},{10,11... | collective-permute-start | bytes 1572872 | tf_op jit(solution)/shard_map/ppermute | solution.py:319
  4.2 12.1 %collective-permute-start.5 = (f32[256,128]{1,0:T(8,128)S(1)}, f32[256,128]{1,0:T(8,128)S(1)}, u32[]{:S(2)}, u32[]{:S(2)}) collective-permute-start(f32[256,128]{1,0:T(8,128)S(1)} %get-tuple-element.55.refs_2_), channel_id=1, source_target_pairs={{0,2},{1,3},{2,0},{3,1},{4,6},{5,7},{6,4},{7,5},{8,10},{9,11},{10,... | collective-permute-start | bytes 393224 | tf_op jit(solution)/shard_map/ppermute | solution.py:319
  8.8 10.6 %collective-permute-start.4 = (f32[256,128]{1,0:T(8,128)S(1)}, f32[256,128]{1,0:T(8,128)S(1)}, u32[]{:S(2)}, u32[]{:S(2)}) collective-permute-start(f32[256,128]{1,0:T(8,128)S(1)} %get-tuple-element.61), channel_id=1, source_target_pairs={{0,2},{1,3},{2,0},{3,1},{4,6},{5,7},{6,4},{7,5},{8,10},{9,11},{10,... | collective-permute-start | bytes 393224 | tf_op jit(solution)/shard_map/ppermute | solution.py:319
  8.8 2.0 %collective-permute-start.1 = (f32[1024,128]{1,0:T(8,128)S(1)}, f32[1024,128]{1,0:T(8,128)S(1)}, u32[]{:S(2)}, u32[]{:S(2)}) collective-permute-start(f32[1024,128]{1,0:T(8,128)S(1)} %states.6.refs_2_), channel_id=1, source_target_pairs={{0,1},{1,0},{2,3},{3,2},{4,5},{5,4},{6,7},{7,6},{8,9},{9,8},{10,11... | collective-permute-start | bytes 1572872 | tf_op jit(solution)/shard_map/ppermute | solution.py:319
  11.0 12.2 %collective-permute-start.2 = (f32[256,128]{1,0:T(8,128)S(1)}, f32[256,128]{1,0:T(8,128)S(1)}, u32[]{:S(2)}, u32[]{:S(2)}) collective-permute-start(f32[256,128]{1,0:T(8,128)S(1)} %get-tuple-element.57), channel_id=1, source_target_pairs={{0,2},{1,3},{2,0},{3,1},{4,6},{5,7},{6,4},{7,5},{8,10},{9,11},{10,... | collective-permute-start | bytes 393224 | tf_op jit(solution)/shard_map/ppermute | solution.py:319
  13.0 9.7 %collective-permute-start.3 = (f32[256,128]{1,0:T(8,128)S(1)}, f32[256,128]{1,0:T(8,128)S(1)}, u32[]{:S(2)}, u32[]{:S(2)}) collective-permute-start(f32[256,128]{1,0:T(8,128)S(1)} %get-tuple-element.59.refs_3_), channel_id=1, source_target_pairs={{0,2},{1,3},{2,0},{3,1},{4,6},{5,7},{6,4},{7,5},{8,10},{9,11},{10,... | collective-permute-start | bytes 393224 | tf_op jit(solution)/shard_map/ppermute | solution.py:319
  16.4 10.1 %collective-permute-start.7 = (f32[256,128]{1,0:T(8,128)S(1)}, f32[256,128]{1,0:T(8,128)S(1)}, u32[]{:S(2)}, u32[]{:S(2)}) collective-permute-start(f32[256,128]{1,0:T(8,128)S(1)} %get-tuple-element.64.refs_2_), channel_id=1, source_target_pairs={{0,4},{1,5},{2,6},{3,7},{4,0},{5,1},{6,2},{7,3},{8,12},{9,13},{10,... | collective-permute-start | bytes 393224 | tf_op jit(solution)/shard_map/ppermute | solution.py:319
  22.7 8.8 %collective-permute-start.6 = (f32[256,128]{1,0:T(8,128)S(1)}, f32[256,128]{1,0:T(8,128)S(1)}, u32[]{:S(2)}, u32[]{:S(2)}) collective-permute-start(f32[256,128]{1,0:T(8,128)S(1)} %get-tuple-element.67.refs_2_), channel_id=1, source_target_pairs={{0,4},{1,5},{2,6},{3,7},{4,0},{5,1},{6,2},{7,3},{8,12},{9,13},{10,... | collective-permute-start | bytes 393224 | tf_op jit(solution)/shard_map/ppermute | solution.py:319
  26.5 6.6 %collective-permute-start.9 = (f32[256,128]{1,0:T(8,128)S(1)}, f32[256,128]{1,0:T(8,128)S(1)}, u32[]{:S(2)}, u32[]{:S(2)}) collective-permute-start(f32[256,128]{1,0:T(8,128)S(1)} %get-tuple-element.70.refs_2_.refs_0_), channel_id=1, source_target_pairs={{0,8},{1,9},{2,10},{3,11},{4,12},{5,13},{6,14},{7,15},{8,0},{9,1},... | collective-permute-start | bytes 393224 | tf_op jit(solution)/shard_map/ppermute | solution.py:319
  31.5 5.8 %collective-permute-start.8 = (f32[256,128]{1,0:T(8,128)S(1)}, f32[256,128]{1,0:T(8,128)S(1)}, u32[]{:S(2)}, u32[]{:S(2)}) collective-permute-start(f32[256,128]{1,0:T(8,128)S(1)} %get-tuple-element.71.refs_2_.refs_0_), channel_id=1, source_target_pairs={{0,16},{1,17},{2,18},{3,19},{4,20},{5,21},{6,22},{7,23},{8,24},{9,... | collective-permute-start | bytes 393224 | tf_op jit(solution)/shard_map/ppermute | solution.py:319
  33.1 5.8 %collective-permute-start.11 = (f32[256,128]{1,0:T(8,128)S(1)}, f32[256,128]{1,0:T(8,128)S(1)}, u32[]{:S(2)}, u32[]{:S(2)}) collective-permute-start(f32[256,128]{1,0:T(8,128)S(1)} %get-tuple-element.72.refs_2_), channel_id=1, source_target_pairs={{0,16},{1,17},{2,18},{3,19},{4,20},{5,21},{6,22},{7,23},{8,24},{9,... | collective-permute-start | bytes 393224 | tf_op jit(solution)/shard_map/ppermute | solution.py:319
  37.3 6.6 %collective-permute-start.10 = (f32[256,128]{1,0:T(8,128)S(1)}, f32[256,128]{1,0:T(8,128)S(1)}, u32[]{:S(2)}, u32[]{:S(2)}) collective-permute-start(f32[256,128]{1,0:T(8,128)S(1)} %get-tuple-element.73.refs_3_), channel_id=1, source_target_pairs={{0,8},{1,9},{2,10},{3,11},{4,12},{5,13},{6,14},{7,15},{8,0},{9,1},... | collective-permute-start | bytes 393224 | tf_op jit(solution)/shard_map/ppermute | solution.py:319
  38.9 11.5 %collective-permute-start.13 = (f32[256,128]{1,0:T(8,128)S(1)}, f32[256,128]{1,0:T(8,128)S(1)}, u32[]{:S(2)}, u32[]{:S(2)}) collective-permute-start(f32[256,128]{1,0:T(8,128)S(1)} %get-tuple-element.80.refs_2_), channel_id=1, source_target_pairs={{0,4},{1,5},{2,6},{3,7},{4,0},{5,1},{6,2},{7,3},{8,12},{9,13},{10,... | collective-permute-start | bytes 393224 | tf_op jit(solution)/shard_map/ppermute | solution.py:319
  39.2 14.8 %collective-permute-start.16 = (f32[256,128]{1,0:T(8,128)S(1)}, f32[256,128]{1,0:T(8,128)S(1)}, u32[]{:S(2)}, u32[]{:S(2)}) collective-permute-start(f32[256,128]{1,0:T(8,128)S(1)} %get-tuple-element.81.refs_3_), channel_id=1, source_target_pairs={{0,2},{1,3},{2,0},{3,1},{4,6},{5,7},{6,4},{7,5},{8,10},{9,11},{10,... | collective-permute-start | bytes 393224 | tf_op jit(solution)/shard_map/ppermute | solution.py:319
  44.0 9.0 %collective-permute-start.12 = (f32[256,128]{1,0:T(8,128)S(1)}, f32[256,128]{1,0:T(8,128)S(1)}, u32[]{:S(2)}, u32[]{:S(2)}) collective-permute-start(f32[256,128]{1,0:T(8,128)S(1)} %get-tuple-element.84.refs_2_), channel_id=1, source_target_pairs={{0,4},{1,5},{2,6},{3,7},{4,0},{5,1},{6,2},{7,3},{8,12},{9,13},{10,... | collective-permute-start | bytes 393224 | tf_op jit(solution)/shard_map/ppermute | solution.py:319
  44.1 6.3 %copy-start = (f32[4096]{0:T(1024)S(1)}, f32[4096]{0:T(1024)}, u32[]{:S(2)}) copy-start(f32[4096]{0:T(1024)} %param.7) | copy-start | bytes 49156
  44.1 17.2 %collective-permute-start.14 = (f32[256,128]{1,0:T(8,128)S(1)}, f32[256,128]{1,0:T(8,128)S(1)}, u32[]{:S(2)}, u32[]{:S(2)}) collective-permute-start(f32[256,128]{1,0:T(8,128)S(1)} %get-tuple-element.85.refs_3_), channel_id=1, source_target_pairs={{0,2},{1,3},{2,0},{3,1},{4,6},{5,7},{6,4},{7,5},{8,10},{9,11},{10,... | collective-permute-start | bytes 393224 | tf_op jit(solution)/shard_map/ppermute | solution.py:319
  50.5 7.2 %collective-permute-start.17 = (f32[256,128]{1,0:T(8,128)S(1)}, f32[256,128]{1,0:T(8,128)S(1)}, u32[]{:S(2)}, u32[]{:S(2)}) collective-permute-start(f32[256,128]{1,0:T(8,128)S(1)} %get-tuple-element.91.refs_2_), channel_id=1, source_target_pairs={{0,2},{1,3},{2,0},{3,1},{4,6},{5,7},{6,4},{7,5},{8,10},{9,11},{10,... | collective-permute-start | bytes 393224 | tf_op jit(solution)/shard_map/ppermute | solution.py:319
  53.0 8.3 %collective-permute-start.15 = (f32[256,128]{1,0:T(8,128)S(1)}, f32[256,128]{1,0:T(8,128)S(1)}, u32[]{:S(2)}, u32[]{:S(2)}) collective-permute-start(f32[256,128]{1,0:T(8,128)S(1)} %get-tuple-element.93.refs_5_), channel_id=1, source_target_pairs={{0,2},{1,3},{2,0},{3,1},{4,6},{5,7},{6,4},{7,5},{8,10},{9,11},{10,... | collective-permute-start | bytes 393224 | tf_op jit(solution)/shard_map/ppermute | solution.py:319
  57.9 2.0 %collective-permute-start.18 = (f32[1024,128]{1,0:T(8,128)S(1)}, f32[1024,128]{1,0:T(8,128)S(1)}, u32[]{:S(2)}, u32[]{:S(2)}) collective-permute-start(f32[1024,128]{1,0:T(8,128)S(1)} %get-tuple-element.99.refs_4_), channel_id=1, source_target_pairs={{0,1},{1,0},{2,3},{3,2},{4,5},{5,4},{6,7},{7,6},{8,9},{9,8},{10,11... | collective-permute-start | bytes 1572872 | tf_op jit(solution)/shard_map/ppermute | solution.py:319
  61.5 2.0 %collective-permute-start.19 = (f32[1024,128]{1,0:T(8,128)S(1)}, f32[1024,128]{1,0:T(8,128)S(1)}, u32[]{:S(2)}, u32[]{:S(2)}) collective-permute-start(f32[1024,128]{1,0:T(8,128)S(1)} %get-tuple-element.102.refs_5_), channel_id=1, source_target_pairs={{0,1},{1,0},{2,3},{3,2},{4,5},{5,4},{6,7},{7,6},{8,9},{9,8},{10,11... | collective-permute-start | bytes 1572872 | tf_op jit(solution)/shard_map/ppermute | solution.py:319

commit v6 on v5

--- a/solution.py
+++ b/solution.py
@@ -40,30 +40,36 @@
     return (half * HALF + chunk * HEADS) * E
 
 
-def state_kernel(chunk, mine, k_ref, v_ref, out_ref, k_buf, v_buf, sems):
-    base = first_column(chunk, mine)
+def load_columns(base, refs, bufs, sems):
     copies = []
     for piece in range(HEADS // PIECE):
-        for n, (ref, buf) in enumerate(((k_ref, k_buf), (v_ref, v_buf))):
-            copy = pltpu.make_async_copy(
-                ref.at[:, lane_tile(base + piece * WIDTH, WIDTH)],
-                buf.at[piece],
-                sems.at[n, piece],
-            )
+        cols = lane_tile(base + piece * WIDTH, WIDTH)
+        here = slice(piece * WIDTH, (piece + 1) * WIDTH)
+        copies.append(
+            [
+                pltpu.make_async_copy(ref.at[:, cols], buf.at[:, here], sems.at[n, piece])
+                for n, (ref, buf) in enumerate(zip(refs, bufs))
+            ]
+        )
+        for copy in copies[-1]:
             copy.start()
-            copies.append(copy)
-    for piece in range(HEADS // PIECE):
-        copies[2 * piece].wait()
-        copies[2 * piece + 1].wait()
-        for h in range(PIECE):
-            cols = slice(h * E, (h + 1) * E)
-            here = (piece * PIECE + h) * E
-            out_ref[here : here + E, :] = lax.dot_general(
-                k_buf[piece, :, cols],
-                v_buf[piece, :, cols],
-                (((0,), (0,)), ((), ())),
-                preferred_element_type=jnp.float32,
-            )
+    return copies
+
+
+def state_kernel(chunk, mine, k_ref, v_ref, out_ref, k_out_ref, v_out_ref, sems):
+    base = first_column(chunk, mine)
+    copies = load_columns(base, (k_ref, v_ref), (k_out_ref, v_out_ref), sems)
+    for h in range(HEADS):
+        if h % PIECE == 0:
+            for copy in copies[h // PIECE]:
+                copy.wait()
+        cols = slice(h * E, (h + 1) * E)
+        out_ref[cols, :] = lax.dot_general(
+            k_out_ref[:, cols],
+            v_out_ref[:, cols],
+            (((0,), (0,)), ((), ())),
+            preferred_element_type=jnp.float32,
+        )
 
 
 def call(kernel, name, arrays, shapes, scratch=(), tie=(), alias=None, mebibytes=4):
@@ -86,17 +92,16 @@
 
 
 def states_of(chunk, mine, keys, values, tie):
-    pieces = HEADS // PIECE
-    buf = pltpu.VMEM((pieces, keys.shape[0], WIDTH), jnp.bfloat16)
+    columns = (pltpu.VMEM, (keys.shape[0], HEADS * E), jnp.bfloat16)
     return call(
         functools.partial(state_kernel, chunk, mine),
         "states",
         [(keys, pltpu.HBM), (values, pltpu.HBM)],
-        [(pltpu.VMEM, (HEADS * E, E), jnp.float32)],
-        [buf, buf, pltpu.SemaphoreType.DMA((2, pieces))],
+        [(pltpu.VMEM, (HEADS * E, E), jnp.float32), columns, columns],
+        [pltpu.SemaphoreType.DMA((2, HEADS // PIECE))],
         tie,
         mebibytes=6,
-    )[0]
+    )
 
 
 def vmem_call(kernel, name, shapes, tie, *arrays):
@@ -221,47 +226,33 @@
     return vmem_call(kernel, "down", [low.shape] * 2, tie, own, got, low)
 
 
-def local_kernel(chunk, mine, q_ref, k_ref, v_ref, out_ref, q_out_ref, k_buf, v_buf, sems):
-    rows = q_ref.shape[0]
+def local_kernel(chunk, mine, q_ref, k_ref, v_ref, out_ref):
+    rows = k_ref.shape[0]
     base = first_column(chunk, mine)
-    copies = []
-    for piece in range(HEADS // PIECE):
-        cols = lane_tile(base + piece * WIDTH, WIDTH)
-        here = slice(piece * WIDTH, (piece + 1) * WIDTH)
-        for n, (ref, buf) in enumerate(((q_ref, q_out_ref), (k_ref, k_buf), (v_ref, v_buf))):
-            copy = pltpu.make_async_copy(ref.at[:, cols], buf.at[:, here], sems.at[n, piece])
-            copy.start()
-            copies.append(copy)
     causal = lax.broadcasted_iota(jnp.int32, (rows, rows), 0) >= lax.broadcasted_iota(
         jnp.int32, (rows, rows), 1
     )
     for h in range(HEADS):
-        if h % PIECE == 0:
-            for n in range(3):
-                copies[h // PIECE * 3 + n].wait()
         cols = slice(h * E, (h + 1) * E)
         scores = lax.dot_general(
-            q_out_ref[:, cols],
-            k_buf[:, cols],
+            q_ref[:, lane_tile(base + h * E, E)],
+            k_ref[:, cols],
             (((1,), (1,)), ((), ())),
             preferred_element_type=jnp.float32,
         )
         weights = jnp.where(causal, scores, 0.0).astype(jnp.bfloat16)
-        out_ref[:, cols] = jnp.dot(weights, v_buf[:, cols], preferred_element_type=jnp.float32)
+        out_ref[:, cols] = jnp.dot(weights, v_ref[:, cols], preferred_element_type=jnp.float32)
 
 
 def local_mix(chunk, mine, queries, keys, values, tie):
-    shape = (queries.shape[0], HEADS * E)
-    buf = pltpu.VMEM(shape, jnp.bfloat16)
     return call(
         functools.partial(local_kernel, chunk, mine),
         "local",
-        [(queries, pltpu.HBM), (keys, pltpu.HBM), (values, pltpu.HBM)],
-        [(pltpu.VMEM, shape, jnp.float32), (pltpu.VMEM, shape, jnp.bfloat16)],
-        [buf, buf, pltpu.SemaphoreType.DMA((3, HEADS // PIECE))],
-        tie,
-        mebibytes=10,
-    )
+        [(queries, pltpu.VMEM), (keys, pltpu.VMEM), (values, pltpu.VMEM)],
+        [(pltpu.VMEM, keys.shape, jnp.float32)],
+        tie=tie,
+        mebibytes=8,
+    )[0]
 
 
 def finish_kernel(chunk, mine, q_ref, m_ref, p_ref, gain_ref, *rest):
@@ -274,7 +265,7 @@
             cols = lane_tile(base + here, E)
             low = p_ref[here : here + E, :].astype(jnp.bfloat16)
             mixed = m_ref[:, here : here + E] + jnp.dot(
-                q_ref[:, here : here + E], low, preferred_element_type=jnp.float32
+                q_ref[:, cols], low, preferred_element_type=jnp.float32
             )
             meansq = jnp.mean(mixed * mixed, axis=-1, keepdims=True)
             normed = mixed * lax.rsqrt(meansq + 1e-6) * gain_ref[:, cols]
@@ -325,13 +316,12 @@
         return array
 
     todo = [(c, mine) for c in chunks for mine in (True, False)]
-    mixed = {}
+    mixed, columns = {}, {}
 
     def some_local():
         if todo:
-            c, mine = todo.pop(0)
-            mixed[c, mine] = local_mix(c, mine, queries, keys, values, latest)
-            after(mixed[c, mine][0])
+            this = todo.pop(0)
+            mixed[this] = after(local_mix(*this, queries, *columns[this], latest))
 
     order = [(levels, levels + 1), (levels + 1, levels)]
 
@@ -345,12 +335,13 @@
     low = [[None] * levels for _ in chunks]
     part_keep, part_got, part_low = ([[None, None] for _ in chunks] for _ in range(3))
     for c in chunks:
-        got[c] = swap(after(states_of(c, False, keys, values, latest)), 0)
-        keep[c] = after(states_of(c, True, keys, values, latest))
+        send, *columns[c, False] = states_of(c, False, keys, values, latest)
+        got[c] = swap(after(send), 0)
+        keep[c], *columns[c, True] = states_of(c, True, keys, values, latest)
+        after(keep[c])
         low[c][0], send_on, send, part_keep[c][1], part_keep[c][0] = first_up(keep[c], got[c], latest)
         part_got[c][1] = swap(after(send_on), 1)
         part_got[c][0] = swap(send, 1)
-    some_local()
     for c in chunks:
         part_low[c][1], send = go_up(1, False, part_keep[c][1], part_got[c][1], latest)
         got[c] = swap(after(send), 2)
@@ -360,10 +351,16 @@
     for level in range(2, levels):
         for c in chunks:
             up(level, c)
+            if level == levels - 1 and c == 0:
+                some_local()
     for c in chunks:
         bit, other = order[c % 2]
         before[c], send = go_along(bit, other, c % 2 == 1, keep[c], got[c], latest)
         got[c] = swap(after(send), other)
+        if c == 0:
+            while todo:
+                some_local()
+            gain = after(vmem_call(copy_kernel, "gain", [gain.shape], latest, gain)[0])
     top = levels - 1
     def part(c, n, before):
         part_keep[c][n], send = part_down(before, part_low[c][n], latest)
@@ -375,9 +372,6 @@
         got[c] = swap(after(send), top)
         if top == 2:
             part(c, 0, keep[c])
-    while todo:
-        some_local()
-    gain = after(vmem_call(copy_kernel, "gain", [gain.shape], latest, gain)[0])
     for level in range(top - 1, 1, -1):
         for c in chunks:
             keep[c], send = go_down(level, keep[c], got[c], low[c][level], latest)
@@ -391,7 +385,7 @@
         keep[c], send = last_down(part_keep[c], part_got[c], low[c][0], latest)
         got[c] = swap(after(send), 0)
         for mine, prefix in ((True, keep[c]), (False, got[c])):
-            out = finish(c, mine, queries.shape, *mixed[c, mine], prefix, gain, out, latest)
+            out = finish(c, mine, queries.shape, mixed[c, mine], queries, prefix, gain, out, latest)
             latest[:] = []
         after(out, pltpu.HBM)
     return out

time: 65.2 us -> 61.5 us (0.943)
  Pallas kernels: 26.8 us -> 21.2 us
  starting transfers between devices: 23.8 us -> 28.2 us
  waiting for transfers between devices: 14 us -> 9.8 us
  local copies, waits for them, and re-layouts: 0.01 us -> 1.87 us
    pallas_call x31, Pallas kernels: 26.8 us -> 21.2 us  [call(): pl.pallas_call(body, in_specs=[pl.BlockSpec(memory_space=space) for _, sp...]
    ppermute x20, starting transfers between devices: 23.8 us -> 28.2 us  [swap(): return lax.ppermute(x, AXES, [(i, i ^ 1 << level) for i in range(devices)])]
    ppermute x20, waiting for transfers between devices: 14 us -> 9.8 us  [swap(): return lax.ppermute(x, AXES, [(i, i ^ 1 << level) for i in range(devices)])]
    unnamed x2 -> x4, local copies, waits for them, and re-layouts: 0.01 us -> 1.87 us
  transfers between devices with their start and end apart: 20 -> 20, of which waited for: 6 -> 9; matrix products, arithmetic and copies ran while one was open for 0% -> 0% of each run, Pallas kernels for 36% -> 29%
where the time goes in v6:
time: 61.5 us; the launch traced here: 61.3 us
  starting transfers between devices  28.2 us (46%)
  Pallas kernels  21.2 us (34%)
  waiting for transfers between devices  9.8 us (16%)
  local copies, waits for them, and re-layouts  1.87 us (3%)
    ppermute x20, starting transfers between devices, swap(): return lax.ppermute(x, AXES, [(i, i ^ 1 << level) for i in range(devices)])  28.2 us
    pallas_call x31, Pallas kernels, call(): pl.pallas_call(body, in_specs=[pl.BlockSpec(memory_space=space) for _, sp...  21.2 us
    ppermute x20, waiting for transfers between devices, swap(): return lax.ppermute(x, AXES, [(i, i ^ 1 << level) for i in range(devices)])  9.8 us
    unnamed x4, local copies, waits for them, and re-layouts  1.87 us
  transfers between devices with their start and end apart: 20, of which 9 were waited for; matrix products, arithmetic and copies ran while one was open for 0% of the time, Pallas kernels for 29%

profile of v6, /device:TPU:0, one launch (start us, length us, event | category | flops | bytes accessed | tf_op | source)
XLA Modules:
  0.0 61.3 jit_solution(12678335146852536918)
XLA Ops:
  0.0 1.8 %states.4 = (f32[1024,128]{1,0:T(8,128)S(1)}, bf16[384,1024]{1,0:T(8,128)(2,1)S(1)}, bf16[384,1024]{1,0:T(8,128)(2,1)S(1)}) custom-call(bf16[384,4096]{1,0:T(8,128)(2,1)} %refs_0_.15, bf16[384,4096]{1,0:T(8,128)(2,1)} %refs_1_.7), custom_call_target="tpu_custom_call" | custom-call | flops 7000000000 | bytes 1 | tf_op jit(solution)/shard_map/states/pallas_call | solution.py:81
  1.8 0.5 collective-permute-start
  2.3 1.8 %states.5 = (f32[1024,128]{1,0:T(8,128)S(1)}, bf16[384,1024]{1,0:T(8,128)(2,1)S(1)}, bf16[384,1024]{1,0:T(8,128)(2,1)S(1)}) custom-call(bf16[384,4096]{1,0:T(8,128)(2,1)} %refs_0_.15, bf16[384,4096]{1,0:T(8,128)(2,1)} %refs_1_.7, f32[1024,128]{1,0:T(8,128)S(1)} %get-tuple-element.59.refs_2_), custom_call_target="tpu_custom_call" | custom-call | flops 7000000000 | bytes 1 | tf_op jit(solution)/shard_map/states/pallas_call | solution.py:81
  4.2 0.1 first_up.2
  4.3 2.7 %collective-permute-start.2 = (f32[256,128]{1,0:T(8,128)S(1)}, f32[256,128]{1,0:T(8,128)S(1)}, u32[]{:S(2)}, u32[]{:S(2)}) collective-permute-start(f32[256,128]{1,0:T(8,128)S(1)} %get-tuple-element.61.refs_2_), channel_id=1, source_target_pairs={{0,2},{1,3},{2,0},{3,1},{4,6},{5,7},{6,4},{7,5},{8,10},{9,11},{10,... | collective-permute-start | bytes 393224 | tf_op jit(solution)/shard_map/ppermute | solution.py:310
  7.0 1.8 %states.6 = (f32[1024,128]{1,0:T(8,128)S(1)}, bf16[384,1024]{1,0:T(8,128)(2,1)S(1)}, bf16[384,1024]{1,0:T(8,128)(2,1)S(1)}) custom-call(bf16[384,4096]{1,0:T(8,128)(2,1)} %refs_0_.15, bf16[384,4096]{1,0:T(8,128)(2,1)} %refs_1_.7, f32[256,128]{1,0:T(8,128)S(1)} %get-tuple-element.61.refs_2_), custom_call_target="tpu_custom_call" | custom-call | flops 7000000000 | bytes 1 | tf_op jit(solution)/shard_map/states/pallas_call | solution.py:81
  8.8 0.1 collective-permute-start.1
  8.9 0.2 collective-permute-start.3
  9.1 1.8 %states.7 = (f32[1024,128]{1,0:T(8,128)S(1)}, bf16[384,1024]{1,0:T(8,128)(2,1)S(1)}, bf16[384,1024]{1,0:T(8,128)(2,1)S(1)}) custom-call(bf16[384,4096]{1,0:T(8,128)(2,1)} %refs_0_.15, bf16[384,4096]{1,0:T(8,128)(2,1)} %refs_1_.7, f32[1024,128]{1,0:T(8,128)S(1)} %get-tuple-element.67.refs_2_), custom_call_target="tpu_custom_call" | custom-call | flops 7000000000 | bytes 1 | tf_op jit(solution)/shard_map/states/pallas_call | solution.py:81
  10.9 0.0 collective-permute-done.3.refs_1_
  10.9 0.1 first_up.3
  11.1 1.9 %collective-permute-start.6 = (f32[256,128]{1,0:T(8,128)S(1)}, f32[256,128]{1,0:T(8,128)S(1)}, u32[]{:S(2)}, u32[]{:S(2)}) collective-permute-start(f32[256,128]{1,0:T(8,128)S(1)} %get-tuple-element.69.refs_2_), channel_id=1, source_target_pairs={{0,2},{1,3},{2,0},{3,1},{4,6},{5,7},{6,4},{7,5},{8,10},{9,11},{10,... | collective-permute-start | bytes 393224 | tf_op jit(solution)/shard_map/ppermute | solution.py:310
  13.0 0.0 collective-permute-done.2.refs_1_
  13.0 2.7 %collective-permute-start.4 = (f32[256,128]{1,0:T(8,128)S(1)}, f32[256,128]{1,0:T(8,128)S(1)}, u32[]{:S(2)}, u32[]{:S(2)}) collective-permute-start(f32[256,128]{1,0:T(8,128)S(1)} %get-tuple-element.70.refs_2_), channel_id=1, source_target_pairs={{0,4},{1,5},{2,6},{3,7},{4,0},{5,1},{6,2},{7,3},{8,12},{9,13},{10,... | collective-permute-start | bytes 393224 | tf_op jit(solution)/shard_map/ppermute | solution.py:310
  15.7 0.4 collective-permute-start.5
  16.2 1.9 %copy-done = bf16[384,4096]{1,0:T(8,128)(2,1)S(1)} copy-done((bf16[384,4096]{1,0:T(8,128)(2,1)S(1)}, bf16[384,4096]{1,0:T(8,128)(2,1)}, u32[]{:S(2)}) %copy-start) | copy-done | bytes 3145752
  18.0 1.8 %local.4.refs_2_.refs_1_ = f32[384,1024]{1,0:T(8,128)S(1)} custom-call(bf16[384,4096]{1,0:T(8,128)(2,1)S(1)} %copy-done, bf16[384,1024]{1,0:T(8,128)(2,1)S(1)} %get-tuple-element.77.refs_1_, bf16[384,1024]{1,0:T(8,128)(2,1)S(1)} %get-tuple-element.78.refs_2_, f32[256,128]{1,0:T(8,128)S(1)} %get-tuple-element.71.refs_3_.refs_0_), custom_call_target="tpu_custom_call" | custom-call | flops 7000000000 | bytes 1 | tf_op jit(solution)/shard_map/local/pallas_call | solution.py:81
  19.8 0.3 collective-permute-done.6.refs_1_
  20.1 0.8 %collective-permute-start.8 = (f32[256,128]{1,0:T(8,128)S(1)}, f32[256,128]{1,0:T(8,128)S(1)}, u32[]{:S(2)}, u32[]{:S(2)}) collective-permute-start(f32[256,128]{1,0:T(8,128)S(1)} %get-tuple-element.79.refs_2_), channel_id=1, source_target_pairs={{0,4},{1,5},{2,6},{3,7},{4,0},{5,1},{6,2},{7,3},{8,12},{9,13},{10,... | collective-permute-start | bytes 393224 | tf_op jit(solution)/shard_map/ppermute | solution.py:310
  21.0 1.9 %collective-permute-done.5.refs_1_ = f32[256,128]{1,0:T(8,128)S(1)} collective-permute-done((f32[256,128]{1,0:T(8,128)S(1)}, f32[256,128]{1,0:T(8,128)S(1)}, u32[]{:S(2)}, u32[]{:S(2)}) %collective-permute-start.5) | collective-permute-done | bytes 131104 | tf_op jit(solution)/shard_map/ppermute | solution.py:310
  22.9 1.8 %local.5.refs_2_.refs_1_ = f32[384,1024]{1,0:T(8,128)S(1)} custom-call(bf16[384,4096]{1,0:T(8,128)(2,1)S(1)} %copy-done, bf16[384,1024]{1,0:T(8,128)(2,1)S(1)} %get-tuple-element.72.refs_1_, bf16[384,1024]{1,0:T(8,128)(2,1)S(1)} %get-tuple-element.73.refs_2_, f32[256,128]{1,0:T(8,128)S(1)} %get-tuple-element.80.refs_3_.refs_0_), custom_call_target="tpu_custom_call" | custom-call | flops 7000000000 | bytes 1 | tf_op jit(solution)/shard_map/local/pallas_call | solution.py:81
  24.7 1.6 %collective-permute-start.7 = (f32[256,128]{1,0:T(8,128)S(1)}, f32[256,128]{1,0:T(8,128)S(1)}, u32[]{:S(2)}, u32[]{:S(2)}) collective-permute-start(f32[256,128]{1,0:T(8,128)S(1)} %get-tuple-element.81.refs_3_.refs_0_), channel_id=1, source_target_pairs={{0,8},{1,9},{2,10},{3,11},{4,12},{5,13},{6,14},{7,15},{8,0},{9,1},... | collective-permute-start | bytes 393224 | tf_op jit(solution)/shard_map/ppermute | solution.py:310
  26.3 1.8 %local.6.refs_2_.refs_1_ = f32[384,1024]{1,0:T(8,128)S(1)} custom-call(bf16[384,4096]{1,0:T(8,128)(2,1)S(1)} %copy-done, bf16[384,1024]{1,0:T(8,128)(2,1)S(1)} %get-tuple-element.82.refs_1_, bf16[384,1024]{1,0:T(8,128)(2,1)S(1)} %get-tuple-element.83.refs_2_, f32[256,128]{1,0:T(8,128)S(1)} %get-tuple-element.81.refs_3_.refs_0_), custom_call_target="tpu_custom_call" | custom-call | flops 7000000000 | bytes 1 | tf_op jit(solution)/shard_map/local/pallas_call | solution.py:81
  28.1 0.7 %collective-permute-done.8.refs_1_ = f32[256,128]{1,0:T(8,128)S(1)} collective-permute-done((f32[256,128]{1,0:T(8,128)S(1)}, f32[256,128]{1,0:T(8,128)S(1)}, u32[]{:S(2)}, u32[]{:S(2)}) %collective-permute-start.8) | collective-permute-done | bytes 131104 | tf_op jit(solution)/shard_map/ppermute | solution.py:310
  28.8 1.7 %collective-permute-start.9 = (f32[256,128]{1,0:T(8,128)S(1)}, f32[256,128]{1,0:T(8,128)S(1)}, u32[]{:S(2)}, u32[]{:S(2)}) collective-permute-start(f32[256,128]{1,0:T(8,128)S(1)} %get-tuple-element.84.refs_2_.refs_0_), channel_id=1, source_target_pairs={{0,16},{1,17},{2,18},{3,19},{4,20},{5,21},{6,22},{7,23},{8,24},{9,... | collective-permute-start | bytes 393224 | tf_op jit(solution)/shard_map/ppermute | solution.py:310
  30.5 1.1 %collective-permute-start.11 = (f32[256,128]{1,0:T(8,128)S(1)}, f32[256,128]{1,0:T(8,128)S(1)}, u32[]{:S(2)}, u32[]{:S(2)}) collective-permute-start(f32[256,128]{1,0:T(8,128)S(1)} %get-tuple-element.85.refs_3_), channel_id=1, source_target_pairs={{0,16},{1,17},{2,18},{3,19},{4,20},{5,21},{6,22},{7,23},{8,24},{9,... | collective-permute-start | bytes 393224 | tf_op jit(solution)/shard_map/ppermute | solution.py:310
  31.6 1.8 %local.7.refs_1_ = f32[384,1024]{1,0:T(8,128)S(1)} custom-call(bf16[384,4096]{1,0:T(8,128)(2,1)S(1)} %copy-done, bf16[384,1024]{1,0:T(8,128)(2,1)S(1)} %get-tuple-element.62.refs_1_, bf16[384,1024]{1,0:T(8,128)(2,1)S(1)} %get-tuple-element.63.refs_2_, f32[256,128]{1,0:T(8,128)S(1)} %get-tuple-element.85.refs_3_), custom_call_target="tpu_custom_call" | custom-call | flops 7000000000 | bytes 1 | tf_op jit(solution)/shard_map/local/pallas_call | solution.py:81
  33.4 1.1 %collective-permute-done.9.refs_1_ = f32[256,128]{1,0:T(8,128)S(1)} collective-permute-done((f32[256,128]{1,0:T(8,128)S(1)}, f32[256,128]{1,0:T(8,128)S(1)}, u32[]{:S(2)}, u32[]{:S(2)}) %collective-permute-start.9) | collective-permute-done | bytes 131104 | tf_op jit(solution)/shard_map/ppermute | solution.py:310
  34.6 1.4 %collective-permute-start.10 = (f32[256,128]{1,0:T(8,128)S(1)}, f32[256,128]{1,0:T(8,128)S(1)}, u32[]{:S(2)}, u32[]{:S(2)}) collective-permute-start(f32[256,128]{1,0:T(8,128)S(1)} %get-tuple-element.86.refs_3_), channel_id=1, source_target_pairs={{0,8},{1,9},{2,10},{3,11},{4,12},{5,13},{6,14},{7,15},{8,0},{9,1},... | collective-permute-start | bytes 393224 | tf_op jit(solution)/shard_map/ppermute | solution.py:310
  36.0 2.5 %collective-permute-start.13 = (f32[256,128]{1,0:T(8,128)S(1)}, f32[256,128]{1,0:T(8,128)S(1)}, u32[]{:S(2)}, u32[]{:S(2)}) collective-permute-start(f32[256,128]{1,0:T(8,128)S(1)} %get-tuple-element.93.refs_2_), channel_id=1, source_target_pairs={{0,4},{1,5},{2,6},{3,7},{4,0},{5,1},{6,2},{7,3},{8,12},{9,13},{10,... | collective-permute-start | bytes 393224 | tf_op jit(solution)/shard_map/ppermute | solution.py:310
  38.6 2.4 %collective-permute-start.16 = (f32[256,128]{1,0:T(8,128)S(1)}, f32[256,128]{1,0:T(8,128)S(1)}, u32[]{:S(2)}, u32[]{:S(2)}) collective-permute-start(f32[256,128]{1,0:T(8,128)S(1)} %get-tuple-element.94.refs_3_), channel_id=1, source_target_pairs={{0,2},{1,3},{2,0},{3,1},{4,6},{5,7},{6,4},{7,5},{8,10},{9,11},{10,... | collective-permute-start | bytes 393224 | tf_op jit(solution)/shard_map/ppermute | solution.py:310
  41.0 1.2 %collective-permute-start.12 = (f32[256,128]{1,0:T(8,128)S(1)}, f32[256,128]{1,0:T(8,128)S(1)}, u32[]{:S(2)}, u32[]{:S(2)}) collective-permute-start(f32[256,128]{1,0:T(8,128)S(1)} %get-tuple-element.97.refs_2_), channel_id=1, source_target_pairs={{0,4},{1,5},{2,6},{3,7},{4,0},{5,1},{6,2},{7,3},{8,12},{9,13},{10,... | collective-permute-start | bytes 393224 | tf_op jit(solution)/shard_map/ppermute | solution.py:310
  42.2 2.4 %collective-permute-start.14 = (f32[256,128]{1,0:T(8,128)S(1)}, f32[256,128]{1,0:T(8,128)S(1)}, u32[]{:S(2)}, u32[]{:S(2)}) collective-permute-start(f32[256,128]{1,0:T(8,128)S(1)} %get-tuple-element.101.refs_2_), channel_id=1, source_target_pairs={{0,2},{1,3},{2,0},{3,1},{4,6},{5,7},{6,4},{7,5},{8,10},{9,11},{10,... | collective-permute-start | bytes 393224 | tf_op jit(solution)/shard_map/ppermute | solution.py:310
  44.7 0.4 collective-permute-done.13.refs_0_
  45.1 1.8 %collective-permute-start.17 = (f32[256,128]{1,0:T(8,128)S(1)}, f32[256,128]{1,0:T(8,128)S(1)}, u32[]{:S(2)}, u32[]{:S(2)}) collective-permute-start(f32[256,128]{1,0:T(8,128)S(1)} %get-tuple-element.102.refs_2_), channel_id=1, source_target_pairs={{0,2},{1,3},{2,0},{3,1},{4,6},{5,7},{6,4},{7,5},{8,10},{9,11},{10,... | collective-permute-start | bytes 393224 | tf_op jit(solution)/shard_map/ppermute | solution.py:310
  46.8 1.8 %collective-permute-done.12.refs_0_ = f32[256,128]{1,0:T(8,128)S(1)} collective-permute-done((f32[256,128]{1,0:T(8,128)S(1)}, f32[256,128]{1,0:T(8,128)S(1)}, u32[]{:S(2)}, u32[]{:S(2)}) %collective-permute-start.12) | collective-permute-done | bytes 131104 | tf_op jit(solution)/shard_map/ppermute | solution.py:310
  48.6 2.5 %collective-permute-start.15 = (f32[256,128]{1,0:T(8,128)S(1)}, f32[256,128]{1,0:T(8,128)S(1)}, u32[]{:S(2)}, u32[]{:S(2)}) collective-permute-start(f32[256,128]{1,0:T(8,128)S(1)} %get-tuple-element.104.refs_5_), channel_id=1, source_target_pairs={{0,2},{1,3},{2,0},{3,1},{4,6},{5,7},{6,4},{7,5},{8,10},{9,11},{10,... | collective-permute-start | bytes 393224 | tf_op jit(solution)/shard_map/ppermute | solution.py:310
  51.1 3.0 %collective-permute-done.17.refs_3_ = f32[256,128]{1,0:T(8,128)S(1)} collective-permute-done((f32[256,128]{1,0:T(8,128)S(1)}, f32[256,128]{1,0:T(8,128)S(1)}, u32[]{:S(2)}, u32[]{:S(2)}) %collective-permute-start.17) | collective-permute-done | bytes 131104 | tf_op jit(solution)/shard_map/ppermute | solution.py:310
  54.0 0.2 last_down.2
  54.2 0.1 collective-permute-start.18
  54.3 1.4 %finish.4.refs_4_ = bf16[384,4096]{1,0:T(8,128)(2,1)} custom-call(bf16[384,4096]{1,0:T(8,128)(2,1)S(1)} %copy-done, f32[384,1024]{1,0:T(8,128)S(1)} %local.4.refs_2_.refs_1_, f32[1024,128]{1,0:T(8,128)S(1)} %get-tuple-element.110.refs_2_, f32[1,4096]{1,0:T(1,128)S(1)} %gain.1.refs_2_.refs_3_, f32[1024,128]{1,0:T(8,128)S(1)} %get-tuple-element.109.refs_4_), custom_call_target="tpu_custom_call" | custom-call | flops 7000000000 | bytes 1 | tf_op jit(solution)/shard_map/finish/pallas_call | solution.py:81
  55.8 0.4 collective-permute-done.18.refs_2_
  56.2 1.4 %finish.5.refs_5_.refs_4_ = bf16[384,4096]{1,0:T(8,128)(2,1)} custom-call(bf16[384,4096]{1,0:T(8,128)(2,1)S(1)} %copy-done, f32[384,1024]{1,0:T(8,128)S(1)} %local.5.refs_2_.refs_1_, f32[1024,128]{1,0:T(8,128)S(1)} %collective-permute-done.18.refs_2_, f32[1,4096]{1,0:T(1,128)S(1)} %gain.1.refs_2_.refs_3_, ...), custom_call_target="tpu_custom_call", output_to_operand_aliasing={{}: (4, {})} | custom-call | flops 7000000000 | bytes 1 | tf_op jit(solution)/shard_map/finish/pallas_call | solution.py:81
  57.7 0.2 last_down.3
  57.9 0.2 collective-permute-start.19
  58.1 1.4 %finish.6.refs_4_ = bf16[384,4096]{1,0:T(8,128)(2,1)} custom-call(bf16[384,4096]{1,0:T(8,128)(2,1)S(1)} %copy-done, f32[384,1024]{1,0:T(8,128)S(1)} %local.6.refs_2_.refs_1_, f32[1024,128]{1,0:T(8,128)S(1)} %get-tuple-element.112.refs_2_, f32[1,4096]{1,0:T(1,128)S(1)} %gain.1.refs_2_.refs_3_, ...), custom_call_target="tpu_custom_call", output_to_operand_aliasing={{}: (4, {})} | custom-call | flops 7000000000 | bytes 1 | tf_op jit(solution)/shard_map/finish/pallas_call | solution.py:81
  59.5 0.3 collective-permute-done.19.refs_2_
  59.8 1.4 %finish.7 = bf16[384,4096]{1,0:T(8,128)(2,1)} custom-call(bf16[384,4096]{1,0:T(8,128)(2,1)S(1)} %copy-done, f32[384,1024]{1,0:T(8,128)S(1)} %local.7.refs_1_, f32[1024,128]{1,0:T(8,128)S(1)} %collective-permute-done.19.refs_2_, f32[1,4096]{1,0:T(1,128)S(1)} %gain.1.refs_2_.refs_3_, bf16[384,4096]{1,0:T(8,128)(2,1)} %finish.6.refs_4_), custom_call_target="tpu_custom_call", output_to_operand_aliasing={{}: (4, {})} | custom-call | flops 7000000000 | bytes 1 | tf_op jit(solution)/shard_map/finish/pallas_call | solution.py:81
  (27 shorter events, 0.4 us)
Async XLA Ops:
  1.8 2.3 %collective-permute-start = (f32[1024,128]{1,0:T(8,128)S(1)}, f32[1024,128]{1,0:T(8,128)S(1)}, u32[]{:S(2)}, u32[]{:S(2)}) collective-permute-start(f32[1024,128]{1,0:T(8,128)S(1)} %get-tuple-element.59.refs_2_), channel_id=1, source_target_pairs={{0,1},{1,0},{2,3},{3,2},{4,5},{5,4},{6,7},{7,6},{8,9},{9,8},{10,11... | collective-permute-start | bytes 1572872 | tf_op jit(solution)/shard_map/ppermute | solution.py:310
  4.3 8.7 %collective-permute-start.2 = (f32[256,128]{1,0:T(8,128)S(1)}, f32[256,128]{1,0:T(8,128)S(1)}, u32[]{:S(2)}, u32[]{:S(2)}) collective-permute-start(f32[256,128]{1,0:T(8,128)S(1)} %get-tuple-element.61.refs_2_), channel_id=1, source_target_pairs={{0,2},{1,3},{2,0},{3,1},{4,6},{5,7},{6,4},{7,5},{8,10},{9,11},{10,... | collective-permute-start | bytes 393224 | tf_op jit(solution)/shard_map/ppermute | solution.py:310
  8.8 7.3 %collective-permute-start.1 = (f32[256,128]{1,0:T(8,128)S(1)}, f32[256,128]{1,0:T(8,128)S(1)}, u32[]{:S(2)}, u32[]{:S(2)}) collective-permute-start(f32[256,128]{1,0:T(8,128)S(1)} %get-tuple-element.65), channel_id=1, source_target_pairs={{0,2},{1,3},{2,0},{3,1},{4,6},{5,7},{6,4},{7,5},{8,10},{9,11},{10,... | collective-permute-start | bytes 393224 | tf_op jit(solution)/shard_map/ppermute | solution.py:310
  8.9 2.0 %collective-permute-start.3 = (f32[1024,128]{1,0:T(8,128)S(1)}, f32[1024,128]{1,0:T(8,128)S(1)}, u32[]{:S(2)}, u32[]{:S(2)}) collective-permute-start(f32[1024,128]{1,0:T(8,128)S(1)} %get-tuple-element.67.refs_2_), channel_id=1, source_target_pairs={{0,1},{1,0},{2,3},{3,2},{4,5},{5,4},{6,7},{7,6},{8,9},{9,8},{10,11... | collective-permute-start | bytes 1572872 | tf_op jit(solution)/shard_map/ppermute | solution.py:310
  11.1 9.0 %collective-permute-start.6 = (f32[256,128]{1,0:T(8,128)S(1)}, f32[256,128]{1,0:T(8,128)S(1)}, u32[]{:S(2)}, u32[]{:S(2)}) collective-permute-start(f32[256,128]{1,0:T(8,128)S(1)} %get-tuple-element.69.refs_2_), channel_id=1, source_target_pairs={{0,2},{1,3},{2,0},{3,1},{4,6},{5,7},{6,4},{7,5},{8,10},{9,11},{10,... | collective-permute-start | bytes 393224 | tf_op jit(solution)/shard_map/ppermute | solution.py:310
  13.0 11.7 %collective-permute-start.4 = (f32[256,128]{1,0:T(8,128)S(1)}, f32[256,128]{1,0:T(8,128)S(1)}, u32[]{:S(2)}, u32[]{:S(2)}) collective-permute-start(f32[256,128]{1,0:T(8,128)S(1)} %get-tuple-element.70.refs_2_), channel_id=1, source_target_pairs={{0,4},{1,5},{2,6},{3,7},{4,0},{5,1},{6,2},{7,3},{8,12},{9,13},{10,... | collective-permute-start | bytes 393224 | tf_op jit(solution)/shard_map/ppermute | solution.py:310
  15.7 7.2 %collective-permute-start.5 = (f32[256,128]{1,0:T(8,128)S(1)}, f32[256,128]{1,0:T(8,128)S(1)}, u32[]{:S(2)}, u32[]{:S(2)}) collective-permute-start(f32[256,128]{1,0:T(8,128)S(1)} %get-tuple-element.75), channel_id=1, source_target_pairs={{0,2},{1,3},{2,0},{3,1},{4,6},{5,7},{6,4},{7,5},{8,10},{9,11},{10,... | collective-permute-start | bytes 393224 | tf_op jit(solution)/shard_map/ppermute | solution.py:310
  16.2 1.9 %copy-start = (bf16[384,4096]{1,0:T(8,128)(2,1)S(1)}, bf16[384,4096]{1,0:T(8,128)(2,1)}, u32[]{:S(2)}) copy-start(bf16[384,4096]{1,0:T(8,128)(2,1)} %refs_0_.23) | copy-start | bytes 9437188
  20.1 8.7 %collective-permute-start.8 = (f32[256,128]{1,0:T(8,128)S(1)}, f32[256,128]{1,0:T(8,128)S(1)}, u32[]{:S(2)}, u32[]{:S(2)}) collective-permute-start(f32[256,128]{1,0:T(8,128)S(1)} %get-tuple-element.79.refs_2_), channel_id=1, source_target_pairs={{0,4},{1,5},{2,6},{3,7},{4,0},{5,1},{6,2},{7,3},{8,12},{9,13},{10,... | collective-permute-start | bytes 393224 | tf_op jit(solution)/shard_map/ppermute | solution.py:310
  24.7 5.8 %collective-permute-start.7 = (f32[256,128]{1,0:T(8,128)S(1)}, f32[256,128]{1,0:T(8,128)S(1)}, u32[]{:S(2)}, u32[]{:S(2)}) collective-permute-start(f32[256,128]{1,0:T(8,128)S(1)} %get-tuple-element.81.refs_3_.refs_0_), channel_id=1, source_target_pairs={{0,8},{1,9},{2,10},{3,11},{4,12},{5,13},{6,14},{7,15},{8,0},{9,1},... | collective-permute-start | bytes 393224 | tf_op jit(solution)/shard_map/ppermute | solution.py:310
  28.8 5.7 %collective-permute-start.9 = (f32[256,128]{1,0:T(8,128)S(1)}, f32[256,128]{1,0:T(8,128)S(1)}, u32[]{:S(2)}, u32[]{:S(2)}) collective-permute-start(f32[256,128]{1,0:T(8,128)S(1)} %get-tuple-element.84.refs_2_.refs_0_), channel_id=1, source_target_pairs={{0,16},{1,17},{2,18},{3,19},{4,20},{5,21},{6,22},{7,23},{8,24},{9,... | collective-permute-start | bytes 393224 | tf_op jit(solution)/shard_map/ppermute | solution.py:310
  30.5 5.4 %collective-permute-start.11 = (f32[256,128]{1,0:T(8,128)S(1)}, f32[256,128]{1,0:T(8,128)S(1)}, u32[]{:S(2)}, u32[]{:S(2)}) collective-permute-start(f32[256,128]{1,0:T(8,128)S(1)} %get-tuple-element.85.refs_3_), channel_id=1, source_target_pairs={{0,16},{1,17},{2,18},{3,19},{4,20},{5,21},{6,22},{7,23},{8,24},{9,... | collective-permute-start | bytes 393224 | tf_op jit(solution)/shard_map/ppermute | solution.py:310
  31.6 1.8 %copy-start.1 = (f32[4096]{0:T(1024)S(1)}, f32[4096]{0:T(1024)}, u32[]{:S(2)}) copy-start(f32[4096]{0:T(1024)} %param.7) | copy-start | bytes 49156
  34.6 6.4 %collective-permute-start.10 = (f32[256,128]{1,0:T(8,128)S(1)}, f32[256,128]{1,0:T(8,128)S(1)}, u32[]{:S(2)}, u32[]{:S(2)}) collective-permute-start(f32[256,128]{1,0:T(8,128)S(1)} %get-tuple-element.86.refs_3_), channel_id=1, source_target_pairs={{0,8},{1,9},{2,10},{3,11},{4,12},{5,13},{6,14},{7,15},{8,0},{9,1},... | collective-permute-start | bytes 393224 | tf_op jit(solution)/shard_map/ppermute | solution.py:310
  36.0 9.0 %collective-permute-start.13 = (f32[256,128]{1,0:T(8,128)S(1)}, f32[256,128]{1,0:T(8,128)S(1)}, u32[]{:S(2)}, u32[]{:S(2)}) collective-permute-start(f32[256,128]{1,0:T(8,128)S(1)} %get-tuple-element.93.refs_2_), channel_id=1, source_target_pairs={{0,4},{1,5},{2,6},{3,7},{4,0},{5,1},{6,2},{7,3},{8,12},{9,13},{10,... | collective-permute-start | bytes 393224 | tf_op jit(solution)/shard_map/ppermute | solution.py:310
  38.6 12.5 %collective-permute-start.16 = (f32[256,128]{1,0:T(8,128)S(1)}, f32[256,128]{1,0:T(8,128)S(1)}, u32[]{:S(2)}, u32[]{:S(2)}) collective-permute-start(f32[256,128]{1,0:T(8,128)S(1)} %get-tuple-element.94.refs_3_), channel_id=1, source_target_pairs={{0,2},{1,3},{2,0},{3,1},{4,6},{5,7},{6,4},{7,5},{8,10},{9,11},{10,... | collective-permute-start | bytes 393224 | tf_op jit(solution)/shard_map/ppermute | solution.py:310
  41.0 7.5 %collective-permute-start.12 = (f32[256,128]{1,0:T(8,128)S(1)}, f32[256,128]{1,0:T(8,128)S(1)}, u32[]{:S(2)}, u32[]{:S(2)}) collective-permute-start(f32[256,128]{1,0:T(8,128)S(1)} %get-tuple-element.97.refs_2_), channel_id=1, source_target_pairs={{0,4},{1,5},{2,6},{3,7},{4,0},{5,1},{6,2},{7,3},{8,12},{9,13},{10,... | collective-permute-start | bytes 393224 | tf_op jit(solution)/shard_map/ppermute | solution.py:310
  42.2 15.4 %collective-permute-start.14 = (f32[256,128]{1,0:T(8,128)S(1)}, f32[256,128]{1,0:T(8,128)S(1)}, u32[]{:S(2)}, u32[]{:S(2)}) collective-permute-start(f32[256,128]{1,0:T(8,128)S(1)} %get-tuple-element.101.refs_2_), channel_id=1, source_target_pairs={{0,2},{1,3},{2,0},{3,1},{4,6},{5,7},{6,4},{7,5},{8,10},{9,11},{10,... | collective-permute-start | bytes 393224 | tf_op jit(solution)/shard_map/ppermute | solution.py:310
  45.1 9.0 %collective-permute-start.17 = (f32[256,128]{1,0:T(8,128)S(1)}, f32[256,128]{1,0:T(8,128)S(1)}, u32[]{:S(2)}, u32[]{:S(2)}) collective-permute-start(f32[256,128]{1,0:T(8,128)S(1)} %get-tuple-element.102.refs_2_), channel_id=1, source_target_pairs={{0,2},{1,3},{2,0},{3,1},{4,6},{5,7},{6,4},{7,5},{8,10},{9,11},{10,... | collective-permute-start | bytes 393224 | tf_op jit(solution)/shard_map/ppermute | solution.py:310
  48.6 9.0 %collective-permute-start.15 = (f32[256,128]{1,0:T(8,128)S(1)}, f32[256,128]{1,0:T(8,128)S(1)}, u32[]{:S(2)}, u32[]{:S(2)}) collective-permute-start(f32[256,128]{1,0:T(8,128)S(1)} %get-tuple-element.104.refs_5_), channel_id=1, source_target_pairs={{0,2},{1,3},{2,0},{3,1},{4,6},{5,7},{6,4},{7,5},{8,10},{9,11},{10,... | collective-permute-start | bytes 393224 | tf_op jit(solution)/shard_map/ppermute | solution.py:310
  54.2 2.0 %collective-permute-start.18 = (f32[1024,128]{1,0:T(8,128)S(1)}, f32[1024,128]{1,0:T(8,128)S(1)}, u32[]{:S(2)}, u32[]{:S(2)}) collective-permute-start(f32[1024,128]{1,0:T(8,128)S(1)} %get-tuple-element.109.refs_4_), channel_id=1, source_target_pairs={{0,1},{1,0},{2,3},{3,2},{4,5},{5,4},{6,7},{7,6},{8,9},{9,8},{10,11... | collective-permute-start | bytes 1572872 | tf_op jit(solution)/shard_map/ppermute | solution.py:310
  57.9 2.0 %collective-permute-start.19 = (f32[1024,128]{1,0:T(8,128)S(1)}, f32[1024,128]{1,0:T(8,128)S(1)}, u32[]{:S(2)}, u32[]{:S(2)}) collective-permute-start(f32[1024,128]{1,0:T(8,128)S(1)} %get-tuple-element.111.refs_5_), channel_id=1, source_target_pairs={{0,1},{1,0},{2,3},{3,2},{4,5},{5,4},{6,7},{7,6},{8,9},{9,8},{10,11... | collective-permute-start | bytes 1572872 | tf_op jit(solution)/shard_map/ppermute | solution.py:310

commit v7 on v6

--- a/solution.py
+++ b/solution.py
@@ -342,44 +342,66 @@
         low[c][0], send_on, send, part_keep[c][1], part_keep[c][0] = first_up(keep[c], got[c], latest)
         part_got[c][1] = swap(after(send_on), 1)
         part_got[c][0] = swap(send, 1)
-    for c in chunks:
+    top = levels - 1
+
+    def goes_on(c):
         part_low[c][1], send = go_up(1, False, part_keep[c][1], part_got[c][1], latest)
         got[c] = swap(after(send), 2)
+
+    def stays(c):
         part_low[c][0], keep[c] = go_up(1, False, part_keep[c][0], part_got[c][0], latest)
         after(keep[c])
-        some_local()
-    for level in range(2, levels):
-        for c in chunks:
-            up(level, c)
-            if level == levels - 1 and c == 0:
-                some_local()
-    for c in chunks:
+
+    def along(c):
         bit, other = order[c % 2]
         before[c], send = go_along(bit, other, c % 2 == 1, keep[c], got[c], latest)
         got[c] = swap(after(send), other)
-        if c == 0:
-            while todo:
-                some_local()
-            gain = after(vmem_call(copy_kernel, "gain", [gain.shape], latest, gain)[0])
-    top = levels - 1
-    def part(c, n, before):
-        part_keep[c][n], send = part_down(before, part_low[c][n], latest)
+
+    def turn(c):
+        bit, turned = order[0][1], c % 2 == 1
+        keep[c], send = turn_down(bit, turned, top, got[c], low[c][top], before[c], latest)
+        got[c] = swap(after(send), top)
+
+    def part(c, n):
+        whole = got[c] if n else keep[c]
+        part_keep[c][n], send = part_down(whole, part_low[c][n], latest)
         part_got[c][n] = swap(after(send), 1)
 
-    for c in chunks:
-        turned = c % 2 == 1
-        keep[c], send = turn_down(order[0][1], turned, top, got[c], low[c][top], before[c], latest)
-        got[c] = swap(after(send), top)
-        if top == 2:
-            part(c, 0, keep[c])
+    goes_on(0)
+    stays(0)
+    some_local()
+    goes_on(1)
+    up(2, 0)
+    stays(1)
+    some_local()
+    if levels == 3:
+        along(0)
+        up(2, 1)
+        some_local()
+        turn(0)
+        along(1)
+        part(0, 0)
+    else:
+        up(2, 1)
+        for level in range(3, levels):
+            for c in chunks:
+                up(level, c)
+        for c in chunks:
+            along(c)
+        turn(0)
+    turn(1)
     for level in range(top - 1, 1, -1):
         for c in chunks:
             keep[c], send = go_down(level, keep[c], got[c], low[c][level], latest)
             got[c] = swap(after(send), level)
-            if level == 2:
-                part(c, 0, keep[c])
-    for c in chunks:
-        part(c, 1, got[c])
+    if levels > 3:
+        part(0, 0)
+    part(0, 1)
+    part(1, 0)
+    while todo:
+        some_local()
+    gain = after(vmem_call(copy_kernel, "gain", [gain.shape], latest, gain)[0])
+    part(1, 1)
     out = None
     for c in chunks:
         keep[c], send = last_down(part_keep[c], part_got[c], low[c][0], latest)

time: 61.5 us -> 56.7 us (0.922)
  waiting for transfers between devices: 9.8 us -> 4.91 us
    ppermute x20, waiting for transfers between devices: 9.8 us -> 4.91 us  [swap(): return lax.ppermute(x, AXES, [(i, i ^ 1 << level) for i in range(devices)])]
  transfers between devices with their start and end apart: 20 -> 20, of which waited for: 9 -> 7; matrix products, arithmetic and copies ran while one was open for 0% -> 0% of each run, Pallas kernels for 29% -> 31%
where the time goes in v7:
time: 56.7 us; the launch traced here: 56.4 us
  starting transfers between devices  28.2 us (50%)
  Pallas kernels  21.2 us (37%)
  waiting for transfers between devices  4.91 us (9%)
  local copies, waits for them, and re-layouts  1.87 us (3%)
    ppermute x20, starting transfers between devices, swap(): return lax.ppermute(x, AXES, [(i, i ^ 1 << level) for i in range(devices)])  28.2 us
    pallas_call x31, Pallas kernels, call(): pl.pallas_call(body, in_specs=[pl.BlockSpec(memory_space=space) for _, sp...  21.2 us
    ppermute x20, waiting for transfers between devices, swap(): return lax.ppermute(x, AXES, [(i, i ^ 1 << level) for i in range(devices)])  4.91 us
    unnamed x4, local copies, waits for them, and re-layouts  1.87 us
  transfers between devices with their start and end apart: 20, of which 7 were waited for; matrix products, arithmetic and copies ran while one was open for 0% of the time, Pallas kernels for 31%

profile of v7, /device:TPU:0, one launch (start us, length us, event | category | flops | bytes accessed | tf_op | source)
XLA Modules:
  0.0 56.4 jit_solution(1952044500003098750)
XLA Ops:
  0.0 1.8 %states.4 = (f32[1024,128]{1,0:T(8,128)S(1)}, bf16[384,1024]{1,0:T(8,128)(2,1)S(1)}, bf16[384,1024]{1,0:T(8,128)(2,1)S(1)}) custom-call(bf16[384,4096]{1,0:T(8,128)(2,1)} %refs_0_.15, bf16[384,4096]{1,0:T(8,128)(2,1)} %refs_1_.7), custom_call_target="tpu_custom_call" | custom-call | flops 7000000000 | bytes 1 | tf_op jit(solution)/shard_map/states/pallas_call | solution.py:81
  1.8 0.5 collective-permute-start
  2.3 1.8 %states.5 = (f32[1024,128]{1,0:T(8,128)S(1)}, bf16[384,1024]{1,0:T(8,128)(2,1)S(1)}, bf16[384,1024]{1,0:T(8,128)(2,1)S(1)}) custom-call(bf16[384,4096]{1,0:T(8,128)(2,1)} %refs_0_.15, bf16[384,4096]{1,0:T(8,128)(2,1)} %refs_1_.7, f32[1024,128]{1,0:T(8,128)S(1)} %get-tuple-element.59.refs_2_), custom_call_target="tpu_custom_call" | custom-call | flops 7000000000 | bytes 1 | tf_op jit(solution)/shard_map/states/pallas_call | solution.py:81
  4.2 0.1 first_up.2
  4.3 2.7 %collective-permute-start.4 = (f32[256,128]{1,0:T(8,128)S(1)}, f32[256,128]{1,0:T(8,128)S(1)}, u32[]{:S(2)}, u32[]{:S(2)}) collective-permute-start(f32[256,128]{1,0:T(8,128)S(1)} %get-tuple-element.61.refs_2_), channel_id=1, source_target_pairs={{0,2},{1,3},{2,0},{3,1},{4,6},{5,7},{6,4},{7,5},{8,10},{9,11},{10,... | collective-permute-start | bytes 393224 | tf_op jit(solution)/shard_map/ppermute | solution.py:310
  7.0 1.8 %states.6 = (f32[1024,128]{1,0:T(8,128)S(1)}, bf16[384,1024]{1,0:T(8,128)(2,1)S(1)}, bf16[384,1024]{1,0:T(8,128)(2,1)S(1)}) custom-call(bf16[384,4096]{1,0:T(8,128)(2,1)} %refs_0_.15, bf16[384,4096]{1,0:T(8,128)(2,1)} %refs_1_.7, f32[256,128]{1,0:T(8,128)S(1)} %get-tuple-element.61.refs_2_), custom_call_target="tpu_custom_call" | custom-call | flops 7000000000 | bytes 1 | tf_op jit(solution)/shard_map/states/pallas_call | solution.py:81
  8.8 0.1 collective-permute-start.3
  8.9 0.2 collective-permute-start.1
  9.1 1.8 %states.7 = (f32[1024,128]{1,0:T(8,128)S(1)}, bf16[384,1024]{1,0:T(8,128)(2,1)S(1)}, bf16[384,1024]{1,0:T(8,128)(2,1)S(1)}) custom-call(bf16[384,4096]{1,0:T(8,128)(2,1)} %refs_0_.15, bf16[384,4096]{1,0:T(8,128)(2,1)} %refs_1_.7, f32[1024,128]{1,0:T(8,128)S(1)} %get-tuple-element.64.refs_2_), custom_call_target="tpu_custom_call" | custom-call | flops 7000000000 | bytes 1 | tf_op jit(solution)/shard_map/states/pallas_call | solution.py:81
  10.9 0.0 collective-permute-done.1.refs_1_
  10.9 0.1 first_up.3
  11.1 1.9 %collective-permute-start.6 = (f32[256,128]{1,0:T(8,128)S(1)}, f32[256,128]{1,0:T(8,128)S(1)}, u32[]{:S(2)}, u32[]{:S(2)}) collective-permute-start(f32[256,128]{1,0:T(8,128)S(1)} %get-tuple-element.71.refs_2_), channel_id=1, source_target_pairs={{0,2},{1,3},{2,0},{3,1},{4,6},{5,7},{6,4},{7,5},{8,10},{9,11},{10,... | collective-permute-start | bytes 393224 | tf_op jit(solution)/shard_map/ppermute | solution.py:310
  13.0 0.0 collective-permute-done.4.refs_1_
  13.0 2.7 %collective-permute-start.5 = (f32[256,128]{1,0:T(8,128)S(1)}, f32[256,128]{1,0:T(8,128)S(1)}, u32[]{:S(2)}, u32[]{:S(2)}) collective-permute-start(f32[256,128]{1,0:T(8,128)S(1)} %get-tuple-element.72.refs_2_), channel_id=1, source_target_pairs={{0,4},{1,5},{2,6},{3,7},{4,0},{5,1},{6,2},{7,3},{8,12},{9,13},{10,... | collective-permute-start | bytes 393224 | tf_op jit(solution)/shard_map/ppermute | solution.py:310
  15.7 0.4 collective-permute-start.2
  16.2 1.9 %copy-done = bf16[384,4096]{1,0:T(8,128)(2,1)S(1)} copy-done((bf16[384,4096]{1,0:T(8,128)(2,1)S(1)}, bf16[384,4096]{1,0:T(8,128)(2,1)}, u32[]{:S(2)}) %copy-start) | copy-done | bytes 3145752
  18.0 1.8 %local.4.refs_2_.refs_1_ = f32[384,1024]{1,0:T(8,128)S(1)} custom-call(bf16[384,4096]{1,0:T(8,128)(2,1)S(1)} %copy-done, bf16[384,1024]{1,0:T(8,128)(2,1)S(1)} %get-tuple-element.75.refs_1_, bf16[384,1024]{1,0:T(8,128)(2,1)S(1)} %get-tuple-element.76.refs_2_, f32[256,128]{1,0:T(8,128)S(1)} %get-tuple-element.73.refs_3_.refs_0_), custom_call_target="tpu_custom_call" | custom-call | flops 7000000000 | bytes 1 | tf_op jit(solution)/shard_map/local/pallas_call | solution.py:81
  19.8 0.3 collective-permute-done.6.refs_1_
  20.1 0.8 %collective-permute-start.7 = (f32[256,128]{1,0:T(8,128)S(1)}, f32[256,128]{1,0:T(8,128)S(1)}, u32[]{:S(2)}, u32[]{:S(2)}) collective-permute-start(f32[256,128]{1,0:T(8,128)S(1)} %get-tuple-element.77.refs_2_), channel_id=1, source_target_pairs={{0,4},{1,5},{2,6},{3,7},{4,0},{5,1},{6,2},{7,3},{8,12},{9,13},{10,... | collective-permute-start | bytes 393224 | tf_op jit(solution)/shard_map/ppermute | solution.py:310
  21.0 1.2 %collective-permute-done.5.refs_1_ = f32[256,128]{1,0:T(8,128)S(1)} collective-permute-done((f32[256,128]{1,0:T(8,128)S(1)}, f32[256,128]{1,0:T(8,128)S(1)}, u32[]{:S(2)}, u32[]{:S(2)}) %collective-permute-start.5) | collective-permute-done | bytes 131104 | tf_op jit(solution)/shard_map/ppermute | solution.py:310
  22.2 1.6 %collective-permute-start.8 = (f32[256,128]{1,0:T(8,128)S(1)}, f32[256,128]{1,0:T(8,128)S(1)}, u32[]{:S(2)}, u32[]{:S(2)}) collective-permute-start(f32[256,128]{1,0:T(8,128)S(1)} %get-tuple-element.78.refs_2_.refs_0_), channel_id=1, source_target_pairs={{0,8},{1,9},{2,10},{3,11},{4,12},{5,13},{6,14},{7,15},{8,0},{9,1},... | collective-permute-start | bytes 393224 | tf_op jit(solution)/shard_map/ppermute | solution.py:310
  23.8 0.0 collective-permute-done.2.refs_1_
  23.8 1.8 %local.5.refs_2_.refs_1_ = f32[384,1024]{1,0:T(8,128)S(1)} custom-call(bf16[384,4096]{1,0:T(8,128)(2,1)S(1)} %copy-done, bf16[384,1024]{1,0:T(8,128)(2,1)S(1)} %get-tuple-element.80.refs_1_, bf16[384,1024]{1,0:T(8,128)(2,1)S(1)} %get-tuple-element.81.refs_2_, f32[256,128]{1,0:T(8,128)S(1)} %get-tuple-element.79.refs_3_.refs_0_), custom_call_target="tpu_custom_call" | custom-call | flops 7000000000 | bytes 1 | tf_op jit(solution)/shard_map/local/pallas_call | solution.py:81
  25.7 1.6 %collective-permute-done.8.refs_1_ = f32[256,128]{1,0:T(8,128)S(1)} collective-permute-done((f32[256,128]{1,0:T(8,128)S(1)}, f32[256,128]{1,0:T(8,128)S(1)}, u32[]{:S(2)}, u32[]{:S(2)}) %collective-permute-start.8) | collective-permute-done | bytes 131104 | tf_op jit(solution)/shard_map/ppermute | solution.py:310
  27.3 1.6 %collective-permute-start.10 = (f32[256,128]{1,0:T(8,128)S(1)}, f32[256,128]{1,0:T(8,128)S(1)}, u32[]{:S(2)}, u32[]{:S(2)}) collective-permute-start(f32[256,128]{1,0:T(8,128)S(1)} %get-tuple-element.82.refs_2_), channel_id=1, source_target_pairs={{0,16},{1,17},{2,18},{3,19},{4,20},{5,21},{6,22},{7,23},{8,24},{9,... | collective-permute-start | bytes 393224 | tf_op jit(solution)/shard_map/ppermute | solution.py:310
  28.9 1.6 %collective-permute-start.9 = (f32[256,128]{1,0:T(8,128)S(1)}, f32[256,128]{1,0:T(8,128)S(1)}, u32[]{:S(2)}, u32[]{:S(2)}) collective-permute-start(f32[256,128]{1,0:T(8,128)S(1)} %get-tuple-element.83.refs_3_.refs_0_), channel_id=1, source_target_pairs={{0,16},{1,17},{2,18},{3,19},{4,20},{5,21},{6,22},{7,23},{8,24},{9,... | collective-permute-start | bytes 393224 | tf_op jit(solution)/shard_map/ppermute | solution.py:310
  30.5 1.8 %local.6.refs_3_.refs_1_ = f32[384,1024]{1,0:T(8,128)S(1)} custom-call(bf16[384,4096]{1,0:T(8,128)(2,1)S(1)} %copy-done, bf16[384,1024]{1,0:T(8,128)(2,1)S(1)} %get-tuple-element.86.refs_1_, bf16[384,1024]{1,0:T(8,128)(2,1)S(1)} %get-tuple-element.87.refs_2_, f32[256,128]{1,0:T(8,128)S(1)} %get-tuple-element.83.refs_3_.refs_0_), custom_call_target="tpu_custom_call" | custom-call | flops 7000000000 | bytes 1 | tf_op jit(solution)/shard_map/local/pallas_call | solution.py:81
  32.3 0.0 collective-permute-done.10.refs_0_
  32.4 1.7 %collective-permute-start.12 = (f32[256,128]{1,0:T(8,128)S(1)}, f32[256,128]{1,0:T(8,128)S(1)}, u32[]{:S(2)}, u32[]{:S(2)}) collective-permute-start(f32[256,128]{1,0:T(8,128)S(1)} %get-tuple-element.88.refs_2_), channel_id=1, source_target_pairs={{0,4},{1,5},{2,6},{3,7},{4,0},{5,1},{6,2},{7,3},{8,12},{9,13},{10,... | collective-permute-start | bytes 393224 | tf_op jit(solution)/shard_map/ppermute | solution.py:310
  34.1 1.5 %collective-permute-start.11 = (f32[256,128]{1,0:T(8,128)S(1)}, f32[256,128]{1,0:T(8,128)S(1)}, u32[]{:S(2)}, u32[]{:S(2)}) collective-permute-start(f32[256,128]{1,0:T(8,128)S(1)} %get-tuple-element.89.refs_2_), channel_id=1, source_target_pairs={{0,8},{1,9},{2,10},{3,11},{4,12},{5,13},{6,14},{7,15},{8,0},{9,1},... | collective-permute-start | bytes 393224 | tf_op jit(solution)/shard_map/ppermute | solution.py:310
  35.6 2.6 %collective-permute-start.16 = (f32[256,128]{1,0:T(8,128)S(1)}, f32[256,128]{1,0:T(8,128)S(1)}, u32[]{:S(2)}, u32[]{:S(2)}) collective-permute-start(f32[256,128]{1,0:T(8,128)S(1)} %get-tuple-element.94.refs_3_), channel_id=1, source_target_pairs={{0,2},{1,3},{2,0},{3,1},{4,6},{5,7},{6,4},{7,5},{8,10},{9,11},{10,... | collective-permute-start | bytes 393224 | tf_op jit(solution)/shard_map/ppermute | solution.py:310
  38.3 0.8 %collective-permute-done.11.refs_0_ = f32[256,128]{1,0:T(8,128)S(1)} collective-permute-done((f32[256,128]{1,0:T(8,128)S(1)}, f32[256,128]{1,0:T(8,128)S(1)}, u32[]{:S(2)}, u32[]{:S(2)}) %collective-permute-start.11) | collective-permute-done | bytes 131104 | tf_op jit(solution)/shard_map/ppermute | solution.py:310
  39.2 1.4 %collective-permute-start.13 = (f32[256,128]{1,0:T(8,128)S(1)}, f32[256,128]{1,0:T(8,128)S(1)}, u32[]{:S(2)}, u32[]{:S(2)}) collective-permute-start(f32[256,128]{1,0:T(8,128)S(1)} %get-tuple-element.98.refs_2_), channel_id=1, source_target_pairs={{0,4},{1,5},{2,6},{3,7},{4,0},{5,1},{6,2},{7,3},{8,12},{9,13},{10,... | collective-permute-start | bytes 393224 | tf_op jit(solution)/shard_map/ppermute | solution.py:310
  40.6 2.6 %collective-permute-start.17 = (f32[256,128]{1,0:T(8,128)S(1)}, f32[256,128]{1,0:T(8,128)S(1)}, u32[]{:S(2)}, u32[]{:S(2)}) collective-permute-start(f32[256,128]{1,0:T(8,128)S(1)} %get-tuple-element.99.refs_2_), channel_id=1, source_target_pairs={{0,2},{1,3},{2,0},{3,1},{4,6},{5,7},{6,4},{7,5},{8,10},{9,11},{10,... | collective-permute-start | bytes 393224 | tf_op jit(solution)/shard_map/ppermute | solution.py:310
  43.2 0.1 collective-permute-start.14
  43.3 1.8 %local.7.refs_1_ = f32[384,1024]{1,0:T(8,128)S(1)} custom-call(bf16[384,4096]{1,0:T(8,128)(2,1)S(1)} %copy-done, bf16[384,1024]{1,0:T(8,128)(2,1)S(1)} %get-tuple-element.62.refs_1_, bf16[384,1024]{1,0:T(8,128)(2,1)S(1)} %get-tuple-element.63.refs_2_, f32[256,128]{1,0:T(8,128)S(1)} %get-tuple-element.100.refs_3_), custom_call_target="tpu_custom_call" | custom-call | flops 7000000000 | bytes 1 | tf_op jit(solution)/shard_map/local/pallas_call | solution.py:81
  45.1 0.1 collective-permute-done.13.refs_0_
  45.2 3.9 %collective-permute-start.15 = (f32[256,128]{1,0:T(8,128)S(1)}, f32[256,128]{1,0:T(8,128)S(1)}, u32[]{:S(2)}, u32[]{:S(2)}) collective-permute-start(f32[256,128]{1,0:T(8,128)S(1)} %get-tuple-element.104.refs_5_), channel_id=1, source_target_pairs={{0,2},{1,3},{2,0},{3,1},{4,6},{5,7},{6,4},{7,5},{8,10},{9,11},{10,... | collective-permute-start | bytes 393224 | tf_op jit(solution)/shard_map/ppermute | solution.py:310
  49.2 0.2 last_down.2
  49.4 0.1 collective-permute-start.18
  49.4 1.4 %finish.4.refs_4_ = bf16[384,4096]{1,0:T(8,128)(2,1)} custom-call(bf16[384,4096]{1,0:T(8,128)(2,1)S(1)} %copy-done, f32[384,1024]{1,0:T(8,128)S(1)} %local.4.refs_2_.refs_1_, f32[1024,128]{1,0:T(8,128)S(1)} %get-tuple-element.110.refs_2_, f32[1,4096]{1,0:T(1,128)S(1)} %gain.1.refs_2_.refs_3_, f32[1024,128]{1,0:T(8,128)S(1)} %get-tuple-element.109.refs_4_), custom_call_target="tpu_custom_call" | custom-call | flops 7000000000 | bytes 1 | tf_op jit(solution)/shard_map/finish/pallas_call | solution.py:81
  50.9 0.4 collective-permute-done.18.refs_2_
  51.3 1.4 %finish.5.refs_5_.refs_4_ = bf16[384,4096]{1,0:T(8,128)(2,1)} custom-call(bf16[384,4096]{1,0:T(8,128)(2,1)S(1)} %copy-done, f32[384,1024]{1,0:T(8,128)S(1)} %local.5.refs_2_.refs_1_, f32[1024,128]{1,0:T(8,128)S(1)} %collective-permute-done.18.refs_2_, f32[1,4096]{1,0:T(1,128)S(1)} %gain.1.refs_2_.refs_3_, ...), custom_call_target="tpu_custom_call", output_to_operand_aliasing={{}: (4, {})} | custom-call | flops 7000000000 | bytes 1 | tf_op jit(solution)/shard_map/finish/pallas_call | solution.py:81
  52.8 0.2 last_down.3
  53.0 0.2 collective-permute-start.19
  53.2 1.4 %finish.6.refs_4_ = bf16[384,4096]{1,0:T(8,128)(2,1)} custom-call(bf16[384,4096]{1,0:T(8,128)(2,1)S(1)} %copy-done, f32[384,1024]{1,0:T(8,128)S(1)} %local.6.refs_3_.refs_1_, f32[1024,128]{1,0:T(8,128)S(1)} %get-tuple-element.112.refs_2_, f32[1,4096]{1,0:T(1,128)S(1)} %gain.1.refs_2_.refs_3_, ...), custom_call_target="tpu_custom_call", output_to_operand_aliasing={{}: (4, {})} | custom-call | flops 7000000000 | bytes 1 | tf_op jit(solution)/shard_map/finish/pallas_call | solution.py:81
  54.7 0.3 collective-permute-done.19.refs_2_
  55.0 1.4 %finish.7 = bf16[384,4096]{1,0:T(8,128)(2,1)} custom-call(bf16[384,4096]{1,0:T(8,128)(2,1)S(1)} %copy-done, f32[384,1024]{1,0:T(8,128)S(1)} %local.7.refs_1_, f32[1024,128]{1,0:T(8,128)S(1)} %collective-permute-done.19.refs_2_, f32[1,4096]{1,0:T(1,128)S(1)} %gain.1.refs_2_.refs_3_, bf16[384,4096]{1,0:T(8,128)(2,1)} %finish.6.refs_4_), custom_call_target="tpu_custom_call", output_to_operand_aliasing={{}: (4, {})} | custom-call | flops 7000000000 | bytes 1 | tf_op jit(solution)/shard_map/finish/pallas_call | solution.py:81
  (27 shorter events, 0.4 us)
Async XLA Ops:
  1.8 2.3 %collective-permute-start = (f32[1024,128]{1,0:T(8,128)S(1)}, f32[1024,128]{1,0:T(8,128)S(1)}, u32[]{:S(2)}, u32[]{:S(2)}) collective-permute-start(f32[1024,128]{1,0:T(8,128)S(1)} %get-tuple-element.59.refs_2_), channel_id=1, source_target_pairs={{0,1},{1,0},{2,3},{3,2},{4,5},{5,4},{6,7},{7,6},{8,9},{9,8},{10,11... | collective-permute-start | bytes 1572872 | tf_op jit(solution)/shard_map/ppermute | solution.py:310
  4.3 8.7 %collective-permute-start.4 = (f32[256,128]{1,0:T(8,128)S(1)}, f32[256,128]{1,0:T(8,128)S(1)}, u32[]{:S(2)}, u32[]{:S(2)}) collective-permute-start(f32[256,128]{1,0:T(8,128)S(1)} %get-tuple-element.61.refs_2_), channel_id=1, source_target_pairs={{0,2},{1,3},{2,0},{3,1},{4,6},{5,7},{6,4},{7,5},{8,10},{9,11},{10,... | collective-permute-start | bytes 393224 | tf_op jit(solution)/shard_map/ppermute | solution.py:310
  8.8 7.3 %collective-permute-start.3 = (f32[256,128]{1,0:T(8,128)S(1)}, f32[256,128]{1,0:T(8,128)S(1)}, u32[]{:S(2)}, u32[]{:S(2)}) collective-permute-start(f32[256,128]{1,0:T(8,128)S(1)} %get-tuple-element.69), channel_id=1, source_target_pairs={{0,2},{1,3},{2,0},{3,1},{4,6},{5,7},{6,4},{7,5},{8,10},{9,11},{10,... | collective-permute-start | bytes 393224 | tf_op jit(solution)/shard_map/ppermute | solution.py:310
  8.9 2.0 %collective-permute-start.1 = (f32[1024,128]{1,0:T(8,128)S(1)}, f32[1024,128]{1,0:T(8,128)S(1)}, u32[]{:S(2)}, u32[]{:S(2)}) collective-permute-start(f32[1024,128]{1,0:T(8,128)S(1)} %get-tuple-element.64.refs_2_), channel_id=1, source_target_pairs={{0,1},{1,0},{2,3},{3,2},{4,5},{5,4},{6,7},{7,6},{8,9},{9,8},{10,11... | collective-permute-start | bytes 1572872 | tf_op jit(solution)/shard_map/ppermute | solution.py:310
  11.1 9.0 %collective-permute-start.6 = (f32[256,128]{1,0:T(8,128)S(1)}, f32[256,128]{1,0:T(8,128)S(1)}, u32[]{:S(2)}, u32[]{:S(2)}) collective-permute-start(f32[256,128]{1,0:T(8,128)S(1)} %get-tuple-element.71.refs_2_), channel_id=1, source_target_pairs={{0,2},{1,3},{2,0},{3,1},{4,6},{5,7},{6,4},{7,5},{8,10},{9,11},{10,... | collective-permute-start | bytes 393224 | tf_op jit(solution)/shard_map/ppermute | solution.py:310
  13.0 9.2 %collective-permute-start.5 = (f32[256,128]{1,0:T(8,128)S(1)}, f32[256,128]{1,0:T(8,128)S(1)}, u32[]{:S(2)}, u32[]{:S(2)}) collective-permute-start(f32[256,128]{1,0:T(8,128)S(1)} %get-tuple-element.72.refs_2_), channel_id=1, source_target_pairs={{0,4},{1,5},{2,6},{3,7},{4,0},{5,1},{6,2},{7,3},{8,12},{9,13},{10,... | collective-permute-start | bytes 393224 | tf_op jit(solution)/shard_map/ppermute | solution.py:310
  15.7 8.1 %collective-permute-start.2 = (f32[256,128]{1,0:T(8,128)S(1)}, f32[256,128]{1,0:T(8,128)S(1)}, u32[]{:S(2)}, u32[]{:S(2)}) collective-permute-start(f32[256,128]{1,0:T(8,128)S(1)} %get-tuple-element.67), channel_id=1, source_target_pairs={{0,2},{1,3},{2,0},{3,1},{4,6},{5,7},{6,4},{7,5},{8,10},{9,11},{10,... | collective-permute-start | bytes 393224 | tf_op jit(solution)/shard_map/ppermute | solution.py:310
  16.2 1.9 %copy-start = (bf16[384,4096]{1,0:T(8,128)(2,1)S(1)}, bf16[384,4096]{1,0:T(8,128)(2,1)}, u32[]{:S(2)}) copy-start(bf16[384,4096]{1,0:T(8,128)(2,1)} %refs_0_.23) | copy-start | bytes 9437188
  20.1 8.7 %collective-permute-start.7 = (f32[256,128]{1,0:T(8,128)S(1)}, f32[256,128]{1,0:T(8,128)S(1)}, u32[]{:S(2)}, u32[]{:S(2)}) collective-permute-start(f32[256,128]{1,0:T(8,128)S(1)} %get-tuple-element.77.refs_2_), channel_id=1, source_target_pairs={{0,4},{1,5},{2,6},{3,7},{4,0},{5,1},{6,2},{7,3},{8,12},{9,13},{10,... | collective-permute-start | bytes 393224 | tf_op jit(solution)/shard_map/ppermute | solution.py:310
  22.2 5.0 %collective-permute-start.8 = (f32[256,128]{1,0:T(8,128)S(1)}, f32[256,128]{1,0:T(8,128)S(1)}, u32[]{:S(2)}, u32[]{:S(2)}) collective-permute-start(f32[256,128]{1,0:T(8,128)S(1)} %get-tuple-element.78.refs_2_.refs_0_), channel_id=1, source_target_pairs={{0,8},{1,9},{2,10},{3,11},{4,12},{5,13},{6,14},{7,15},{8,0},{9,1},... | collective-permute-start | bytes 393224 | tf_op jit(solution)/shard_map/ppermute | solution.py:310
  27.3 5.0 %collective-permute-start.10 = (f32[256,128]{1,0:T(8,128)S(1)}, f32[256,128]{1,0:T(8,128)S(1)}, u32[]{:S(2)}, u32[]{:S(2)}) collective-permute-start(f32[256,128]{1,0:T(8,128)S(1)} %get-tuple-element.82.refs_2_), channel_id=1, source_target_pairs={{0,16},{1,17},{2,18},{3,19},{4,20},{5,21},{6,22},{7,23},{8,24},{9,... | collective-permute-start | bytes 393224 | tf_op jit(solution)/shard_map/ppermute | solution.py:310
  28.9 5.1 %collective-permute-start.9 = (f32[256,128]{1,0:T(8,128)S(1)}, f32[256,128]{1,0:T(8,128)S(1)}, u32[]{:S(2)}, u32[]{:S(2)}) collective-permute-start(f32[256,128]{1,0:T(8,128)S(1)} %get-tuple-element.83.refs_3_.refs_0_), channel_id=1, source_target_pairs={{0,16},{1,17},{2,18},{3,19},{4,20},{5,21},{6,22},{7,23},{8,24},{9,... | collective-permute-start | bytes 393224 | tf_op jit(solution)/shard_map/ppermute | solution.py:310
  32.4 8.2 %collective-permute-start.12 = (f32[256,128]{1,0:T(8,128)S(1)}, f32[256,128]{1,0:T(8,128)S(1)}, u32[]{:S(2)}, u32[]{:S(2)}) collective-permute-start(f32[256,128]{1,0:T(8,128)S(1)} %get-tuple-element.88.refs_2_), channel_id=1, source_target_pairs={{0,4},{1,5},{2,6},{3,7},{4,0},{5,1},{6,2},{7,3},{8,12},{9,13},{10,... | collective-permute-start | bytes 393224 | tf_op jit(solution)/shard_map/ppermute | solution.py:310
  34.1 5.0 %collective-permute-start.11 = (f32[256,128]{1,0:T(8,128)S(1)}, f32[256,128]{1,0:T(8,128)S(1)}, u32[]{:S(2)}, u32[]{:S(2)}) collective-permute-start(f32[256,128]{1,0:T(8,128)S(1)} %get-tuple-element.89.refs_2_), channel_id=1, source_target_pairs={{0,8},{1,9},{2,10},{3,11},{4,12},{5,13},{6,14},{7,15},{8,0},{9,1},... | collective-permute-start | bytes 393224 | tf_op jit(solution)/shard_map/ppermute | solution.py:310
  35.6 13.5 %collective-permute-start.16 = (f32[256,128]{1,0:T(8,128)S(1)}, f32[256,128]{1,0:T(8,128)S(1)}, u32[]{:S(2)}, u32[]{:S(2)}) collective-permute-start(f32[256,128]{1,0:T(8,128)S(1)} %get-tuple-element.94.refs_3_), channel_id=1, source_target_pairs={{0,2},{1,3},{2,0},{3,1},{4,6},{5,7},{6,4},{7,5},{8,10},{9,11},{10,... | collective-permute-start | bytes 393224 | tf_op jit(solution)/shard_map/ppermute | solution.py:310
  39.2 6.0 %collective-permute-start.13 = (f32[256,128]{1,0:T(8,128)S(1)}, f32[256,128]{1,0:T(8,128)S(1)}, u32[]{:S(2)}, u32[]{:S(2)}) collective-permute-start(f32[256,128]{1,0:T(8,128)S(1)} %get-tuple-element.98.refs_2_), channel_id=1, source_target_pairs={{0,4},{1,5},{2,6},{3,7},{4,0},{5,1},{6,2},{7,3},{8,12},{9,13},{10,... | collective-permute-start | bytes 393224 | tf_op jit(solution)/shard_map/ppermute | solution.py:310
  40.6 8.6 %collective-permute-start.17 = (f32[256,128]{1,0:T(8,128)S(1)}, f32[256,128]{1,0:T(8,128)S(1)}, u32[]{:S(2)}, u32[]{:S(2)}) collective-permute-start(f32[256,128]{1,0:T(8,128)S(1)} %get-tuple-element.99.refs_2_), channel_id=1, source_target_pairs={{0,2},{1,3},{2,0},{3,1},{4,6},{5,7},{6,4},{7,5},{8,10},{9,11},{10,... | collective-permute-start | bytes 393224 | tf_op jit(solution)/shard_map/ppermute | solution.py:310
  43.2 9.6 %collective-permute-start.14 = (f32[256,128]{1,0:T(8,128)S(1)}, f32[256,128]{1,0:T(8,128)S(1)}, u32[]{:S(2)}, u32[]{:S(2)}) collective-permute-start(f32[256,128]{1,0:T(8,128)S(1)} %get-tuple-element.100.refs_3_), channel_id=1, source_target_pairs={{0,2},{1,3},{2,0},{3,1},{4,6},{5,7},{6,4},{7,5},{8,10},{9,11},{10,... | collective-permute-start | bytes 393224 | tf_op jit(solution)/shard_map/ppermute | solution.py:310
  43.3 1.8 %copy-start.1 = (f32[4096]{0:T(1024)S(1)}, f32[4096]{0:T(1024)}, u32[]{:S(2)}) copy-start(f32[4096]{0:T(1024)} %param.7) | copy-start | bytes 49156
  45.2 7.6 %collective-permute-start.15 = (f32[256,128]{1,0:T(8,128)S(1)}, f32[256,128]{1,0:T(8,128)S(1)}, u32[]{:S(2)}, u32[]{:S(2)}) collective-permute-start(f32[256,128]{1,0:T(8,128)S(1)} %get-tuple-element.104.refs_5_), channel_id=1, source_target_pairs={{0,2},{1,3},{2,0},{3,1},{4,6},{5,7},{6,4},{7,5},{8,10},{9,11},{10,... | collective-permute-start | bytes 393224 | tf_op jit(solution)/shard_map/ppermute | solution.py:310
  49.4 2.0 %collective-permute-start.18 = (f32[1024,128]{1,0:T(8,128)S(1)}, f32[1024,128]{1,0:T(8,128)S(1)}, u32[]{:S(2)}, u32[]{:S(2)}) collective-permute-start(f32[1024,128]{1,0:T(8,128)S(1)} %get-tuple-element.109.refs_4_), channel_id=1, source_target_pairs={{0,1},{1,0},{2,3},{3,2},{4,5},{5,4},{6,7},{7,6},{8,9},{9,8},{10,11... | collective-permute-start | bytes 1572872 | tf_op jit(solution)/shard_map/ppermute | solution.py:310
  53.0 2.0 %collective-permute-start.19 = (f32[1024,128]{1,0:T(8,128)S(1)}, f32[1024,128]{1,0:T(8,128)S(1)}, u32[]{:S(2)}, u32[]{:S(2)}) collective-permute-start(f32[1024,128]{1,0:T(8,128)S(1)} %get-tuple-element.111.refs_5_), channel_id=1, source_target_pairs={{0,1},{1,0},{2,3},{3,2},{4,5},{5,4},{6,7},{7,6},{8,9},{9,8},{10,11... | collective-permute-start | bytes 1572872 | tf_op jit(solution)/shard_map/ppermute | solution.py:310

commit v8 on v7

--- a/solution.py
+++ b/solution.py
@@ -14,6 +14,7 @@
 CHUNKS = 2
 HEADS = HALF // CHUNKS
 PIECE = 4
+OUT_PIECE = 2
 HINT = 7 * 10**9
 WIDTH = PIECE * E
 
@@ -181,18 +182,14 @@
     return vmem_call(kernel, "up", shapes, tie, keep, got)
 
 
-def group_kernel(bit, other, turned, total_ref, got_ref, before_ref, send_ref):
+def group_kernel(bit, total_ref, got_ref, before_ref, send_ref):
     total, got = total_ref[...], got_ref[...]
-    before = jnp.where(bit_of(bit) == 0, 0.0, got)
-    before_ref[...] = before
-    if turned:
-        send_ref[...] = before + jnp.where(bit_of(other) == 0, total, 0.0)
-    else:
-        send_ref[...] = total + got
-
-
-def go_along(bit, other, turned, total, got, tie):
-    kernel = functools.partial(group_kernel, bit, other, turned)
+    before_ref[...] = jnp.where(bit_of(bit) == 0, 0.0, got)
+    send_ref[...] = total + got
+
+
+def go_along(bit, total, got, tie):
+    kernel = functools.partial(group_kernel, bit)
     return vmem_call(kernel, "group", [total.shape] * 2, tie, total, got)
 
 
@@ -202,15 +199,13 @@
     send_ref[...] = before + jnp.where(lower, low, 0.0)
 
 
-def top_kernel(bit, turned, level, got_ref, low_ref, before_ref, own_ref, send_ref):
-    got = got_ref[...]
-    if not turned:
-        got = jnp.where(bit_of(bit) == 0, 0.0, got)
-    split(level, before_ref[...] + got, low_ref[...], own_ref, send_ref)
-
-
-def turn_down(bit, turned, level, got, low, before, tie):
-    kernel = functools.partial(top_kernel, bit, turned, level)
+def top_kernel(bit, level, got_ref, low_ref, before_ref, own_ref, send_ref):
+    before = before_ref[...] + jnp.where(bit_of(bit) == 0, 0.0, got_ref[...])
+    split(level, before, low_ref[...], own_ref, send_ref)
+
+
+def turn_down(bit, level, got, low, before, tie):
+    kernel = functools.partial(top_kernel, bit, level)
     return vmem_call(kernel, "top", [low.shape] * 2, tie, got, low, before)
 
 
@@ -259,9 +254,9 @@
     out_ref, buf, sems = rest[-3:]
     base = first_column(chunk, mine)
     stores = []
-    for piece in range(HEADS // PIECE):
-        for h in range(PIECE):
-            here = (piece * PIECE + h) * E
+    for piece in range(HEADS // OUT_PIECE):
+        for h in range(OUT_PIECE):
+            here = (piece * OUT_PIECE + h) * E
             cols = lane_tile(base + here, E)
             low = p_ref[here : here + E, :].astype(jnp.bfloat16)
             mixed = m_ref[:, here : here + E] + jnp.dot(
@@ -271,7 +266,7 @@
             normed = mixed * lax.rsqrt(meansq + 1e-6) * gain_ref[:, cols]
             buf[piece, :, h * E : (h + 1) * E] = normed.astype(jnp.bfloat16)
         copy = pltpu.make_async_copy(
-            buf.at[piece], out_ref.at[:, lane_tile(base + piece * WIDTH, WIDTH)], sems.at[piece]
+            buf.at[piece], out_ref.at[:, lane_tile(base + piece * OUT_PIECE * E, OUT_PIECE * E)], sems.at[piece]
         )
         copy.start()
         stores.append(copy)
@@ -280,7 +275,7 @@
 
 
 def finish(chunk, mine, shape, mixed, queries, prefix, gain, out, tie):
-    pieces = HEADS // PIECE
+    pieces = HEADS // OUT_PIECE
     arrays = [(queries, pltpu.VMEM), (mixed, pltpu.VMEM), (prefix, pltpu.VMEM), (gain, pltpu.VMEM)]
     if out is not None:
         arrays.append((out, pltpu.HBM))
@@ -290,7 +285,7 @@
         arrays,
         [(pltpu.HBM, shape, jnp.bfloat16)],
         [
-            pltpu.VMEM((pieces, shape[0], WIDTH), jnp.bfloat16),
+            pltpu.VMEM((pieces, shape[0], OUT_PIECE * E), jnp.bfloat16),
             pltpu.SemaphoreType.DMA((pieces,)),
         ],
         tie,
@@ -323,13 +318,10 @@
             this = todo.pop(0)
             mixed[this] = after(local_mix(*this, queries, *columns[this], latest))
 
-    order = [(levels, levels + 1), (levels + 1, levels)]
-
     def up(level, c):
         halve = level < levels - 1
         low[c][level], keep[c], *send = go_up(level, halve, keep[c], got[c], latest)
-        along = level + 1 if halve else order[c % 2][0]
-        got[c] = swap(after(send[0] if halve else keep[c]), along)
+        got[c] = swap(after(send[0] if halve else keep[c]), level + 1)
 
     keep, got, before = [None] * CHUNKS, [None] * CHUNKS, [None] * CHUNKS
     low = [[None] * levels for _ in chunks]
@@ -353,13 +345,11 @@
         after(keep[c])
 
     def along(c):
-        bit, other = order[c % 2]
-        before[c], send = go_along(bit, other, c % 2 == 1, keep[c], got[c], latest)
-        got[c] = swap(after(send), other)
+        before[c], send = go_along(levels, keep[c], got[c], latest)
+        got[c] = swap(after(send), levels + 1)
 
     def turn(c):
-        bit, turned = order[0][1], c % 2 == 1
-        keep[c], send = turn_down(bit, turned, top, got[c], low[c][top], before[c], latest)
+        keep[c], send = turn_down(levels + 1, top, got[c], low[c][top], before[c], latest)
         got[c] = swap(after(send), top)
 
     def part(c, n):
@@ -401,11 +391,14 @@
     while todo:
         some_local()
     gain = after(vmem_call(copy_kernel, "gain", [gain.shape], latest, gain)[0])
+    def last(c):
+        keep[c], send = last_down(part_keep[c], part_got[c], low[c][0], latest)
+        got[c] = swap(after(send), 0)
+
     part(1, 1)
     out = None
     for c in chunks:
-        keep[c], send = last_down(part_keep[c], part_got[c], low[c][0], latest)
-        got[c] = swap(after(send), 0)
+        last(c)
         for mine, prefix in ((True, keep[c]), (False, got[c])):
             out = finish(c, mine, queries.shape, mixed[c, mine], queries, prefix, gain, out, latest)
             latest[:] = []

time: 56.7 us -> 55.8 us (0.984)
  starting transfers between devices: 28.2 us -> 25.8 us
  waiting for transfers between devices: 4.91 us -> 6.66 us
    ppermute x20, starting transfers between devices: 28.2 us -> 25.8 us  [swap(): return lax.ppermute(x, AXES, [(i, i ^ 1 << level) for i in range(devices)])]
    ppermute x20, waiting for transfers between devices: 4.91 us -> 6.66 us  [swap(): return lax.ppermute(x, AXES, [(i, i ^ 1 << level) for i in range(devices)])]
  transfers between devices with their start and end apart: 20 -> 20, of which waited for: 7 -> 8; matrix products, arithmetic and copies ran while one was open for 0% -> 0% of each run, Pallas kernels for 31% -> 31%
where the time goes in v8:
time: 55.8 us; the launch traced here: 55.6 us
  starting transfers between devices  25.8 us (46%)
  Pallas kernels  21 us (38%)
  waiting for transfers between devices  6.66 us (12%)
  local copies, waits for them, and re-layouts  1.87 us (3%)
    ppermute x20, starting transfers between devices, swap(): return lax.ppermute(x, AXES, [(i, i ^ 1 << level) for i in range(devices)])  25.8 us
    pallas_call x31, Pallas kernels, call(): pl.pallas_call(body, in_specs=[pl.BlockSpec(memory_space=space) for _, sp...  21 us
    ppermute x20, waiting for transfers between devices, swap(): return lax.ppermute(x, AXES, [(i, i ^ 1 << level) for i in range(devices)])  6.66 us
    unnamed x4, local copies, waits for them, and re-layouts  1.87 us
  transfers between devices with their start and end apart: 20, of which 8 were waited for; matrix products, arithmetic and copies ran while one was open for 0% of the time, Pallas kernels for 31%

profile of v8, /device:TPU:0, one launch (start us, length us, event | category | flops | bytes accessed | tf_op | source)
XLA Modules:
  0.0 55.6 jit_solution(7997054229783443117)
XLA Ops:
  0.0 1.8 %states.4 = (f32[1024,128]{1,0:T(8,128)S(1)}, bf16[384,1024]{1,0:T(8,128)(2,1)S(1)}, bf16[384,1024]{1,0:T(8,128)(2,1)S(1)}) custom-call(bf16[384,4096]{1,0:T(8,128)(2,1)} %refs_0_.15, bf16[384,4096]{1,0:T(8,128)(2,1)} %refs_1_.7), custom_call_target="tpu_custom_call" | custom-call | flops 7000000000 | bytes 1 | tf_op jit(solution)/shard_map/states/pallas_call | solution.py:82
  1.8 0.5 collective-permute-start
  2.3 1.8 %states.5 = (f32[1024,128]{1,0:T(8,128)S(1)}, bf16[384,1024]{1,0:T(8,128)(2,1)S(1)}, bf16[384,1024]{1,0:T(8,128)(2,1)S(1)}) custom-call(bf16[384,4096]{1,0:T(8,128)(2,1)} %refs_0_.15, bf16[384,4096]{1,0:T(8,128)(2,1)} %refs_1_.7, f32[1024,128]{1,0:T(8,128)S(1)} %get-tuple-element.59.refs_2_), custom_call_target="tpu_custom_call" | custom-call | flops 7000000000 | bytes 1 | tf_op jit(solution)/shard_map/states/pallas_call | solution.py:82
  4.1 0.0 collective-permute-done.refs_1_
  4.2 0.1 first_up.2
  4.3 2.7 %collective-permute-start.4 = (f32[256,128]{1,0:T(8,128)S(1)}, f32[256,128]{1,0:T(8,128)S(1)}, u32[]{:S(2)}, u32[]{:S(2)}) collective-permute-start(f32[256,128]{1,0:T(8,128)S(1)} %get-tuple-element.61.refs_2_), channel_id=1, source_target_pairs={{0,2},{1,3},{2,0},{3,1},{4,6},{5,7},{6,4},{7,5},{8,10},{9,11},{10,... | collective-permute-start | bytes 393224 | tf_op jit(solution)/shard_map/ppermute | solution.py:305
  7.0 1.8 %states.6 = (f32[1024,128]{1,0:T(8,128)S(1)}, bf16[384,1024]{1,0:T(8,128)(2,1)S(1)}, bf16[384,1024]{1,0:T(8,128)(2,1)S(1)}) custom-call(bf16[384,4096]{1,0:T(8,128)(2,1)} %refs_0_.15, bf16[384,4096]{1,0:T(8,128)(2,1)} %refs_1_.7, f32[256,128]{1,0:T(8,128)S(1)} %get-tuple-element.61.refs_2_), custom_call_target="tpu_custom_call" | custom-call | flops 7000000000 | bytes 1 | tf_op jit(solution)/shard_map/states/pallas_call | solution.py:82
  8.8 0.1 collective-permute-start.3
  8.9 0.2 collective-permute-start.1
  9.1 1.8 %states.7 = (f32[1024,128]{1,0:T(8,128)S(1)}, bf16[384,1024]{1,0:T(8,128)(2,1)S(1)}, bf16[384,1024]{1,0:T(8,128)(2,1)S(1)}) custom-call(bf16[384,4096]{1,0:T(8,128)(2,1)} %refs_0_.15, bf16[384,4096]{1,0:T(8,128)(2,1)} %refs_1_.7, f32[1024,128]{1,0:T(8,128)S(1)} %get-tuple-element.64.refs_2_), custom_call_target="tpu_custom_call" | custom-call | flops 7000000000 | bytes 1 | tf_op jit(solution)/shard_map/states/pallas_call | solution.py:82
  10.9 0.1 first_up.3
  11.1 1.9 %collective-permute-start.6 = (f32[256,128]{1,0:T(8,128)S(1)}, f32[256,128]{1,0:T(8,128)S(1)}, u32[]{:S(2)}, u32[]{:S(2)}) collective-permute-start(f32[256,128]{1,0:T(8,128)S(1)} %get-tuple-element.71.refs_2_), channel_id=1, source_target_pairs={{0,2},{1,3},{2,0},{3,1},{4,6},{5,7},{6,4},{7,5},{8,10},{9,11},{10,... | collective-permute-start | bytes 393224 | tf_op jit(solution)/shard_map/ppermute | solution.py:305
  13.0 0.0 collective-permute-done.4.refs_1_
  13.0 2.7 %collective-permute-start.5 = (f32[256,128]{1,0:T(8,128)S(1)}, f32[256,128]{1,0:T(8,128)S(1)}, u32[]{:S(2)}, u32[]{:S(2)}) collective-permute-start(f32[256,128]{1,0:T(8,128)S(1)} %get-tuple-element.72.refs_2_), channel_id=1, source_target_pairs={{0,4},{1,5},{2,6},{3,7},{4,0},{5,1},{6,2},{7,3},{8,12},{9,13},{10,... | collective-permute-start | bytes 393224 | tf_op jit(solution)/shard_map/ppermute | solution.py:305
  15.7 0.4 collective-permute-start.2
  16.2 1.9 %copy-done = bf16[384,4096]{1,0:T(8,128)(2,1)S(1)} copy-done((bf16[384,4096]{1,0:T(8,128)(2,1)S(1)}, bf16[384,4096]{1,0:T(8,128)(2,1)}, u32[]{:S(2)}) %copy-start) | copy-done | bytes 3145752
  18.0 1.8 %local.4.refs_2_.refs_1_ = f32[384,1024]{1,0:T(8,128)S(1)} custom-call(bf16[384,4096]{1,0:T(8,128)(2,1)S(1)} %copy-done, bf16[384,1024]{1,0:T(8,128)(2,1)S(1)} %get-tuple-element.75.refs_1_, bf16[384,1024]{1,0:T(8,128)(2,1)S(1)} %get-tuple-element.76.refs_2_, f32[256,128]{1,0:T(8,128)S(1)} %get-tuple-element.73.refs_3_.refs_0_), custom_call_target="tpu_custom_call" | custom-call | flops 7000000000 | bytes 1 | tf_op jit(solution)/shard_map/local/pallas_call | solution.py:82
  19.8 0.3 collective-permute-done.6.refs_1_
  20.1 0.8 %collective-permute-start.7 = (f32[256,128]{1,0:T(8,128)S(1)}, f32[256,128]{1,0:T(8,128)S(1)}, u32[]{:S(2)}, u32[]{:S(2)}) collective-permute-start(f32[256,128]{1,0:T(8,128)S(1)} %get-tuple-element.77.refs_2_), channel_id=1, source_target_pairs={{0,4},{1,5},{2,6},{3,7},{4,0},{5,1},{6,2},{7,3},{8,12},{9,13},{10,... | collective-permute-start | bytes 393224 | tf_op jit(solution)/shard_map/ppermute | solution.py:305
  21.0 1.2 %collective-permute-done.5.refs_1_ = f32[256,128]{1,0:T(8,128)S(1)} collective-permute-done((f32[256,128]{1,0:T(8,128)S(1)}, f32[256,128]{1,0:T(8,128)S(1)}, u32[]{:S(2)}, u32[]{:S(2)}) %collective-permute-start.5) | collective-permute-done | bytes 131104 | tf_op jit(solution)/shard_map/ppermute | solution.py:305
  22.2 1.6 %collective-permute-start.8 = (f32[256,128]{1,0:T(8,128)S(1)}, f32[256,128]{1,0:T(8,128)S(1)}, u32[]{:S(2)}, u32[]{:S(2)}) collective-permute-start(f32[256,128]{1,0:T(8,128)S(1)} %get-tuple-element.78.refs_2_.refs_0_), channel_id=1, source_target_pairs={{0,8},{1,9},{2,10},{3,11},{4,12},{5,13},{6,14},{7,15},{8,0},{9,1},... | collective-permute-start | bytes 393224 | tf_op jit(solution)/shard_map/ppermute | solution.py:305
  23.8 1.8 %local.5.refs_2_.refs_1_ = f32[384,1024]{1,0:T(8,128)S(1)} custom-call(bf16[384,4096]{1,0:T(8,128)(2,1)S(1)} %copy-done, bf16[384,1024]{1,0:T(8,128)(2,1)S(1)} %get-tuple-element.80.refs_1_, bf16[384,1024]{1,0:T(8,128)(2,1)S(1)} %get-tuple-element.81.refs_2_, f32[256,128]{1,0:T(8,128)S(1)} %get-tuple-element.79.refs_3_.refs_0_), custom_call_target="tpu_custom_call" | custom-call | flops 7000000000 | bytes 1 | tf_op jit(solution)/shard_map/local/pallas_call | solution.py:82
  25.7 1.6 %collective-permute-done.8.refs_1_ = f32[256,128]{1,0:T(8,128)S(1)} collective-permute-done((f32[256,128]{1,0:T(8,128)S(1)}, f32[256,128]{1,0:T(8,128)S(1)}, u32[]{:S(2)}, u32[]{:S(2)}) %collective-permute-start.8) | collective-permute-done | bytes 131104 | tf_op jit(solution)/shard_map/ppermute | solution.py:305
  27.3 1.6 %collective-permute-start.10 = (f32[256,128]{1,0:T(8,128)S(1)}, f32[256,128]{1,0:T(8,128)S(1)}, u32[]{:S(2)}, u32[]{:S(2)}) collective-permute-start(f32[256,128]{1,0:T(8,128)S(1)} %get-tuple-element.82.refs_2_), channel_id=1, source_target_pairs={{0,16},{1,17},{2,18},{3,19},{4,20},{5,21},{6,22},{7,23},{8,24},{9,... | collective-permute-start | bytes 393224 | tf_op jit(solution)/shard_map/ppermute | solution.py:305
  28.9 1.6 %collective-permute-start.9 = (f32[256,128]{1,0:T(8,128)S(1)}, f32[256,128]{1,0:T(8,128)S(1)}, u32[]{:S(2)}, u32[]{:S(2)}) collective-permute-start(f32[256,128]{1,0:T(8,128)S(1)} %get-tuple-element.83.refs_3_.refs_0_), channel_id=1, source_target_pairs={{0,8},{1,9},{2,10},{3,11},{4,12},{5,13},{6,14},{7,15},{8,0},{9,1},... | collective-permute-start | bytes 393224 | tf_op jit(solution)/shard_map/ppermute | solution.py:305
  30.5 1.8 %local.6.refs_3_.refs_1_ = f32[384,1024]{1,0:T(8,128)S(1)} custom-call(bf16[384,4096]{1,0:T(8,128)(2,1)S(1)} %copy-done, bf16[384,1024]{1,0:T(8,128)(2,1)S(1)} %get-tuple-element.86.refs_1_, bf16[384,1024]{1,0:T(8,128)(2,1)S(1)} %get-tuple-element.87.refs_2_, f32[256,128]{1,0:T(8,128)S(1)} %get-tuple-element.83.refs_3_.refs_0_), custom_call_target="tpu_custom_call" | custom-call | flops 7000000000 | bytes 1 | tf_op jit(solution)/shard_map/local/pallas_call | solution.py:82
  32.3 0.0 collective-permute-done.10.refs_0_
  32.4 1.0 %collective-permute-start.12 = (f32[256,128]{1,0:T(8,128)S(1)}, f32[256,128]{1,0:T(8,128)S(1)}, u32[]{:S(2)}, u32[]{:S(2)}) collective-permute-start(f32[256,128]{1,0:T(8,128)S(1)} %get-tuple-element.88.refs_2_), channel_id=1, source_target_pairs={{0,4},{1,5},{2,6},{3,7},{4,0},{5,1},{6,2},{7,3},{8,12},{9,13},{10,... | collective-permute-start | bytes 393224 | tf_op jit(solution)/shard_map/ppermute | solution.py:305
  33.4 0.6 %collective-permute-done.9.refs_1_ = f32[256,128]{1,0:T(8,128)S(1)} collective-permute-done((f32[256,128]{1,0:T(8,128)S(1)}, f32[256,128]{1,0:T(8,128)S(1)}, u32[]{:S(2)}, u32[]{:S(2)}) %collective-permute-start.9) | collective-permute-done | bytes 131104 | tf_op jit(solution)/shard_map/ppermute | solution.py:305
  34.0 1.6 %collective-permute-start.11 = (f32[256,128]{1,0:T(8,128)S(1)}, f32[256,128]{1,0:T(8,128)S(1)}, u32[]{:S(2)}, u32[]{:S(2)}) collective-permute-start(f32[256,128]{1,0:T(8,128)S(1)} %get-tuple-element.89.refs_2_), channel_id=1, source_target_pairs={{0,16},{1,17},{2,18},{3,19},{4,20},{5,21},{6,22},{7,23},{8,24},{9,... | collective-permute-start | bytes 393224 | tf_op jit(solution)/shard_map/ppermute | solution.py:305
  35.6 1.9 %collective-permute-start.16 = (f32[256,128]{1,0:T(8,128)S(1)}, f32[256,128]{1,0:T(8,128)S(1)}, u32[]{:S(2)}, u32[]{:S(2)}) collective-permute-start(f32[256,128]{1,0:T(8,128)S(1)} %get-tuple-element.94.refs_3_), channel_id=1, source_target_pairs={{0,2},{1,3},{2,0},{3,1},{4,6},{5,7},{6,4},{7,5},{8,10},{9,11},{10,... | collective-permute-start | bytes 393224 | tf_op jit(solution)/shard_map/ppermute | solution.py:305
  37.5 1.5 %collective-permute-done.11.refs_0_ = f32[256,128]{1,0:T(8,128)S(1)} collective-permute-done((f32[256,128]{1,0:T(8,128)S(1)}, f32[256,128]{1,0:T(8,128)S(1)}, u32[]{:S(2)}, u32[]{:S(2)}) %collective-permute-start.11) | collective-permute-done | bytes 131104 | tf_op jit(solution)/shard_map/ppermute | solution.py:305
  39.1 1.5 %collective-permute-start.13 = (f32[256,128]{1,0:T(8,128)S(1)}, f32[256,128]{1,0:T(8,128)S(1)}, u32[]{:S(2)}, u32[]{:S(2)}) collective-permute-start(f32[256,128]{1,0:T(8,128)S(1)} %get-tuple-element.98.refs_2_), channel_id=1, source_target_pairs={{0,4},{1,5},{2,6},{3,7},{4,0},{5,1},{6,2},{7,3},{8,12},{9,13},{10,... | collective-permute-start | bytes 393224 | tf_op jit(solution)/shard_map/ppermute | solution.py:305
  40.6 2.0 %collective-permute-start.17 = (f32[256,128]{1,0:T(8,128)S(1)}, f32[256,128]{1,0:T(8,128)S(1)}, u32[]{:S(2)}, u32[]{:S(2)}) collective-permute-start(f32[256,128]{1,0:T(8,128)S(1)} %get-tuple-element.99.refs_2_), channel_id=1, source_target_pairs={{0,2},{1,3},{2,0},{3,1},{4,6},{5,7},{6,4},{7,5},{8,10},{9,11},{10,... | collective-permute-start | bytes 393224 | tf_op jit(solution)/shard_map/ppermute | solution.py:305
  42.6 0.1 collective-permute-start.14
  42.8 1.8 %local.7.refs_1_ = f32[384,1024]{1,0:T(8,128)S(1)} custom-call(bf16[384,4096]{1,0:T(8,128)(2,1)S(1)} %copy-done, bf16[384,1024]{1,0:T(8,128)(2,1)S(1)} %get-tuple-element.62.refs_1_, bf16[384,1024]{1,0:T(8,128)(2,1)S(1)} %get-tuple-element.63.refs_2_, f32[256,128]{1,0:T(8,128)S(1)} %get-tuple-element.100.refs_3_), custom_call_target="tpu_custom_call" | custom-call | flops 7000000000 | bytes 1 | tf_op jit(solution)/shard_map/local/pallas_call | solution.py:82
  44.6 0.5 collective-permute-done.13.refs_0_
  45.2 3.2 %collective-permute-start.15 = (f32[256,128]{1,0:T(8,128)S(1)}, f32[256,128]{1,0:T(8,128)S(1)}, u32[]{:S(2)}, u32[]{:S(2)}) collective-permute-start(f32[256,128]{1,0:T(8,128)S(1)} %get-tuple-element.104.refs_5_), channel_id=1, source_target_pairs={{0,2},{1,3},{2,0},{3,1},{4,6},{5,7},{6,4},{7,5},{8,10},{9,11},{10,... | collective-permute-start | bytes 393224 | tf_op jit(solution)/shard_map/ppermute | solution.py:305
  48.4 0.2 last_down.2
  48.6 0.1 collective-permute-start.18
  48.7 1.4 %finish.4.refs_4_ = bf16[384,4096]{1,0:T(8,128)(2,1)} custom-call(bf16[384,4096]{1,0:T(8,128)(2,1)S(1)} %copy-done, f32[384,1024]{1,0:T(8,128)S(1)} %local.4.refs_2_.refs_1_, f32[1024,128]{1,0:T(8,128)S(1)} %get-tuple-element.110.refs_2_, f32[1,4096]{1,0:T(1,128)S(1)} %gain.1.refs_2_.refs_3_, f32[1024,128]{1,0:T(8,128)S(1)} %get-tuple-element.109.refs_4_), custom_call_target="tpu_custom_call" | custom-call | flops 7000000000 | bytes 1 | tf_op jit(solution)/shard_map/finish/pallas_call | solution.py:82
  50.1 0.5 collective-permute-done.18.refs_2_
  50.6 1.4 %finish.5.refs_5_.refs_4_ = bf16[384,4096]{1,0:T(8,128)(2,1)} custom-call(bf16[384,4096]{1,0:T(8,128)(2,1)S(1)} %copy-done, f32[384,1024]{1,0:T(8,128)S(1)} %local.5.refs_2_.refs_1_, f32[1024,128]{1,0:T(8,128)S(1)} %collective-permute-done.18.refs_2_, f32[1,4096]{1,0:T(1,128)S(1)} %gain.1.refs_2_.refs_3_, ...), custom_call_target="tpu_custom_call", output_to_operand_aliasing={{}: (4, {})} | custom-call | flops 7000000000 | bytes 1 | tf_op jit(solution)/shard_map/finish/pallas_call | solution.py:82
  52.0 0.2 last_down.3
  52.2 0.2 collective-permute-start.19
  52.4 1.4 %finish.6.refs_4_ = bf16[384,4096]{1,0:T(8,128)(2,1)} custom-call(bf16[384,4096]{1,0:T(8,128)(2,1)S(1)} %copy-done, f32[384,1024]{1,0:T(8,128)S(1)} %local.6.refs_3_.refs_1_, f32[1024,128]{1,0:T(8,128)S(1)} %get-tuple-element.112.refs_2_, f32[1,4096]{1,0:T(1,128)S(1)} %gain.1.refs_2_.refs_3_, ...), custom_call_target="tpu_custom_call", output_to_operand_aliasing={{}: (4, {})} | custom-call | flops 7000000000 | bytes 1 | tf_op jit(solution)/shard_map/finish/pallas_call | solution.py:82
  53.8 0.4 collective-permute-done.19.refs_2_
  54.2 1.4 %finish.7 = bf16[384,4096]{1,0:T(8,128)(2,1)} custom-call(bf16[384,4096]{1,0:T(8,128)(2,1)S(1)} %copy-done, f32[384,1024]{1,0:T(8,128)S(1)} %local.7.refs_1_, f32[1024,128]{1,0:T(8,128)S(1)} %collective-permute-done.19.refs_2_, f32[1,4096]{1,0:T(1,128)S(1)} %gain.1.refs_2_.refs_3_, bf16[384,4096]{1,0:T(8,128)(2,1)} %finish.6.refs_4_), custom_call_target="tpu_custom_call", output_to_operand_aliasing={{}: (4, {})} | custom-call | flops 7000000000 | bytes 1 | tf_op jit(solution)/shard_map/finish/pallas_call | solution.py:82
  (27 shorter events, 0.4 us)
Async XLA Ops:
  1.8 2.3 %collective-permute-start = (f32[1024,128]{1,0:T(8,128)S(1)}, f32[1024,128]{1,0:T(8,128)S(1)}, u32[]{:S(2)}, u32[]{:S(2)}) collective-permute-start(f32[1024,128]{1,0:T(8,128)S(1)} %get-tuple-element.59.refs_2_), channel_id=1, source_target_pairs={{0,1},{1,0},{2,3},{3,2},{4,5},{5,4},{6,7},{7,6},{8,9},{9,8},{10,11... | collective-permute-start | bytes 1572872 | tf_op jit(solution)/shard_map/ppermute | solution.py:305
  4.3 8.7 %collective-permute-start.4 = (f32[256,128]{1,0:T(8,128)S(1)}, f32[256,128]{1,0:T(8,128)S(1)}, u32[]{:S(2)}, u32[]{:S(2)}) collective-permute-start(f32[256,128]{1,0:T(8,128)S(1)} %get-tuple-element.61.refs_2_), channel_id=1, source_target_pairs={{0,2},{1,3},{2,0},{3,1},{4,6},{5,7},{6,4},{7,5},{8,10},{9,11},{10,... | collective-permute-start | bytes 393224 | tf_op jit(solution)/shard_map/ppermute | solution.py:305
  8.8 7.3 %collective-permute-start.3 = (f32[256,128]{1,0:T(8,128)S(1)}, f32[256,128]{1,0:T(8,128)S(1)}, u32[]{:S(2)}, u32[]{:S(2)}) collective-permute-start(f32[256,128]{1,0:T(8,128)S(1)} %get-tuple-element.69), channel_id=1, source_target_pairs={{0,2},{1,3},{2,0},{3,1},{4,6},{5,7},{6,4},{7,5},{8,10},{9,11},{10,... | collective-permute-start | bytes 393224 | tf_op jit(solution)/shard_map/ppermute | solution.py:305
  8.9 2.0 %collective-permute-start.1 = (f32[1024,128]{1,0:T(8,128)S(1)}, f32[1024,128]{1,0:T(8,128)S(1)}, u32[]{:S(2)}, u32[]{:S(2)}) collective-permute-start(f32[1024,128]{1,0:T(8,128)S(1)} %get-tuple-element.64.refs_2_), channel_id=1, source_target_pairs={{0,1},{1,0},{2,3},{3,2},{4,5},{5,4},{6,7},{7,6},{8,9},{9,8},{10,11... | collective-permute-start | bytes 1572872 | tf_op jit(solution)/shard_map/ppermute | solution.py:305
  11.1 9.0 %collective-permute-start.6 = (f32[256,128]{1,0:T(8,128)S(1)}, f32[256,128]{1,0:T(8,128)S(1)}, u32[]{:S(2)}, u32[]{:S(2)}) collective-permute-start(f32[256,128]{1,0:T(8,128)S(1)} %get-tuple-element.71.refs_2_), channel_id=1, source_target_pairs={{0,2},{1,3},{2,0},{3,1},{4,6},{5,7},{6,4},{7,5},{8,10},{9,11},{10,... | collective-permute-start | bytes 393224 | tf_op jit(solution)/shard_map/ppermute | solution.py:305
  13.0 9.2 %collective-permute-start.5 = (f32[256,128]{1,0:T(8,128)S(1)}, f32[256,128]{1,0:T(8,128)S(1)}, u32[]{:S(2)}, u32[]{:S(2)}) collective-permute-start(f32[256,128]{1,0:T(8,128)S(1)} %get-tuple-element.72.refs_2_), channel_id=1, source_target_pairs={{0,4},{1,5},{2,6},{3,7},{4,0},{5,1},{6,2},{7,3},{8,12},{9,13},{10,... | collective-permute-start | bytes 393224 | tf_op jit(solution)/shard_map/ppermute | solution.py:305
  15.7 8.1 %collective-permute-start.2 = (f32[256,128]{1,0:T(8,128)S(1)}, f32[256,128]{1,0:T(8,128)S(1)}, u32[]{:S(2)}, u32[]{:S(2)}) collective-permute-start(f32[256,128]{1,0:T(8,128)S(1)} %get-tuple-element.67), channel_id=1, source_target_pairs={{0,2},{1,3},{2,0},{3,1},{4,6},{5,7},{6,4},{7,5},{8,10},{9,11},{10,... | collective-permute-start | bytes 393224 | tf_op jit(solution)/shard_map/ppermute | solution.py:305
  16.2 1.9 %copy-start = (bf16[384,4096]{1,0:T(8,128)(2,1)S(1)}, bf16[384,4096]{1,0:T(8,128)(2,1)}, u32[]{:S(2)}) copy-start(bf16[384,4096]{1,0:T(8,128)(2,1)} %refs_0_.23) | copy-start | bytes 9437188
  20.1 8.7 %collective-permute-start.7 = (f32[256,128]{1,0:T(8,128)S(1)}, f32[256,128]{1,0:T(8,128)S(1)}, u32[]{:S(2)}, u32[]{:S(2)}) collective-permute-start(f32[256,128]{1,0:T(8,128)S(1)} %get-tuple-element.77.refs_2_), channel_id=1, source_target_pairs={{0,4},{1,5},{2,6},{3,7},{4,0},{5,1},{6,2},{7,3},{8,12},{9,13},{10,... | collective-permute-start | bytes 393224 | tf_op jit(solution)/shard_map/ppermute | solution.py:305
  22.2 5.0 %collective-permute-start.8 = (f32[256,128]{1,0:T(8,128)S(1)}, f32[256,128]{1,0:T(8,128)S(1)}, u32[]{:S(2)}, u32[]{:S(2)}) collective-permute-start(f32[256,128]{1,0:T(8,128)S(1)} %get-tuple-element.78.refs_2_.refs_0_), channel_id=1, source_target_pairs={{0,8},{1,9},{2,10},{3,11},{4,12},{5,13},{6,14},{7,15},{8,0},{9,1},... | collective-permute-start | bytes 393224 | tf_op jit(solution)/shard_map/ppermute | solution.py:305
  27.3 5.0 %collective-permute-start.10 = (f32[256,128]{1,0:T(8,128)S(1)}, f32[256,128]{1,0:T(8,128)S(1)}, u32[]{:S(2)}, u32[]{:S(2)}) collective-permute-start(f32[256,128]{1,0:T(8,128)S(1)} %get-tuple-element.82.refs_2_), channel_id=1, source_target_pairs={{0,16},{1,17},{2,18},{3,19},{4,20},{5,21},{6,22},{7,23},{8,24},{9,... | collective-permute-start | bytes 393224 | tf_op jit(solution)/shard_map/ppermute | solution.py:305
  28.9 5.0 %collective-permute-start.9 = (f32[256,128]{1,0:T(8,128)S(1)}, f32[256,128]{1,0:T(8,128)S(1)}, u32[]{:S(2)}, u32[]{:S(2)}) collective-permute-start(f32[256,128]{1,0:T(8,128)S(1)} %get-tuple-element.83.refs_3_.refs_0_), channel_id=1, source_target_pairs={{0,8},{1,9},{2,10},{3,11},{4,12},{5,13},{6,14},{7,15},{8,0},{9,1},... | collective-permute-start | bytes 393224 | tf_op jit(solution)/shard_map/ppermute | solution.py:305
  32.4 8.2 %collective-permute-start.12 = (f32[256,128]{1,0:T(8,128)S(1)}, f32[256,128]{1,0:T(8,128)S(1)}, u32[]{:S(2)}, u32[]{:S(2)}) collective-permute-start(f32[256,128]{1,0:T(8,128)S(1)} %get-tuple-element.88.refs_2_), channel_id=1, source_target_pairs={{0,4},{1,5},{2,6},{3,7},{4,0},{5,1},{6,2},{7,3},{8,12},{9,13},{10,... | collective-permute-start | bytes 393224 | tf_op jit(solution)/shard_map/ppermute | solution.py:305
  34.0 5.0 %collective-permute-start.11 = (f32[256,128]{1,0:T(8,128)S(1)}, f32[256,128]{1,0:T(8,128)S(1)}, u32[]{:S(2)}, u32[]{:S(2)}) collective-permute-start(f32[256,128]{1,0:T(8,128)S(1)} %get-tuple-element.89.refs_2_), channel_id=1, source_target_pairs={{0,16},{1,17},{2,18},{3,19},{4,20},{5,21},{6,22},{7,23},{8,24},{9,... | collective-permute-start | bytes 393224 | tf_op jit(solution)/shard_map/ppermute | solution.py:305
  35.6 12.8 %collective-permute-start.16 = (f32[256,128]{1,0:T(8,128)S(1)}, f32[256,128]{1,0:T(8,128)S(1)}, u32[]{:S(2)}, u32[]{:S(2)}) collective-permute-start(f32[256,128]{1,0:T(8,128)S(1)} %get-tuple-element.94.refs_3_), channel_id=1, source_target_pairs={{0,2},{1,3},{2,0},{3,1},{4,6},{5,7},{6,4},{7,5},{8,10},{9,11},{10,... | collective-permute-start | bytes 393224 | tf_op jit(solution)/shard_map/ppermute | solution.py:305
  39.1 6.1 %collective-permute-start.13 = (f32[256,128]{1,0:T(8,128)S(1)}, f32[256,128]{1,0:T(8,128)S(1)}, u32[]{:S(2)}, u32[]{:S(2)}) collective-permute-start(f32[256,128]{1,0:T(8,128)S(1)} %get-tuple-element.98.refs_2_), channel_id=1, source_target_pairs={{0,4},{1,5},{2,6},{3,7},{4,0},{5,1},{6,2},{7,3},{8,12},{9,13},{10,... | collective-permute-start | bytes 393224 | tf_op jit(solution)/shard_map/ppermute | solution.py:305
  40.6 7.8 %collective-permute-start.17 = (f32[256,128]{1,0:T(8,128)S(1)}, f32[256,128]{1,0:T(8,128)S(1)}, u32[]{:S(2)}, u32[]{:S(2)}) collective-permute-start(f32[256,128]{1,0:T(8,128)S(1)} %get-tuple-element.99.refs_2_), channel_id=1, source_target_pairs={{0,2},{1,3},{2,0},{3,1},{4,6},{5,7},{6,4},{7,5},{8,10},{9,11},{10,... | collective-permute-start | bytes 393224 | tf_op jit(solution)/shard_map/ppermute | solution.py:305
  42.6 9.4 %collective-permute-start.14 = (f32[256,128]{1,0:T(8,128)S(1)}, f32[256,128]{1,0:T(8,128)S(1)}, u32[]{:S(2)}, u32[]{:S(2)}) collective-permute-start(f32[256,128]{1,0:T(8,128)S(1)} %get-tuple-element.100.refs_3_), channel_id=1, source_target_pairs={{0,2},{1,3},{2,0},{3,1},{4,6},{5,7},{6,4},{7,5},{8,10},{9,11},{10,... | collective-permute-start | bytes 393224 | tf_op jit(solution)/shard_map/ppermute | solution.py:305
  42.8 1.8 %copy-start.1 = (f32[4096]{0:T(1024)S(1)}, f32[4096]{0:T(1024)}, u32[]{:S(2)}) copy-start(f32[4096]{0:T(1024)} %param.7) | copy-start | bytes 49156
  45.2 6.8 %collective-permute-start.15 = (f32[256,128]{1,0:T(8,128)S(1)}, f32[256,128]{1,0:T(8,128)S(1)}, u32[]{:S(2)}, u32[]{:S(2)}) collective-permute-start(f32[256,128]{1,0:T(8,128)S(1)} %get-tuple-element.104.refs_5_), channel_id=1, source_target_pairs={{0,2},{1,3},{2,0},{3,1},{4,6},{5,7},{6,4},{7,5},{8,10},{9,11},{10,... | collective-permute-start | bytes 393224 | tf_op jit(solution)/shard_map/ppermute | solution.py:305
  48.6 2.0 %collective-permute-start.18 = (f32[1024,128]{1,0:T(8,128)S(1)}, f32[1024,128]{1,0:T(8,128)S(1)}, u32[]{:S(2)}, u32[]{:S(2)}) collective-permute-start(f32[1024,128]{1,0:T(8,128)S(1)} %get-tuple-element.109.refs_4_), channel_id=1, source_target_pairs={{0,1},{1,0},{2,3},{3,2},{4,5},{5,4},{6,7},{7,6},{8,9},{9,8},{10,11... | collective-permute-start | bytes 1572872 | tf_op jit(solution)/shard_map/ppermute | solution.py:305
  52.2 2.0 %collective-permute-start.19 = (f32[1024,128]{1,0:T(8,128)S(1)}, f32[1024,128]{1,0:T(8,128)S(1)}, u32[]{:S(2)}, u32[]{:S(2)}) collective-permute-start(f32[1024,128]{1,0:T(8,128)S(1)} %get-tuple-element.111.refs_5_), channel_id=1, source_target_pairs={{0,1},{1,0},{2,3},{3,2},{4,5},{5,4},{6,7},{7,6},{8,9},{9,8},{10,11... | collective-permute-start | bytes 1572872 | tf_op jit(solution)/shard_map/ppermute | solution.py:305

commit v9 on v8

--- a/solution.py
+++ b/solution.py
@@ -16,6 +16,7 @@
 PIECE = 4
 OUT_PIECE = 2
 HINT = 7 * 10**9
+HINTS = {"up": 10**9}
 WIDTH = PIECE * E
 
 
@@ -87,7 +88,7 @@
         scratch_shapes=scratch,
         input_output_aliases={} if alias is None else {alias: 0},
         compiler_params=limit(mebibytes),
-        cost_estimate=pl.CostEstimate(flops=HINT, bytes_accessed=1, transcendentals=0),
+        cost_estimate=pl.CostEstimate(flops=HINTS.get(name, HINT), bytes_accessed=1, transcendentals=0),
         name=name,
     )(*[pltpu.with_memory_space_constraint(x, space) for x, space in operands])
 
@@ -360,6 +361,7 @@
     goes_on(0)
     stays(0)
     some_local()
+    some_local()
     goes_on(1)
     up(2, 0)
     stays(1)
@@ -367,7 +369,6 @@
     if levels == 3:
         along(0)
         up(2, 1)
-        some_local()
         turn(0)
         along(1)
         part(0, 0)
@@ -387,7 +388,6 @@
     if levels > 3:
         part(0, 0)
     part(0, 1)
-    part(1, 0)
     while todo:
         some_local()
     gain = after(vmem_call(copy_kernel, "gain", [gain.shape], latest, gain)[0])
@@ -395,6 +395,7 @@
         keep[c], send = last_down(part_keep[c], part_got[c], low[c][0], latest)
         got[c] = swap(after(send), 0)
 
+    part(1, 0)
     part(1, 1)
     out = None
     for c in chunks:

time: 55.8 us -> 55.8 us (level)
  local copies, waits for them, and re-layouts: 1.87 us -> 0.01 us
  waiting for transfers between devices: 6.66 us -> 8.35 us
    unnamed x4, local copies, waits for them, and re-layouts: 1.87 us -> 0.01 us
    ppermute x20, waiting for transfers between devices: 6.66 us -> 8.35 us  [swap(): return lax.ppermute(x, AXES, [(i, i ^ 1 << level) for i in range(devices)])]
  transfers between devices with their start and end apart: 20 -> 20, of which waited for: 8 -> 9; matrix products, arithmetic and copies ran while one was open for 0% -> 0% of each run, Pallas kernels for 31% -> 31%
where the time goes in v9:
time: 55.8 us; the launch traced here: 55.6 us
  starting transfers between devices  26 us (47%)
  Pallas kernels  21 us (38%)
  waiting for transfers between devices  8.35 us (15%)
    ppermute x20, starting transfers between devices, swap(): return lax.ppermute(x, AXES, [(i, i ^ 1 << level) for i in range(devices)])  26 us
    pallas_call x31, Pallas kernels, call(): pl.pallas_call(body, in_specs=[pl.BlockSpec(memory_space=space) for _, sp...  21 us
    ppermute x20, waiting for transfers between devices, swap(): return lax.ppermute(x, AXES, [(i, i ^ 1 << level) for i in range(devices)])  8.35 us
  transfers between devices with their start and end apart: 20, of which 9 were waited for; matrix products, arithmetic and copies ran while one was open for 0% of the time, Pallas kernels for 31%

profile of v9, /device:TPU:0, one launch (start us, length us, event | category | flops | bytes accessed | tf_op | source)
XLA Modules:
  0.0 55.6 jit_solution(17880760187440996787)
XLA Ops:
  0.0 1.8 %states.4 = (f32[1024,128]{1,0:T(8,128)S(1)}, bf16[384,1024]{1,0:T(8,128)(2,1)S(1)}, bf16[384,1024]{1,0:T(8,128)(2,1)S(1)}) custom-call(bf16[384,4096]{1,0:T(8,128)(2,1)} %refs_0_.15, bf16[384,4096]{1,0:T(8,128)(2,1)} %refs_1_.7), custom_call_target="tpu_custom_call" | custom-call | flops 7000000000 | bytes 1 | tf_op jit(solution)/shard_map/states/pallas_call | solution.py:83
  1.8 0.5 collective-permute-start
  2.3 1.8 %states.5 = (f32[1024,128]{1,0:T(8,128)S(1)}, bf16[384,1024]{1,0:T(8,128)(2,1)S(1)}, bf16[384,1024]{1,0:T(8,128)(2,1)S(1)}) custom-call(bf16[384,4096]{1,0:T(8,128)(2,1)} %refs_0_.15, bf16[384,4096]{1,0:T(8,128)(2,1)} %refs_1_.7, f32[1024,128]{1,0:T(8,128)S(1)} %get-tuple-element.59.refs_2_), custom_call_target="tpu_custom_call" | custom-call | flops 7000000000 | bytes 1 | tf_op jit(solution)/shard_map/states/pallas_call | solution.py:83
  4.2 0.1 first_up.2
  4.3 2.7 %collective-permute-start.2 = (f32[256,128]{1,0:T(8,128)S(1)}, f32[256,128]{1,0:T(8,128)S(1)}, u32[]{:S(2)}, u32[]{:S(2)}) collective-permute-start(f32[256,128]{1,0:T(8,128)S(1)} %get-tuple-element.61.refs_2_), channel_id=1, source_target_pairs={{0,2},{1,3},{2,0},{3,1},{4,6},{5,7},{6,4},{7,5},{8,10},{9,11},{10,... | collective-permute-start | bytes 393224 | tf_op jit(solution)/shard_map/ppermute | solution.py:306
  7.0 1.8 %states.6 = (f32[1024,128]{1,0:T(8,128)S(1)}, bf16[384,1024]{1,0:T(8,128)(2,1)S(1)}, bf16[384,1024]{1,0:T(8,128)(2,1)S(1)}) custom-call(bf16[384,4096]{1,0:T(8,128)(2,1)} %refs_0_.15, bf16[384,4096]{1,0:T(8,128)(2,1)} %refs_1_.7, f32[256,128]{1,0:T(8,128)S(1)} %get-tuple-element.61.refs_2_), custom_call_target="tpu_custom_call" | custom-call | flops 7000000000 | bytes 1 | tf_op jit(solution)/shard_map/states/pallas_call | solution.py:83
  8.8 0.1 collective-permute-start.1
  8.9 0.2 collective-permute-start.3
  9.1 1.8 %states.7 = (f32[1024,128]{1,0:T(8,128)S(1)}, bf16[384,1024]{1,0:T(8,128)(2,1)S(1)}, bf16[384,1024]{1,0:T(8,128)(2,1)S(1)}) custom-call(bf16[384,4096]{1,0:T(8,128)(2,1)} %refs_0_.15, bf16[384,4096]{1,0:T(8,128)(2,1)} %refs_1_.7, f32[1024,128]{1,0:T(8,128)S(1)} %get-tuple-element.67.refs_2_), custom_call_target="tpu_custom_call" | custom-call | flops 7000000000 | bytes 1 | tf_op jit(solution)/shard_map/states/pallas_call | solution.py:83
  10.9 0.0 collective-permute-done.3.refs_1_
  10.9 0.1 first_up.3
  11.1 1.9 %collective-permute-start.5 = (f32[256,128]{1,0:T(8,128)S(1)}, f32[256,128]{1,0:T(8,128)S(1)}, u32[]{:S(2)}, u32[]{:S(2)}) collective-permute-start(f32[256,128]{1,0:T(8,128)S(1)} %get-tuple-element.69.refs_2_), channel_id=1, source_target_pairs={{0,2},{1,3},{2,0},{3,1},{4,6},{5,7},{6,4},{7,5},{8,10},{9,11},{10,... | collective-permute-start | bytes 393224 | tf_op jit(solution)/shard_map/ppermute | solution.py:306
  13.0 2.7 %collective-permute-start.4 = (f32[256,128]{1,0:T(8,128)S(1)}, f32[256,128]{1,0:T(8,128)S(1)}, u32[]{:S(2)}, u32[]{:S(2)}) collective-permute-start(f32[256,128]{1,0:T(8,128)S(1)} %get-tuple-element.70.refs_2_), channel_id=1, source_target_pairs={{0,4},{1,5},{2,6},{3,7},{4,0},{5,1},{6,2},{7,3},{8,12},{9,13},{10,... | collective-permute-start | bytes 393224 | tf_op jit(solution)/shard_map/ppermute | solution.py:306
  15.7 0.4 collective-permute-start.7
  16.2 1.8 %local.4.refs_3_.refs_1_ = f32[384,1024]{1,0:T(8,128)S(1)} custom-call(bf16[384,4096]{1,0:T(8,128)(2,1)S(1)} %copy-done, bf16[384,1024]{1,0:T(8,128)(2,1)S(1)} %get-tuple-element.75.refs_1_, bf16[384,1024]{1,0:T(8,128)(2,1)S(1)} %get-tuple-element.76.refs_2_, f32[256,128]{1,0:T(8,128)S(1)} %get-tuple-element.71.refs_3_.refs_0_), custom_call_target="tpu_custom_call" | custom-call | flops 7000000000 | bytes 1 | tf_op jit(solution)/shard_map/local/pallas_call | solution.py:83
  18.0 1.8 %local.5.refs_2_.refs_1_ = f32[384,1024]{1,0:T(8,128)S(1)} custom-call(bf16[384,4096]{1,0:T(8,128)(2,1)S(1)} %copy-done, bf16[384,1024]{1,0:T(8,128)(2,1)S(1)} %get-tuple-element.73.refs_1_, bf16[384,1024]{1,0:T(8,128)(2,1)S(1)} %get-tuple-element.74.refs_2_, f32[384,1024]{1,0:T(8,128)S(1)} %local.4.refs_3_.refs_1_), custom_call_target="tpu_custom_call" | custom-call | flops 7000000000 | bytes 1 | tf_op jit(solution)/shard_map/local/pallas_call | solution.py:83
  19.8 0.3 collective-permute-done.5.refs_1_
  20.1 1.1 %collective-permute-start.9 = (f32[256,128]{1,0:T(8,128)S(1)}, f32[256,128]{1,0:T(8,128)S(1)}, u32[]{:S(2)}, u32[]{:S(2)}) collective-permute-start(f32[256,128]{1,0:T(8,128)S(1)} %get-tuple-element.77.refs_2_), channel_id=1, source_target_pairs={{0,4},{1,5},{2,6},{3,7},{4,0},{5,1},{6,2},{7,3},{8,12},{9,13},{10,... | collective-permute-start | bytes 393224 | tf_op jit(solution)/shard_map/ppermute | solution.py:306
  21.2 1.0 %collective-permute-done.4.refs_1_ = f32[256,128]{1,0:T(8,128)S(1)} collective-permute-done((f32[256,128]{1,0:T(8,128)S(1)}, f32[256,128]{1,0:T(8,128)S(1)}, u32[]{:S(2)}, u32[]{:S(2)}) %collective-permute-start.4) | collective-permute-done | bytes 131104 | tf_op jit(solution)/shard_map/ppermute | solution.py:306
  22.3 1.6 %collective-permute-start.6 = (f32[256,128]{1,0:T(8,128)S(1)}, f32[256,128]{1,0:T(8,128)S(1)}, u32[]{:S(2)}, u32[]{:S(2)}) collective-permute-start(f32[256,128]{1,0:T(8,128)S(1)} %get-tuple-element.78.refs_2_.refs_0_), channel_id=1, source_target_pairs={{0,8},{1,9},{2,10},{3,11},{4,12},{5,13},{6,14},{7,15},{8,0},{9,1},... | collective-permute-start | bytes 393224 | tf_op jit(solution)/shard_map/ppermute | solution.py:306
  23.8 0.0 collective-permute-done.7.refs_1_
  23.8 1.8 %local.6.refs_2_.refs_1_ = f32[384,1024]{1,0:T(8,128)S(1)} custom-call(bf16[384,4096]{1,0:T(8,128)(2,1)S(1)} %copy-done, bf16[384,1024]{1,0:T(8,128)(2,1)S(1)} %get-tuple-element.79.refs_1_, bf16[384,1024]{1,0:T(8,128)(2,1)S(1)} %get-tuple-element.80.refs_2_, f32[256,128]{1,0:T(8,128)S(1)} %get-tuple-element.83.refs_3_.refs_0_), custom_call_target="tpu_custom_call" | custom-call | flops 7000000000 | bytes 1 | tf_op jit(solution)/shard_map/local/pallas_call | solution.py:83
  25.7 1.6 %collective-permute-done.6.refs_1_ = f32[256,128]{1,0:T(8,128)S(1)} collective-permute-done((f32[256,128]{1,0:T(8,128)S(1)}, f32[256,128]{1,0:T(8,128)S(1)}, u32[]{:S(2)}, u32[]{:S(2)}) %collective-permute-start.6) | collective-permute-done | bytes 131104 | tf_op jit(solution)/shard_map/ppermute | solution.py:306
  27.3 1.6 %collective-permute-start.8 = (f32[256,128]{1,0:T(8,128)S(1)}, f32[256,128]{1,0:T(8,128)S(1)}, u32[]{:S(2)}, u32[]{:S(2)}) collective-permute-start(f32[256,128]{1,0:T(8,128)S(1)} %get-tuple-element.84.refs_2_), channel_id=1, source_target_pairs={{0,16},{1,17},{2,18},{3,19},{4,20},{5,21},{6,22},{7,23},{8,24},{9,... | collective-permute-start | bytes 393224 | tf_op jit(solution)/shard_map/ppermute | solution.py:306
  28.9 1.6 %collective-permute-start.11 = (f32[256,128]{1,0:T(8,128)S(1)}, f32[256,128]{1,0:T(8,128)S(1)}, u32[]{:S(2)}, u32[]{:S(2)}) collective-permute-start(f32[256,128]{1,0:T(8,128)S(1)} %get-tuple-element.87.refs_3_.refs_0_), channel_id=1, source_target_pairs={{0,8},{1,9},{2,10},{3,11},{4,12},{5,13},{6,14},{7,15},{8,0},{9,1},... | collective-permute-start | bytes 393224 | tf_op jit(solution)/shard_map/ppermute | solution.py:306
  30.5 1.8 %collective-permute-done.8.refs_0_ = f32[256,128]{1,0:T(8,128)S(1)} collective-permute-done((f32[256,128]{1,0:T(8,128)S(1)}, f32[256,128]{1,0:T(8,128)S(1)}, u32[]{:S(2)}, u32[]{:S(2)}) %collective-permute-start.8) | collective-permute-done | bytes 131104 | tf_op jit(solution)/shard_map/ppermute | solution.py:306
  32.4 1.0 %collective-permute-start.10 = (f32[256,128]{1,0:T(8,128)S(1)}, f32[256,128]{1,0:T(8,128)S(1)}, u32[]{:S(2)}, u32[]{:S(2)}) collective-permute-start(f32[256,128]{1,0:T(8,128)S(1)} %get-tuple-element.88.refs_2_), channel_id=1, source_target_pairs={{0,4},{1,5},{2,6},{3,7},{4,0},{5,1},{6,2},{7,3},{8,12},{9,13},{10,... | collective-permute-start | bytes 393224 | tf_op jit(solution)/shard_map/ppermute | solution.py:306
  33.4 0.6 %collective-permute-done.11.refs_1_ = f32[256,128]{1,0:T(8,128)S(1)} collective-permute-done((f32[256,128]{1,0:T(8,128)S(1)}, f32[256,128]{1,0:T(8,128)S(1)}, u32[]{:S(2)}, u32[]{:S(2)}) %collective-permute-start.11) | collective-permute-done | bytes 131104 | tf_op jit(solution)/shard_map/ppermute | solution.py:306
  34.0 1.6 %collective-permute-start.12 = (f32[256,128]{1,0:T(8,128)S(1)}, f32[256,128]{1,0:T(8,128)S(1)}, u32[]{:S(2)}, u32[]{:S(2)}) collective-permute-start(f32[256,128]{1,0:T(8,128)S(1)} %get-tuple-element.90.refs_2_), channel_id=1, source_target_pairs={{0,16},{1,17},{2,18},{3,19},{4,20},{5,21},{6,22},{7,23},{8,24},{9,... | collective-permute-start | bytes 393224 | tf_op jit(solution)/shard_map/ppermute | solution.py:306
  35.6 1.9 %collective-permute-start.16 = (f32[256,128]{1,0:T(8,128)S(1)}, f32[256,128]{1,0:T(8,128)S(1)}, u32[]{:S(2)}, u32[]{:S(2)}) collective-permute-start(f32[256,128]{1,0:T(8,128)S(1)} %get-tuple-element.95.refs_3_), channel_id=1, source_target_pairs={{0,2},{1,3},{2,0},{3,1},{4,6},{5,7},{6,4},{7,5},{8,10},{9,11},{10,... | collective-permute-start | bytes 393224 | tf_op jit(solution)/shard_map/ppermute | solution.py:306
  37.5 1.5 %collective-permute-done.12.refs_0_ = f32[256,128]{1,0:T(8,128)S(1)} collective-permute-done((f32[256,128]{1,0:T(8,128)S(1)}, f32[256,128]{1,0:T(8,128)S(1)}, u32[]{:S(2)}, u32[]{:S(2)}) %collective-permute-start.12) | collective-permute-done | bytes 131104 | tf_op jit(solution)/shard_map/ppermute | solution.py:306
  39.1 1.5 %collective-permute-start.13 = (f32[256,128]{1,0:T(8,128)S(1)}, f32[256,128]{1,0:T(8,128)S(1)}, u32[]{:S(2)}, u32[]{:S(2)}) collective-permute-start(f32[256,128]{1,0:T(8,128)S(1)} %get-tuple-element.96.refs_2_), channel_id=1, source_target_pairs={{0,4},{1,5},{2,6},{3,7},{4,0},{5,1},{6,2},{7,3},{8,12},{9,13},{10,... | collective-permute-start | bytes 393224 | tf_op jit(solution)/shard_map/ppermute | solution.py:306
  40.5 0.0 collective-permute-done.10.refs_0_
  40.6 2.0 %collective-permute-start.17 = (f32[256,128]{1,0:T(8,128)S(1)}, f32[256,128]{1,0:T(8,128)S(1)}, u32[]{:S(2)}, u32[]{:S(2)}) collective-permute-start(f32[256,128]{1,0:T(8,128)S(1)} %get-tuple-element.97.refs_3_), channel_id=1, source_target_pairs={{0,2},{1,3},{2,0},{3,1},{4,6},{5,7},{6,4},{7,5},{8,10},{9,11},{10,... | collective-permute-start | bytes 393224 | tf_op jit(solution)/shard_map/ppermute | solution.py:306
  42.6 1.8 %local.7.refs_1_ = f32[384,1024]{1,0:T(8,128)S(1)} custom-call(bf16[384,4096]{1,0:T(8,128)(2,1)S(1)} %copy-done, bf16[384,1024]{1,0:T(8,128)(2,1)S(1)} %get-tuple-element.62.refs_1_, bf16[384,1024]{1,0:T(8,128)(2,1)S(1)} %get-tuple-element.63.refs_2_, f32[256,128]{1,0:T(8,128)S(1)} %get-tuple-element.97.refs_3_), custom_call_target="tpu_custom_call" | custom-call | flops 7000000000 | bytes 1 | tf_op jit(solution)/shard_map/local/pallas_call | solution.py:83
  44.4 0.2 collective-permute-start.14
  44.6 0.5 collective-permute-done.13.refs_0_
  45.2 3.2 %collective-permute-start.15 = (f32[256,128]{1,0:T(8,128)S(1)}, f32[256,128]{1,0:T(8,128)S(1)}, u32[]{:S(2)}, u32[]{:S(2)}) collective-permute-start(f32[256,128]{1,0:T(8,128)S(1)} %get-tuple-element.104.refs_5_), channel_id=1, source_target_pairs={{0,2},{1,3},{2,0},{3,1},{4,6},{5,7},{6,4},{7,5},{8,10},{9,11},{10,... | collective-permute-start | bytes 393224 | tf_op jit(solution)/shard_map/ppermute | solution.py:306
  48.4 0.2 last_down.2
  48.6 0.1 collective-permute-start.18
  48.7 1.4 %finish.4.refs_4_ = bf16[384,4096]{1,0:T(8,128)(2,1)} custom-call(bf16[384,4096]{1,0:T(8,128)(2,1)S(1)} %copy-done, f32[384,1024]{1,0:T(8,128)S(1)} %local.4.refs_3_.refs_1_, f32[1024,128]{1,0:T(8,128)S(1)} %get-tuple-element.110.refs_2_, f32[1,4096]{1,0:T(1,128)S(1)} %gain.1.refs_2_.refs_3_, f32[1024,128]{1,0:T(8,128)S(1)} %get-tuple-element.109.refs_4_), custom_call_target="tpu_custom_call" | custom-call | flops 7000000000 | bytes 1 | tf_op jit(solution)/shard_map/finish/pallas_call | solution.py:83
  50.1 0.5 collective-permute-done.18.refs_2_
  50.6 1.4 %finish.5.refs_5_.refs_4_ = bf16[384,4096]{1,0:T(8,128)(2,1)} custom-call(bf16[384,4096]{1,0:T(8,128)(2,1)S(1)} %copy-done, f32[384,1024]{1,0:T(8,128)S(1)} %local.5.refs_2_.refs_1_, f32[1024,128]{1,0:T(8,128)S(1)} %collective-permute-done.18.refs_2_, f32[1,4096]{1,0:T(1,128)S(1)} %gain.1.refs_2_.refs_3_, ...), custom_call_target="tpu_custom_call", output_to_operand_aliasing={{}: (4, {})} | custom-call | flops 7000000000 | bytes 1 | tf_op jit(solution)/shard_map/finish/pallas_call | solution.py:83
  52.0 0.2 last_down.3
  52.2 0.2 collective-permute-start.19
  52.4 1.4 %finish.6.refs_4_ = bf16[384,4096]{1,0:T(8,128)(2,1)} custom-call(bf16[384,4096]{1,0:T(8,128)(2,1)S(1)} %copy-done, f32[384,1024]{1,0:T(8,128)S(1)} %local.6.refs_2_.refs_1_, f32[1024,128]{1,0:T(8,128)S(1)} %get-tuple-element.112.refs_2_, f32[1,4096]{1,0:T(1,128)S(1)} %gain.1.refs_2_.refs_3_, ...), custom_call_target="tpu_custom_call", output_to_operand_aliasing={{}: (4, {})} | custom-call | flops 7000000000 | bytes 1 | tf_op jit(solution)/shard_map/finish/pallas_call | solution.py:83
  53.8 0.4 collective-permute-done.19.refs_2_
  54.2 1.4 %finish.7 = bf16[384,4096]{1,0:T(8,128)(2,1)} custom-call(bf16[384,4096]{1,0:T(8,128)(2,1)S(1)} %copy-done, f32[384,1024]{1,0:T(8,128)S(1)} %local.7.refs_1_, f32[1024,128]{1,0:T(8,128)S(1)} %collective-permute-done.19.refs_2_, f32[1,4096]{1,0:T(1,128)S(1)} %gain.1.refs_2_.refs_3_, bf16[384,4096]{1,0:T(8,128)(2,1)} %finish.6.refs_4_), custom_call_target="tpu_custom_call", output_to_operand_aliasing={{}: (4, {})} | custom-call | flops 7000000000 | bytes 1 | tf_op jit(solution)/shard_map/finish/pallas_call | solution.py:83
  (27 shorter events, 0.4 us)
Async XLA Ops:
  1.8 2.3 %collective-permute-start = (f32[1024,128]{1,0:T(8,128)S(1)}, f32[1024,128]{1,0:T(8,128)S(1)}, u32[]{:S(2)}, u32[]{:S(2)}) collective-permute-start(f32[1024,128]{1,0:T(8,128)S(1)} %get-tuple-element.59.refs_2_), channel_id=1, source_target_pairs={{0,1},{1,0},{2,3},{3,2},{4,5},{5,4},{6,7},{7,6},{8,9},{9,8},{10,11... | collective-permute-start | bytes 1572872 | tf_op jit(solution)/shard_map/ppermute | solution.py:306
  4.3 8.7 %collective-permute-start.2 = (f32[256,128]{1,0:T(8,128)S(1)}, f32[256,128]{1,0:T(8,128)S(1)}, u32[]{:S(2)}, u32[]{:S(2)}) collective-permute-start(f32[256,128]{1,0:T(8,128)S(1)} %get-tuple-element.61.refs_2_), channel_id=1, source_target_pairs={{0,2},{1,3},{2,0},{3,1},{4,6},{5,7},{6,4},{7,5},{8,10},{9,11},{10,... | collective-permute-start | bytes 393224 | tf_op jit(solution)/shard_map/ppermute | solution.py:306
  8.8 7.3 %collective-permute-start.1 = (f32[256,128]{1,0:T(8,128)S(1)}, f32[256,128]{1,0:T(8,128)S(1)}, u32[]{:S(2)}, u32[]{:S(2)}) collective-permute-start(f32[256,128]{1,0:T(8,128)S(1)} %get-tuple-element.65), channel_id=1, source_target_pairs={{0,2},{1,3},{2,0},{3,1},{4,6},{5,7},{6,4},{7,5},{8,10},{9,11},{10,... | collective-permute-start | bytes 393224 | tf_op jit(solution)/shard_map/ppermute | solution.py:306
  8.9 2.0 %collective-permute-start.3 = (f32[1024,128]{1,0:T(8,128)S(1)}, f32[1024,128]{1,0:T(8,128)S(1)}, u32[]{:S(2)}, u32[]{:S(2)}) collective-permute-start(f32[1024,128]{1,0:T(8,128)S(1)} %get-tuple-element.67.refs_2_), channel_id=1, source_target_pairs={{0,1},{1,0},{2,3},{3,2},{4,5},{5,4},{6,7},{7,6},{8,9},{9,8},{10,11... | collective-permute-start | bytes 1572872 | tf_op jit(solution)/shard_map/ppermute | solution.py:306
  11.1 9.0 %collective-permute-start.5 = (f32[256,128]{1,0:T(8,128)S(1)}, f32[256,128]{1,0:T(8,128)S(1)}, u32[]{:S(2)}, u32[]{:S(2)}) collective-permute-start(f32[256,128]{1,0:T(8,128)S(1)} %get-tuple-element.69.refs_2_), channel_id=1, source_target_pairs={{0,2},{1,3},{2,0},{3,1},{4,6},{5,7},{6,4},{7,5},{8,10},{9,11},{10,... | collective-permute-start | bytes 393224 | tf_op jit(solution)/shard_map/ppermute | solution.py:306
  13.0 3.2 %copy-start = (bf16[384,4096]{1,0:T(8,128)(2,1)S(1)}, bf16[384,4096]{1,0:T(8,128)(2,1)}, u32[]{:S(2)}) copy-start(bf16[384,4096]{1,0:T(8,128)(2,1)} %refs_0_.23) | copy-start | bytes 9437188
  13.0 9.2 %collective-permute-start.4 = (f32[256,128]{1,0:T(8,128)S(1)}, f32[256,128]{1,0:T(8,128)S(1)}, u32[]{:S(2)}, u32[]{:S(2)}) collective-permute-start(f32[256,128]{1,0:T(8,128)S(1)} %get-tuple-element.70.refs_2_), channel_id=1, source_target_pairs={{0,4},{1,5},{2,6},{3,7},{4,0},{5,1},{6,2},{7,3},{8,12},{9,13},{10,... | collective-permute-start | bytes 393224 | tf_op jit(solution)/shard_map/ppermute | solution.py:306
  15.7 8.1 %collective-permute-start.7 = (f32[256,128]{1,0:T(8,128)S(1)}, f32[256,128]{1,0:T(8,128)S(1)}, u32[]{:S(2)}, u32[]{:S(2)}) collective-permute-start(f32[256,128]{1,0:T(8,128)S(1)} %get-tuple-element.82), channel_id=1, source_target_pairs={{0,2},{1,3},{2,0},{3,1},{4,6},{5,7},{6,4},{7,5},{8,10},{9,11},{10,... | collective-permute-start | bytes 393224 | tf_op jit(solution)/shard_map/ppermute | solution.py:306
  20.1 8.8 %collective-permute-start.9 = (f32[256,128]{1,0:T(8,128)S(1)}, f32[256,128]{1,0:T(8,128)S(1)}, u32[]{:S(2)}, u32[]{:S(2)}) collective-permute-start(f32[256,128]{1,0:T(8,128)S(1)} %get-tuple-element.77.refs_2_), channel_id=1, source_target_pairs={{0,4},{1,5},{2,6},{3,7},{4,0},{5,1},{6,2},{7,3},{8,12},{9,13},{10,... | collective-permute-start | bytes 393224 | tf_op jit(solution)/shard_map/ppermute | solution.py:306
  22.3 5.0 %collective-permute-start.6 = (f32[256,128]{1,0:T(8,128)S(1)}, f32[256,128]{1,0:T(8,128)S(1)}, u32[]{:S(2)}, u32[]{:S(2)}) collective-permute-start(f32[256,128]{1,0:T(8,128)S(1)} %get-tuple-element.78.refs_2_.refs_0_), channel_id=1, source_target_pairs={{0,8},{1,9},{2,10},{3,11},{4,12},{5,13},{6,14},{7,15},{8,0},{9,1},... | collective-permute-start | bytes 393224 | tf_op jit(solution)/shard_map/ppermute | solution.py:306
  27.3 5.0 %collective-permute-start.8 = (f32[256,128]{1,0:T(8,128)S(1)}, f32[256,128]{1,0:T(8,128)S(1)}, u32[]{:S(2)}, u32[]{:S(2)}) collective-permute-start(f32[256,128]{1,0:T(8,128)S(1)} %get-tuple-element.84.refs_2_), channel_id=1, source_target_pairs={{0,16},{1,17},{2,18},{3,19},{4,20},{5,21},{6,22},{7,23},{8,24},{9,... | collective-permute-start | bytes 393224 | tf_op jit(solution)/shard_map/ppermute | solution.py:306
  28.9 5.0 %collective-permute-start.11 = (f32[256,128]{1,0:T(8,128)S(1)}, f32[256,128]{1,0:T(8,128)S(1)}, u32[]{:S(2)}, u32[]{:S(2)}) collective-permute-start(f32[256,128]{1,0:T(8,128)S(1)} %get-tuple-element.87.refs_3_.refs_0_), channel_id=1, source_target_pairs={{0,8},{1,9},{2,10},{3,11},{4,12},{5,13},{6,14},{7,15},{8,0},{9,1},... | collective-permute-start | bytes 393224 | tf_op jit(solution)/shard_map/ppermute | solution.py:306
  32.4 8.2 %collective-permute-start.10 = (f32[256,128]{1,0:T(8,128)S(1)}, f32[256,128]{1,0:T(8,128)S(1)}, u32[]{:S(2)}, u32[]{:S(2)}) collective-permute-start(f32[256,128]{1,0:T(8,128)S(1)} %get-tuple-element.88.refs_2_), channel_id=1, source_target_pairs={{0,4},{1,5},{2,6},{3,7},{4,0},{5,1},{6,2},{7,3},{8,12},{9,13},{10,... | collective-permute-start | bytes 393224 | tf_op jit(solution)/shard_map/ppermute | solution.py:306
  34.0 5.0 %collective-permute-start.12 = (f32[256,128]{1,0:T(8,128)S(1)}, f32[256,128]{1,0:T(8,128)S(1)}, u32[]{:S(2)}, u32[]{:S(2)}) collective-permute-start(f32[256,128]{1,0:T(8,128)S(1)} %get-tuple-element.90.refs_2_), channel_id=1, source_target_pairs={{0,16},{1,17},{2,18},{3,19},{4,20},{5,21},{6,22},{7,23},{8,24},{9,... | collective-permute-start | bytes 393224 | tf_op jit(solution)/shard_map/ppermute | solution.py:306
  35.6 12.8 %collective-permute-start.16 = (f32[256,128]{1,0:T(8,128)S(1)}, f32[256,128]{1,0:T(8,128)S(1)}, u32[]{:S(2)}, u32[]{:S(2)}) collective-permute-start(f32[256,128]{1,0:T(8,128)S(1)} %get-tuple-element.95.refs_3_), channel_id=1, source_target_pairs={{0,2},{1,3},{2,0},{3,1},{4,6},{5,7},{6,4},{7,5},{8,10},{9,11},{10,... | collective-permute-start | bytes 393224 | tf_op jit(solution)/shard_map/ppermute | solution.py:306
  39.1 6.1 %collective-permute-start.13 = (f32[256,128]{1,0:T(8,128)S(1)}, f32[256,128]{1,0:T(8,128)S(1)}, u32[]{:S(2)}, u32[]{:S(2)}) collective-permute-start(f32[256,128]{1,0:T(8,128)S(1)} %get-tuple-element.96.refs_2_), channel_id=1, source_target_pairs={{0,4},{1,5},{2,6},{3,7},{4,0},{5,1},{6,2},{7,3},{8,12},{9,13},{10,... | collective-permute-start | bytes 393224 | tf_op jit(solution)/shard_map/ppermute | solution.py:306
  40.6 7.8 %collective-permute-start.17 = (f32[256,128]{1,0:T(8,128)S(1)}, f32[256,128]{1,0:T(8,128)S(1)}, u32[]{:S(2)}, u32[]{:S(2)}) collective-permute-start(f32[256,128]{1,0:T(8,128)S(1)} %get-tuple-element.97.refs_3_), channel_id=1, source_target_pairs={{0,2},{1,3},{2,0},{3,1},{4,6},{5,7},{6,4},{7,5},{8,10},{9,11},{10,... | collective-permute-start | bytes 393224 | tf_op jit(solution)/shard_map/ppermute | solution.py:306
  42.6 1.8 %copy-start.1 = (f32[4096]{0:T(1024)S(1)}, f32[4096]{0:T(1024)}, u32[]{:S(2)}) copy-start(f32[4096]{0:T(1024)} %param.7) | copy-start | bytes 49156
  44.4 7.5 %collective-permute-start.14 = (f32[256,128]{1,0:T(8,128)S(1)}, f32[256,128]{1,0:T(8,128)S(1)}, u32[]{:S(2)}, u32[]{:S(2)}) collective-permute-start(f32[256,128]{1,0:T(8,128)S(1)} %get-tuple-element.102.refs_2_), channel_id=1, source_target_pairs={{0,2},{1,3},{2,0},{3,1},{4,6},{5,7},{6,4},{7,5},{8,10},{9,11},{10,... | collective-permute-start | bytes 393224 | tf_op jit(solution)/shard_map/ppermute | solution.py:306
  45.2 6.8 %collective-permute-start.15 = (f32[256,128]{1,0:T(8,128)S(1)}, f32[256,128]{1,0:T(8,128)S(1)}, u32[]{:S(2)}, u32[]{:S(2)}) collective-permute-start(f32[256,128]{1,0:T(8,128)S(1)} %get-tuple-element.104.refs_5_), channel_id=1, source_target_pairs={{0,2},{1,3},{2,0},{3,1},{4,6},{5,7},{6,4},{7,5},{8,10},{9,11},{10,... | collective-permute-start | bytes 393224 | tf_op jit(solution)/shard_map/ppermute | solution.py:306
  48.6 2.0 %collective-permute-start.18 = (f32[1024,128]{1,0:T(8,128)S(1)}, f32[1024,128]{1,0:T(8,128)S(1)}, u32[]{:S(2)}, u32[]{:S(2)}) collective-permute-start(f32[1024,128]{1,0:T(8,128)S(1)} %get-tuple-element.109.refs_4_), channel_id=1, source_target_pairs={{0,1},{1,0},{2,3},{3,2},{4,5},{5,4},{6,7},{7,6},{8,9},{9,8},{10,11... | collective-permute-start | bytes 1572872 | tf_op jit(solution)/shard_map/ppermute | solution.py:306
  52.2 2.0 %collective-permute-start.19 = (f32[1024,128]{1,0:T(8,128)S(1)}, f32[1024,128]{1,0:T(8,128)S(1)}, u32[]{:S(2)}, u32[]{:S(2)}) collective-permute-start(f32[1024,128]{1,0:T(8,128)S(1)} %get-tuple-element.111.refs_5_), channel_id=1, source_target_pairs={{0,1},{1,0},{2,3},{3,2},{4,5},{5,4},{6,7},{7,6},{8,9},{9,8},{10,11... | collective-permute-start | bytes 1572872 | tf_op jit(solution)/shard_map/ppermute | solution.py:306
